TPU v7x, 32 devices: a whole 2x2x4 slice. The times are simulated.
32 devices in a mesh: grp: 8 (over z, y), in: 4 (over x, core).
Axes of the slice: x: 2, y: 2, z: 4, core: 2. Of those that a mesh axis runs over, the one named last changes fastest.
Arguments:
- picture_embeds: bfloat16 [4096, 1152], P(('grp', 'in')), may hold values from -0.1875 to 0.1875
- caption_embeds: bfloat16 [4096, 1152], P(('grp', 'in')), may hold values from -0.1875 to 0.1875
- sharpness_factor: float32 [1], replicated, may hold values from 10 to 30
- additive_shift_term: float32 [1], replicated, may hold values from -4 to -2
Outputs:
- image_grad: bfloat16 [4096, 1152], P(('grp', 'in'))
- text_grad: bfloat16 [4096, 1152], P(('grp', 'in'))
All inputs are finite; a program needn't handle non-finite values.
Results may differ from a plain program's by a relative error of at most 0.0046.
Values may be sent and summed in bfloat16 or wider, within the bound.
No kernel may reach another device: no remote copies, remote signals or barrier semaphores. Data moves between devices by JAX's collectives and lax.ppermute only.
A program may use at most 64 MiB of HBM per device.

v0:
```python
import jax
import jax.numpy as jnp
from jax import lax
from jax.sharding import PartitionSpec as P

STEPS = 2


def from_behind(array, axis, by):
    peers = lax.axis_size(axis)
    return lax.ppermute(array, axis, [(i, (i + by) % peers) for i in range(peers)])


def similarity_derivative(
    local_batch_count,
    counterpart_batch,
    sharpness_scalar,
    additive_term_scalar,
    matching_mask,
    initial_step_flag,
):
    similarity_matrix = (
        sharpness_scalar
        * jnp.dot(local_batch_count, counterpart_batch.T, preferred_element_type=jnp.float32)
        + additive_term_scalar
    )
    loss_multipliers = jax.nn.sigmoid(similarity_matrix)
    if initial_step_flag:
        loss_multipliers = loss_multipliers - matching_mask
    label_signs = (sharpness_scalar * loss_multipliers).astype(jnp.bfloat16)
    return jnp.dot(label_signs, counterpart_batch, preferred_element_type=jnp.float32)


def shards(picture_embeds, caption_embeds, sharpness_factor, additive_shift_term):
    row_count = picture_embeds.shape[0]
    width = picture_embeds.shape[1]
    group_size = lax.axis_size("in")
    member = lax.axis_index("in")
    sharpness_scalar = sharpness_factor[0]
    additive_term_scalar = additive_shift_term[0]
    row_ids = lax.broadcasted_iota(jnp.int32, (row_count, row_count * group_size), 0)
    col_ids = lax.broadcasted_iota(jnp.int32, (row_count, row_count * group_size), 1)
    matching_mask = (col_ids == row_ids + member * row_count).astype(jnp.float32)
    image_total = jnp.zeros((row_count, width), jnp.float32)
    text_total = jnp.zeros((row_count, width), jnp.float32)
    caption_block, picture_block = (
        lax.all_gather(caption_embeds, "in", axis=0, tiled=True),
        lax.all_gather(picture_embeds, "in", axis=0, tiled=True),
    )
    for batch_start_index in range(STEPS):
        if batch_start_index > 0:
            caption_block = from_behind(caption_block, "grp", 1)
            picture_block = from_behind(picture_block, "grp", -1)
        image_total = image_total + similarity_derivative(
            picture_embeds,
            caption_block,
            sharpness_scalar,
            additive_term_scalar,
            matching_mask,
            batch_start_index == 0,
        )
        text_total = text_total + similarity_derivative(
            caption_embeds,
            picture_block,
            sharpness_scalar,
            additive_term_scalar,
            matching_mask,
            batch_start_index == 0,
        )
    return (image_total.astype(jnp.bfloat16), text_total.astype(jnp.bfloat16))


def solution(mesh):
    placed = (P(("grp", "in"), None), P(("grp", "in"), None), P(), P())
    return jax.shard_map(
        shards,
        mesh=mesh,
        in_specs=placed,
        out_specs=(P(("grp", "in"), None), P(("grp", "in"), None)),
        check_vma=False,
    )
```

profile of v0, /device:TPU:0, one launch (start us, length us, event | category | flops | bytes accessed | tf_op | source)
XLA Modules:
  0.0 96.1 jit_solution(15950280900027180201)
XLA Ops:
  7.2 0.0 all-gather.5.cloned.1.call-start
  7.2 0.7 all-gather.5.cloned.1.call-update
  7.9 0.0 all-gather.3.cloned.1.call-start
  7.9 0.7 all-gather.3.cloned.1.call-update
  8.6 21.1 %all-gather.5.cloned.1.call-done = bf16[512,1152]{1,0:T(8,128)(2,1)} async-done(((bf16[128,1152]{1,0:T(8,128)(2,1)}), bf16[512,1152]{1,0:T(8,128)(2,1)}) %all-gather.5.cloned.1.call-update) | async-done | bytes 1179664 | tf_op jit(solution)/shard_map/all_gather | solution.py:48
  29.7 4.2 %collective-permute-start.1 = (bf16[512,1152]{1,0:T(8,128)(2,1)}, bf16[512,1152]{1,0:T(8,128)(2,1)S(1)}, u32[]{:S(2)}, u32[]{:S(2)}) collective-permute-start(bf16[512,1152]{1,0:T(8,128)(2,1)} %all-gather.5.cloned.1.call-done), channel_id=1, source_target_pairs={{0,28},{4,0},{8,4},{12,8},{16,12},{20,16},{24,20},{28,24},{1,29},{... | collective-permute-start | bytes 3538952 | tf_op jit(solution)/shard_map/ppermute | solution.py:11
  34.0 14.8 %all-gather.3.cloned.1.call-done = bf16[512,1152]{1,0:T(8,128)(2,1)} async-done(((bf16[128,1152]{1,0:T(8,128)(2,1)}), bf16[512,1152]{1,0:T(8,128)(2,1)}) %all-gather.3.cloned.1.call-update) | async-done | bytes 1179664 | tf_op jit(solution)/shard_map/all_gather | solution.py:47
  48.8 1.5 %collective-permute-start = (bf16[512,1152]{1,0:T(8,128)(2,1)}, bf16[512,1152]{1,0:T(8,128)(2,1)}, u32[]{:S(2)}, u32[]{:S(2)}) collective-permute-start(bf16[512,1152]{1,0:T(8,128)(2,1)} %all-gather.3.cloned.1.call-done), channel_id=1, source_target_pairs={{0,4},{4,8},{8,12},{12,16},{16,20},{20,24},{24,28},{28,0},{1,5},{5... | collective-permute-start | bytes 3538952 | tf_op jit(solution)/shard_map/ppermute | solution.py:11
  51.6 0.0 copy-start.1
  51.6 0.0 copy-start.2
  51.6 3.5 %fusion.33 = f32[128,1152]{1,0:T(8,128)} fusion(bf16[512,1152]{1,0:T(8,128)(2,1)} %all-gather.5.cloned.1.call-done, bf16[128,1152]{1,0:T(8,128)(2,1)} %param.5, s32[128]{0:T(128)S(1)} %iota_add_fusion, f32[]{:T(128)} %bitcast.20, f32[]{:T(128)} %bitcast.16), kind=kOutput, calls=%fused_computation.39 | convolution fusion | flops 302645248 | bytes 2064904 | tf_op jit(solution)/shard_map/dot_general | solution.py:31
  55.1 0.0 copy-done.1
  55.1 0.0 copy-done.2
  55.1 0.0 copy-start
  55.1 0.8 fusion.32
  56.0 27.4 %collective-permute-done.1 = bf16[512,1152]{1,0:T(8,128)(2,1)S(1)} collective-permute-done((bf16[512,1152]{1,0:T(8,128)(2,1)}, bf16[512,1152]{1,0:T(8,128)(2,1)S(1)}, u32[]{:S(2)}, u32[]{:S(2)}) %collective-permute-start.1) | collective-permute-done | bytes 1179680 | tf_op jit(solution)/shard_map/ppermute | solution.py:11
  83.3 0.0 copy-done
  83.3 2.6 %fusion.1 = bf16[128,1152]{1,0:T(8,128)(2,1)} fusion(f32[128,1152]{1,0:T(8,128)} %fusion.33, bf16[512,1152]{1,0:T(8,128)(2,1)S(1)} %collective-permute-done.1, bf16[128,1152]{1,0:T(8,128)(2,1)S(1)} %copy-done, f32[]{:T(128)} %bitcast.19, f32[]{:T(128)} %bitcast.14), kind=kOutput, calls=%fused_computation.3 | convolution fusion | flops 302743552 | bytes 2359304 | tf_op jit(solution)/shard_map/dot_general | solution.py:31
  86.0 0.0 collective-permute-done
  86.0 3.2 %fusion = bf16[128,1152]{1,0:T(8,128)(2,1)} fusion(f32[128,1152]{1,0:T(8,128)S(1)} %fusion.32, bf16[512,1152]{1,0:T(8,128)(2,1)} %collective-permute-done, bf16[128,1152]{1,0:T(8,128)(2,1)S(1)} %copy-done.1, f32[]{:T(128)} %bitcast.21, f32[]{:T(128)} %bitcast.15), kind=kOutput, calls=%fused_computation.2 | convolution fusion | flops 302743552 | bytes 2359304 | tf_op jit(solution)/shard_map/dot_general | solution.py:31
  (1 shorter events, 0.0 us)
Async XLA Ops:
  7.2 22.6 %all-gather.5.cloned.1.call-start = ((), (), s32[]{:S(2)}) async-start(), calls=%async_computation.1 | async-start | bytes 1474560 | tf_op jit(solution)/shard_map/all_gather | solution.py:48
  7.9 40.9 %all-gather.3.cloned.1.call-start = ((), (), s32[]{:S(2)}) async-start(), calls=%async_computation | async-start | bytes 1474560 | tf_op jit(solution)/shard_map/all_gather | solution.py:47
  29.7 53.6 %collective-permute-start.1 = (bf16[512,1152]{1,0:T(8,128)(2,1)}, bf16[512,1152]{1,0:T(8,128)(2,1)S(1)}, u32[]{:S(2)}, u32[]{:S(2)}) collective-permute-start(bf16[512,1152]{1,0:T(8,128)(2,1)} %all-gather.5.cloned.1.call-done), channel_id=1, source_target_pairs={{0,28},{4,0},{8,4},{12,8},{16,12},{20,16},{24,20},{28,24},{1,29},{... | collective-permute-start | bytes 3538952 | tf_op jit(solution)/shard_map/ppermute | solution.py:11
  48.8 37.2 %collective-permute-start = (bf16[512,1152]{1,0:T(8,128)(2,1)}, bf16[512,1152]{1,0:T(8,128)(2,1)}, u32[]{:S(2)}, u32[]{:S(2)}) collective-permute-start(bf16[512,1152]{1,0:T(8,128)(2,1)} %all-gather.3.cloned.1.call-done), channel_id=1, source_target_pairs={{0,4},{4,8},{8,12},{12,16},{16,20},{20,24},{24,28},{28,0},{1,5},{5... | collective-permute-start | bytes 3538952 | tf_op jit(solution)/shard_map/ppermute | solution.py:11
  51.6 3.5 %copy-start.1 = (bf16[128,1152]{1,0:T(8,128)(2,1)S(1)}, bf16[128,1152]{1,0:T(8,128)(2,1)}, u32[]{:S(2)}) copy-start(bf16[128,1152]{1,0:T(8,128)(2,1)} %param.4) | copy-start | bytes 884740
  51.6 3.5 %copy-start.2 = (bf16[512,1152]{1,0:T(8,128)(2,1)S(1)}, bf16[512,1152]{1,0:T(8,128)(2,1)}, u32[]{:S(2)}) copy-start(bf16[512,1152]{1,0:T(8,128)(2,1)} %all-gather.3.cloned.1.call-done) | copy-start | bytes 3538948
  55.1 28.2 %copy-start = (bf16[128,1152]{1,0:T(8,128)(2,1)S(1)}, bf16[128,1152]{1,0:T(8,128)(2,1)}, u32[]{:S(2)}) copy-start(bf16[128,1152]{1,0:T(8,128)(2,1)} %param.5) | copy-start | bytes 884740
Sparse Core Ops, SparseCore 0:
  9.6 20.1 all-gather.4
  31.3 17.4 all-gather.2
where the time goes:
time: 96.3 us; the launch traced here: 96.1 us
  waiting for transfers between devices  64.7 us (67%)
  between operations  15.4 us (16%)
  matrix products  10.2 us (11%)
  starting transfers between devices  5.79 us (6%)
    ppermute x2, waiting for transfers between devices, from_behind(): lax.ppermute(array, axis, [(i, (i + by) % peers) for i in range(peers)])  27.4 us
    all_gather x1, waiting for transfers between devices, shards(): lax.all_gather(picture_embeds, 'in', axis=0, tiled=True)  21.1 us
    all_gather x1, waiting for transfers between devices, shards(): lax.all_gather(caption_embeds, 'in', axis=0, tiled=True)  14.8 us
    dot_general x4, matrix products, similarity_derivative(): jnp.dot(label_signs, counterpart_batch, preferred_element_type=jnp.float32)  10.2 us
    ppermute x2, starting transfers between devices, from_behind(): lax.ppermute(array, axis, [(i, (i + by) % peers) for i in range(peers)])  5.71 us
  transfers between devices with their start and end apart: 4, of which 3 were waited for; matrix products, arithmetic and copies ran while one was open for 7% of the time, Pallas kernels for 0%

commit v1 on v0

v1 whole, which is shorter than its diff:
```python
import jax
import jax.numpy as jnp
from jax import lax
from jax.sharding import PartitionSpec as P

CORES = 2


def moved(array, axis, target):
    peers = lax.axis_size(axis)
    return lax.ppermute(array, axis, [(i, target(i) % peers) for i in range(peers)])


def swapped(array):
    return moved(array, "in", lambda i: i ^ 1)


def pulled(rows, others, scale, shift, diagonal):
    total = None
    for position, other in enumerate(others):
        logits = scale * jnp.dot(rows, other.T, preferred_element_type=jnp.float32) + shift
        slope = jax.nn.sigmoid(logits)
        if diagonal and position == 0:
            slope = slope - jnp.eye(rows.shape[0], dtype=jnp.float32)
        weights = (scale * slope).astype(jnp.bfloat16)
        term = jnp.dot(weights, other, preferred_element_type=jnp.float32)
        total = term if total is None else total + term
    return total


def shards(images, texts, sharpness_factor, additive_shift_term):
    scale = sharpness_factor[0]
    shift = additive_shift_term[0]
    chips = lax.axis_size("in") // CORES

    near_images = [moved(images, "in", lambda i, k=k: i - CORES * k) for k in range(1, chips)]
    back_texts = moved(texts, "grp", lambda i: i + 1)
    own_images = [images, swapped(images)]
    own_texts = [texts, swapped(texts)]
    far_images = [swapped(block) for block in near_images]
    all_texts = own_texts + [back_texts, swapped(back_texts)]
    all_images = own_images + near_images + far_images

    sent_images = [
        moved(
            pulled(block, all_texts, scale, shift, False).astype(jnp.bfloat16),
            "in",
            lambda i, k=k: i + CORES * k,
        )
        for k, block in enumerate(near_images, 1)
    ]
    sent_texts = moved(
        pulled(back_texts, all_images, scale, shift, False).astype(jnp.bfloat16),
        "grp",
        lambda i: i - 1,
    )
    image_total = pulled(images, all_texts, scale, shift, True)
    text_total = pulled(texts, all_images, scale, shift, True)
    for block in sent_images:
        image_total = image_total + block.astype(jnp.float32)
    text_total = text_total + sent_texts.astype(jnp.float32)
    return image_total.astype(jnp.bfloat16), text_total.astype(jnp.bfloat16)


def solution(mesh):
    rows = P(("grp", "in"), None)
    return jax.shard_map(
        shards,
        mesh=mesh,
        in_specs=(rows, rows, P(), P()),
        out_specs=(rows, rows),
        check_vma=False,
    )
```

time: 96.3 us -> 43.2 us (0.45)
  waiting for transfers between devices: 64.7 us -> 11.3 us
  between operations: 15.4 us -> 2.02 us
  matrix products: 10.2 us -> 22.3 us
  starting transfers between devices: 5.79 us -> 7.21 us
    all_gather x2 -> x0, waiting for transfers between devices: 35.9 us -> none  [the longest x1 21.1 us: shards(): lax.all_gather(picture_embeds, 'in', axis=0, tiled=True)]
    ppermute x2 -> x8, waiting for transfers between devices: 27.4 us -> 11.3 us  [moved(): lax.ppermute(array, axis, [(i, target(i) % peers) for i in range(peers)])]
    dot_general x4 -> x16, matrix products: 10.2 us -> 22.3 us  [pulled(): term = jnp.dot(weights, other, preferred_element_type=jnp.float32)]
    ppermute x2 -> x8, starting transfers between devices: 5.71 us -> 7.21 us  [moved(): lax.ppermute(array, axis, [(i, target(i) % peers) for i in range(peers)])]
    unnamed x2 -> x0, waiting for transfers between devices: 1.38 us -> none
  transfers between devices with their start and end apart: 4 -> 8, of which waited for: 3 -> 4; matrix products, arithmetic and copies ran while one was open for 7% -> 49% of each run, Pallas kernels for 0% -> 0%
where the time goes in v1:
time: 43.2 us; the launch traced here: 42.8 us
  matrix products  22.3 us (52%)
  waiting for transfers between devices  11.3 us (26%)
  starting transfers between devices  7.21 us (17%)
  between operations  2.02 us (5%)
    dot_general x16, matrix products, pulled(): term = jnp.dot(weights, other, preferred_element_type=jnp.float32)  22.3 us
    ppermute x8, waiting for transfers between devices, moved(): lax.ppermute(array, axis, [(i, target(i) % peers) for i in range(peers)])  11.3 us
    ppermute x8, starting transfers between devices, moved(): lax.ppermute(array, axis, [(i, target(i) % peers) for i in range(peers)])  7.21 us
  transfers between devices with their start and end apart: 8, of which 4 were waited for; matrix products, arithmetic and copies ran while one was open for 49% of the time, Pallas kernels for 0%

profile of v1, /device:TPU:0, one launch (start us, length us, event | category | flops | bytes accessed | tf_op | source)
XLA Modules:
  0.0 42.8 jit_solution(15548310298913134660)
XLA Ops:
  0.6 0.5 %collective-permute-start.5 = (bf16[128,1152]{1,0:T(8,128)(2,1)}, bf16[128,1152]{1,0:T(8,128)(2,1)S(1)}, u32[]{:S(2)}, u32[]{:S(2)}) collective-permute-start(bf16[128,1152]{1,0:T(8,128)(2,1)} %param.4), channel_id=1, source_target_pairs={{0,1},{1,0},{2,3},{3,2},{4,5},{5,4},{6,7},{7,6},{8,9},{9,8},{10,11... | collective-permute-start | bytes 884744 | tf_op jit(solution)/shard_map/ppermute | solution.py:11
  1.1 2.6 %collective-permute-start.3 = (bf16[128,1152]{1,0:T(8,128)(2,1)}, bf16[128,1152]{1,0:T(8,128)(2,1)S(1)}, u32[]{:S(2)}, u32[]{:S(2)}) collective-permute-start(bf16[128,1152]{1,0:T(8,128)(2,1)} %param.4), channel_id=1, source_target_pairs={{0,2},{1,3},{2,0},{3,1},{4,6},{5,7},{6,4},{7,5},{8,10},{9,11},{10,... | collective-permute-start | bytes 884744 | tf_op jit(solution)/shard_map/ppermute | solution.py:11
  3.7 1.5 %collective-permute-start.1 = (bf16[128,1152]{1,0:T(8,128)(2,1)}, bf16[128,1152]{1,0:T(8,128)(2,1)S(1)}, u32[]{:S(2)}, u32[]{:S(2)}) collective-permute-start(bf16[128,1152]{1,0:T(8,128)(2,1)} %param.5), channel_id=1, source_target_pairs={{0,4},{4,8},{8,12},{12,16},{16,20},{20,24},{24,28},{28,0},{1,5},{5... | collective-permute-start | bytes 884744 | tf_op jit(solution)/shard_map/ppermute | solution.py:11
  5.2 0.0 collective-permute-start
  6.5 0.0 copy-start
  6.5 0.0 copy-start.1
  6.6 2.6 %fusion.122 = f32[128,1152]{1,0:T(8,128)} fusion(bf16[128,1152]{1,0:T(8,128)(2,1)} %param.4, bf16[128,1152]{1,0:T(8,128)(2,1)} %param.5, f32[]{:T(128)} %bitcast.74, f32[]{:T(128)} %bitcast.64), kind=kOutput, calls=%fused_computation.150 | convolution fusion | flops 75661312 | bytes 1179656 | tf_op jit(solution)/shard_map/dot_general | solution.py:26
  9.1 0.0 copy-done
  9.1 0.0 copy-done.1
  9.1 1.4 %fusion.123 = f32[128,1152]{1,0:T(8,128)} fusion(bf16[128,1152]{1,0:T(8,128)(2,1)S(1)} %copy-done, bf16[128,1152]{1,0:T(8,128)(2,1)S(1)} %copy-done.1, f32[]{:T(128)} %bitcast.66, f32[]{:T(128)} %bitcast.65), kind=kOutput, calls=%fused_computation.151 | convolution fusion | flops 75661312 | bytes 1179656 | tf_op jit(solution)/shard_map/dot_general | solution.py:26
  10.5 1.0 %collective-permute-done.3 = bf16[128,1152]{1,0:T(8,128)(2,1)S(1)} collective-permute-done((bf16[128,1152]{1,0:T(8,128)(2,1)}, bf16[128,1152]{1,0:T(8,128)(2,1)S(1)}, u32[]{:S(2)}, u32[]{:S(2)}) %collective-permute-start.3) | collective-permute-done | bytes 294944 | tf_op jit(solution)/shard_map/ppermute | solution.py:11
  11.5 0.0 collective-permute-start.6
  11.5 4.3 %collective-permute-done.1 = bf16[128,1152]{1,0:T(8,128)(2,1)S(1)} collective-permute-done((bf16[128,1152]{1,0:T(8,128)(2,1)}, bf16[128,1152]{1,0:T(8,128)(2,1)S(1)}, u32[]{:S(2)}, u32[]{:S(2)}) %collective-permute-start.1) | collective-permute-done | bytes 294944 | tf_op jit(solution)/shard_map/ppermute | solution.py:11
  15.8 0.0 collective-permute-start.2
  15.8 0.5 %fusion.120 = f32[128,1152]{1,0:T(8,128)S(1)} fusion(bf16[128,1152]{1,0:T(8,128)(2,1)S(1)} %copy-done.1, bf16[128,1152]{1,0:T(8,128)(2,1)S(1)} %collective-permute-done.1, f32[]{:T(128)} %bitcast.70, f32[]{:T(128)} %bitcast.62), kind=kOutput, calls=%fused_computation.148 | convolution fusion | flops 75612160 | bytes 1179656 | tf_op jit(solution)/shard_map/dot_general | solution.py:26
  16.4 0.0 collective-permute-done.5
  16.4 0.5 %convolution_add_fusion.2 = f32[128,1152]{1,0:T(8,128)S(1)} fusion(f32[128,1152]{1,0:T(8,128)S(1)} %fusion.120, bf16[128,1152]{1,0:T(8,128)(2,1)S(1)} %collective-permute-done.5, bf16[128,1152]{1,0:T(8,128)(2,1)S(1)} %collective-permute-done.1, f32[]{:T(128)} %bitcast.69, f32[]{:T(128)} %bitcast.54), kind=kOutput, calls=%fused_computation.2 | convolution fusion | flops 75759616 | bytes 1769480 | tf_op jit(solution)/shard_map/dot_general | solution.py:26
  16.9 1.4 %convolution_add_fusion.1 = f32[128,1152]{1,0:T(8,128)} fusion(f32[128,1152]{1,0:T(8,128)S(1)} %convolution_add_fusion.2, bf16[128,1152]{1,0:T(8,128)(2,1)S(1)} %collective-permute-done.3, bf16[128,1152]{1,0:T(8,128)(2,1)S(1)} %collective-permute-done.1, f32[]{:T(128)} %bitcast.68, f32[]{:T(128)} %bitcast.58), kind=kOutput, calls=%fused_computation.1 | convolution fusion | flops 75759616 | bytes 1769480 | tf_op jit(solution)/shard_map/dot_general | solution.py:26
  18.3 1.6 %convolution_add_fusion.5 = f32[128,1152]{1,0:T(8,128)S(1)} fusion(f32[128,1152]{1,0:T(8,128)} %fusion.122, bf16[128,1152]{1,0:T(8,128)(2,1)S(1)} %collective-permute-done.5, bf16[128,1152]{1,0:T(8,128)(2,1)S(1)} %copy-done, f32[]{:T(128)} %bitcast.73, f32[]{:T(128)} %bitcast.60), kind=kOutput, calls=%fused_computation.6 | convolution fusion | flops 75759616 | bytes 1769480 | tf_op jit(solution)/shard_map/dot_general | solution.py:26
  19.9 1.4 %fusion.121 = f32[128,1152]{1,0:T(8,128)} fusion(bf16[128,1152]{1,0:T(8,128)(2,1)S(1)} %copy-done, bf16[128,1152]{1,0:T(8,128)(2,1)S(1)} %collective-permute-done.3, f32[]{:T(128)} %bitcast.78, f32[]{:T(128)} %bitcast.57), kind=kOutput, calls=%fused_computation.149 | convolution fusion | flops 75612160 | bytes 1179656 | tf_op jit(solution)/shard_map/dot_general | solution.py:26
  21.3 0.5 %convolution_add_fusion.4 = f32[128,1152]{1,0:T(8,128)S(1)} fusion(f32[128,1152]{1,0:T(8,128)S(1)} %convolution_add_fusion.5, bf16[128,1152]{1,0:T(8,128)(2,1)S(1)} %collective-permute-done.3, bf16[128,1152]{1,0:T(8,128)(2,1)S(1)} %copy-done, f32[]{:T(128)} %bitcast.72, f32[]{:T(128)} %bitcast.56), kind=kOutput, calls=%fused_computation.5 | convolution fusion | flops 75759616 | bytes 1769480 | tf_op jit(solution)/shard_map/dot_general | solution.py:26
  21.8 0.0 collective-permute-done
  21.8 1.6 %convolution_add_fusion.8 = f32[128,1152]{1,0:T(8,128)S(1)} fusion(f32[128,1152]{1,0:T(8,128)} %fusion.121, bf16[128,1152]{1,0:T(8,128)(2,1)S(1)} %collective-permute-done, bf16[128,1152]{1,0:T(8,128)(2,1)S(1)} %collective-permute-done.3, f32[]{:T(128)} %bitcast.77, f32[]{:T(128)} %bitcast.55), kind=kOutput, calls=%fused_computation.9 | convolution fusion | flops 75759616 | bytes 1769480 | tf_op jit(solution)/shard_map/dot_general | solution.py:26
  23.4 1.4 %convolution_add_fusion.7 = f32[128,1152]{1,0:T(8,128)} fusion(f32[128,1152]{1,0:T(8,128)S(1)} %convolution_add_fusion.8, bf16[128,1152]{1,0:T(8,128)(2,1)S(1)} %collective-permute-done.1, bf16[128,1152]{1,0:T(8,128)(2,1)S(1)} %collective-permute-done.3, f32[]{:T(128)} %bitcast.76, f32[]{:T(128)} %bitcast.53), kind=kOutput, calls=%fused_computation.8 | convolution fusion | flops 75759616 | bytes 1769480 | tf_op jit(solution)/shard_map/dot_general | solution.py:26
  24.8 1.6 %convolution_add_fusion.11 = f32[128,1152]{1,0:T(8,128)S(1)} fusion(f32[128,1152]{1,0:T(8,128)} %fusion.123, bf16[128,1152]{1,0:T(8,128)(2,1)S(1)} %collective-permute-done, bf16[128,1152]{1,0:T(8,128)(2,1)S(1)} %copy-done.1, f32[]{:T(128)} %bitcast.81, f32[]{:T(128)} %bitcast.63), kind=kOutput, calls=%fused_computation.13 | convolution fusion | flops 75759616 | bytes 1769480 | tf_op jit(solution)/shard_map/dot_general | solution.py:26
  26.4 0.0 collective-permute-done.6
  26.4 1.6 %fusion.5 = bf16[128,1152]{1,0:T(8,128)(2,1)S(1)} fusion(f32[128,1152]{1,0:T(8,128)} %convolution_add_fusion.1, bf16[128,1152]{1,0:T(8,128)(2,1)S(1)} %collective-permute-done.6, bf16[128,1152]{1,0:T(8,128)(2,1)S(1)} %collective-permute-done.1, f32[]{:T(128)} %bitcast.67, f32[]{:T(128)} %bitcast.50), kind=kOutput, calls=%fused_computation.17 | convolution fusion | flops 75907072 | bytes 1474568 | tf_op jit(solution)/shard_map/dot_general | solution.py:26
  28.1 1.8 %collective-permute-start.7 = (bf16[128,1152]{1,0:T(8,128)(2,1)S(1)}, bf16[128,1152]{1,0:T(8,128)(2,1)S(1)}, u32[]{:S(2)}, u32[]{:S(2)}) collective-permute-start(bf16[128,1152]{1,0:T(8,128)(2,1)S(1)} %fusion.5), channel_id=1, source_target_pairs={{0,28},{4,0},{8,4},{12,8},{16,12},{20,16},{24,20},{28,24},{1,29},{... | collective-permute-start | bytes 884744 | tf_op jit(solution)/shard_map/ppermute | solution.py:11
  29.9 0.0 collective-permute-done.2
  29.9 2.3 %fusion.3 = bf16[128,1152]{1,0:T(8,128)(2,1)} fusion(f32[128,1152]{1,0:T(8,128)} %convolution_add_fusion.7, bf16[128,1152]{1,0:T(8,128)(2,1)S(1)} %collective-permute-done.2, bf16[128,1152]{1,0:T(8,128)(2,1)S(1)} %collective-permute-done.3, f32[]{:T(128)} %bitcast.75, f32[]{:T(128)} %bitcast.51), kind=kOutput, calls=%fused_computation.15 | convolution fusion | flops 75907072 | bytes 1474568 | tf_op jit(solution)/shard_map/dot_general | solution.py:26
  32.2 0.8 %collective-permute-start.4 = (bf16[128,1152]{1,0:T(8,128)(2,1)}, bf16[128,1152]{1,0:T(8,128)(2,1)S(1)}, u32[]{:S(2)}, u32[]{:S(2)}) collective-permute-start(bf16[128,1152]{1,0:T(8,128)(2,1)} %fusion.3), channel_id=1, source_target_pairs={{0,2},{1,3},{2,0},{3,1},{4,6},{5,7},{6,4},{7,5},{8,10},{9,11},{10,... | collective-permute-start | bytes 884744 | tf_op jit(solution)/shard_map/ppermute | solution.py:11
  33.0 1.4 %convolution_add_fusion.10 = f32[128,1152]{1,0:T(8,128)} fusion(f32[128,1152]{1,0:T(8,128)S(1)} %convolution_add_fusion.11, bf16[128,1152]{1,0:T(8,128)(2,1)S(1)} %collective-permute-done.1, bf16[128,1152]{1,0:T(8,128)(2,1)S(1)} %copy-done.1, f32[]{:T(128)} %bitcast.80, f32[]{:T(128)} %bitcast.61), kind=kOutput, calls=%fused_computation.12 | convolution fusion | flops 75759616 | bytes 1769480 | tf_op jit(solution)/shard_map/dot_general | solution.py:26
  34.3 3.2 %collective-permute-done.7 = bf16[128,1152]{1,0:T(8,128)(2,1)S(1)} collective-permute-done((bf16[128,1152]{1,0:T(8,128)(2,1)S(1)}, bf16[128,1152]{1,0:T(8,128)(2,1)S(1)}, u32[]{:S(2)}, u32[]{:S(2)}) %collective-permute-start.7) | collective-permute-done | bytes 294944 | tf_op jit(solution)/shard_map/ppermute | solution.py:11
  37.5 0.0 copy-start.2
  37.5 1.3 %fusion.4 = bf16[128,1152]{1,0:T(8,128)(2,1)} fusion(f32[128,1152]{1,0:T(8,128)S(1)} %convolution_add_fusion.4, bf16[128,1152]{1,0:T(8,128)(2,1)S(1)} %collective-permute-done.6, bf16[128,1152]{1,0:T(8,128)(2,1)S(1)} %copy-done, bf16[128,1152]{1,0:T(8,128)(2,1)S(1)} %collective-permute-done.7, f32[]{:T(128)} %bitcast.71, f32[]{:T(128)} %bitcast.52), kind=kOutput, calls=%fused_computation.16 | convolution fusion | flops 76201984 | bytes 1769480 | tf_op jit(solution)/shard_map/dot_general | solution.py:26
  38.8 2.7 %collective-permute-done.4 = bf16[128,1152]{1,0:T(8,128)(2,1)S(1)} collective-permute-done((bf16[128,1152]{1,0:T(8,128)(2,1)}, bf16[128,1152]{1,0:T(8,128)(2,1)S(1)}, u32[]{:S(2)}, u32[]{:S(2)}) %collective-permute-start.4) | collective-permute-done | bytes 294944 | tf_op jit(solution)/shard_map/ppermute | solution.py:11
  41.5 0.0 copy-done.2
  41.5 1.3 %fusion.2 = bf16[128,1152]{1,0:T(8,128)(2,1)} fusion(f32[128,1152]{1,0:T(8,128)S(1)} %copy-done.2, bf16[128,1152]{1,0:T(8,128)(2,1)S(1)} %collective-permute-done.2, bf16[128,1152]{1,0:T(8,128)(2,1)S(1)} %copy-done.1, bf16[128,1152]{1,0:T(8,128)(2,1)S(1)} %collective-permute-done.4, f32[]{:T(128)} %bitcast.79, f32[]{:T(128)} %bitcast.59), kind=kOutput, calls=%fused_computation.14 | convolution fusion | flops 76201984 | bytes 1769480 | tf_op jit(solution)/shard_map/dot_general | solution.py:26
Async XLA Ops:
  0.6 15.7 %collective-permute-start.5 = (bf16[128,1152]{1,0:T(8,128)(2,1)}, bf16[128,1152]{1,0:T(8,128)(2,1)S(1)}, u32[]{:S(2)}, u32[]{:S(2)}) collective-permute-start(bf16[128,1152]{1,0:T(8,128)(2,1)} %param.4), channel_id=1, source_target_pairs={{0,1},{1,0},{2,3},{3,2},{4,5},{5,4},{6,7},{7,6},{8,9},{9,8},{10,11... | collective-permute-start | bytes 884744 | tf_op jit(solution)/shard_map/ppermute | solution.py:11
  1.1 10.4 %collective-permute-start.3 = (bf16[128,1152]{1,0:T(8,128)(2,1)}, bf16[128,1152]{1,0:T(8,128)(2,1)S(1)}, u32[]{:S(2)}, u32[]{:S(2)}) collective-permute-start(bf16[128,1152]{1,0:T(8,128)(2,1)} %param.4), channel_id=1, source_target_pairs={{0,2},{1,3},{2,0},{3,1},{4,6},{5,7},{6,4},{7,5},{8,10},{9,11},{10,... | collective-permute-start | bytes 884744 | tf_op jit(solution)/shard_map/ppermute | solution.py:11
  3.7 12.1 %collective-permute-start.1 = (bf16[128,1152]{1,0:T(8,128)(2,1)}, bf16[128,1152]{1,0:T(8,128)(2,1)S(1)}, u32[]{:S(2)}, u32[]{:S(2)}) collective-permute-start(bf16[128,1152]{1,0:T(8,128)(2,1)} %param.5), channel_id=1, source_target_pairs={{0,4},{4,8},{8,12},{12,16},{16,20},{20,24},{24,28},{28,0},{1,5},{5... | collective-permute-start | bytes 884744 | tf_op jit(solution)/shard_map/ppermute | solution.py:11
  5.2 16.6 %collective-permute-start = (bf16[128,1152]{1,0:T(8,128)(2,1)}, bf16[128,1152]{1,0:T(8,128)(2,1)S(1)}, u32[]{:S(2)}, u32[]{:S(2)}) collective-permute-start(bf16[128,1152]{1,0:T(8,128)(2,1)} %param.5), channel_id=1, source_target_pairs={{0,1},{1,0},{2,3},{3,2},{4,5},{5,4},{6,7},{7,6},{8,9},{9,8},{10,11... | collective-permute-start | bytes 884744 | tf_op jit(solution)/shard_map/ppermute | solution.py:11
  6.5 2.6 %copy-start = (bf16[128,1152]{1,0:T(8,128)(2,1)S(1)}, bf16[128,1152]{1,0:T(8,128)(2,1)}, u32[]{:S(2)}) copy-start(bf16[128,1152]{1,0:T(8,128)(2,1)} %param.5) | copy-start | bytes 884740
  6.5 2.6 %copy-start.1 = (bf16[128,1152]{1,0:T(8,128)(2,1)S(1)}, bf16[128,1152]{1,0:T(8,128)(2,1)}, u32[]{:S(2)}) copy-start(bf16[128,1152]{1,0:T(8,128)(2,1)} %param.4) | copy-start | bytes 884740
  11.5 14.9 %collective-permute-start.6 = (bf16[128,1152]{1,0:T(8,128)(2,1)S(1)}, bf16[128,1152]{1,0:T(8,128)(2,1)S(1)}, u32[]{:S(2)}, u32[]{:S(2)}) collective-permute-start(bf16[128,1152]{1,0:T(8,128)(2,1)S(1)} %collective-permute-done.3), channel_id=1, source_target_pairs={{0,1},{1,0},{2,3},{3,2},{4,5},{5,4},{6,7},{7,6},{8,9},{9,8},{10,11... | collective-permute-start | bytes 884744 | tf_op jit(solution)/shard_map/ppermute | solution.py:11
  15.8 14.0 %collective-permute-start.2 = (bf16[128,1152]{1,0:T(8,128)(2,1)S(1)}, bf16[128,1152]{1,0:T(8,128)(2,1)S(1)}, u32[]{:S(2)}, u32[]{:S(2)}) collective-permute-start(bf16[128,1152]{1,0:T(8,128)(2,1)S(1)} %collective-permute-done.1), channel_id=1, source_target_pairs={{0,1},{1,0},{2,3},{3,2},{4,5},{5,4},{6,7},{7,6},{8,9},{9,8},{10,11... | collective-permute-start | bytes 884744 | tf_op jit(solution)/shard_map/ppermute | solution.py:11
  28.1 9.5 %collective-permute-start.7 = (bf16[128,1152]{1,0:T(8,128)(2,1)S(1)}, bf16[128,1152]{1,0:T(8,128)(2,1)S(1)}, u32[]{:S(2)}, u32[]{:S(2)}) collective-permute-start(bf16[128,1152]{1,0:T(8,128)(2,1)S(1)} %fusion.5), channel_id=1, source_target_pairs={{0,28},{4,0},{8,4},{12,8},{16,12},{20,16},{24,20},{28,24},{1,29},{... | collective-permute-start | bytes 884744 | tf_op jit(solution)/shard_map/ppermute | solution.py:11
  32.2 9.3 %collective-permute-start.4 = (bf16[128,1152]{1,0:T(8,128)(2,1)}, bf16[128,1152]{1,0:T(8,128)(2,1)S(1)}, u32[]{:S(2)}, u32[]{:S(2)}) collective-permute-start(bf16[128,1152]{1,0:T(8,128)(2,1)} %fusion.3), channel_id=1, source_target_pairs={{0,2},{1,3},{2,0},{3,1},{4,6},{5,7},{6,4},{7,5},{8,10},{9,11},{10,... | collective-permute-start | bytes 884744 | tf_op jit(solution)/shard_map/ppermute | solution.py:11
  37.5 4.0 %copy-start.2 = (f32[128,1152]{1,0:T(8,128)S(1)}, f32[128,1152]{1,0:T(8,128)}, u32[]{:S(2)}) copy-start(f32[128,1152]{1,0:T(8,128)} %convolution_add_fusion.10) | copy-start | bytes 1769476

commit v2 on v1

v2 whole, which is shorter than its diff:
```python
import jax
import jax.numpy as jnp
from jax import lax
from jax.experimental import pallas as pl
from jax.experimental.pallas import tpu as pltpu
from jax.sharding import PartitionSpec as P

CORES = 2


def moved(array, axis, target):
    peers = lax.axis_size(axis)
    return lax.ppermute(array, axis, [(i, target(i) % peers) for i in range(peers)])


def swapped(array):
    return moved(array, "in", lambda i: i ^ 1)


def pulled(rows, others, starts, pair, out_types, scale, shift):
    height, width = rows[0].shape
    n_rows, n_others, n_starts = len(rows), len(others), len(starts)

    def kernel(scale_ref, shift_ref, *refs):
        row_refs = refs[:n_rows]
        other_refs = refs[n_rows : n_rows + n_others]
        start_refs = refs[n_rows + n_others : n_rows + n_others + n_starts]
        out_refs = refs[n_rows + n_others + n_starts :]
        scale_now, shift_now = scale_ref[0], shift_ref[0]
        left = jnp.concatenate([ref[...] for ref in row_refs], axis=0)
        right = jnp.concatenate([ref[...] for ref in other_refs], axis=0)
        logits = lax.dot_general(
            left, right, (((1,), (1,)), ((), ())), preferred_element_type=jnp.float32
        )
        slope = jax.nn.sigmoid(scale_now * logits + shift_now)
        if pair is not None:
            row_ids = lax.broadcasted_iota(jnp.int32, slope.shape, 0)
            col_ids = lax.broadcasted_iota(jnp.int32, slope.shape, 1)
            matched = (col_ids - row_ids == (pair[1] - pair[0]) * height) & (
                row_ids // height == pair[0]
            )
            slope = slope - matched.astype(jnp.float32)
        weights = (scale_now * slope).astype(jnp.bfloat16)
        terms = jnp.dot(weights, right, preferred_element_type=jnp.float32)
        for i, out_ref in enumerate(out_refs):
            term = terms[i * height : (i + 1) * height]
            if n_starts:
                term = term + start_refs[i][...]
            out_ref[...] = term.astype(out_ref.dtype)

    vmem = pl.BlockSpec(memory_space=pltpu.VMEM)
    smem = pl.BlockSpec(memory_space=pltpu.SMEM)
    flops = 4 * height * height * width * n_rows * n_others
    return pl.pallas_call(
        kernel,
        out_shape=[jax.ShapeDtypeStruct((height, width), t) for t in out_types],
        in_specs=[smem, smem] + [vmem] * (n_rows + n_others + n_starts),
        out_specs=[vmem] * n_rows,
        cost_estimate=pl.CostEstimate(flops=flops, bytes_accessed=0, transcendentals=0),
    )(scale, shift, *rows, *others, *starts)


def shards(images, texts, scale, shift):
    chips = lax.axis_size("in") // CORES
    f32, bf16 = jnp.float32, jnp.bfloat16

    back_texts = moved(texts, "grp", lambda i: i + 1)
    near_images = [moved(images, "in", lambda i, k=k: i - CORES * k) for k in range(1, chips)]
    core_images, core_texts = swapped(images), swapped(texts)
    far_images = [swapped(block) for block in near_images]
    far_texts = swapped(back_texts)

    rows = [images] + near_images
    starts = pulled(
        rows, [texts, core_texts], [], (0, 0), [f32] * chips, scale, shift
    )
    text_total, sent_texts = pulled(
        [texts, back_texts],
        [images, core_images] + near_images + far_images,
        [],
        (0, 0),
        [f32, bf16],
        scale,
        shift,
    )
    sent_texts = moved(sent_texts, "grp", lambda i: i - 1)
    image_total, *sent_images = pulled(
        rows, [back_texts, far_texts], starts, None, [f32] + [bf16] * (chips - 1), scale, shift
    )
    for k, block in enumerate(sent_images, 1):
        image_total = image_total + moved(block, "in", lambda i, k=k: i + CORES * k).astype(f32)
    text_total = text_total + sent_texts.astype(f32)
    return image_total.astype(bf16), text_total.astype(bf16)


def solution(mesh):
    rows = P(("grp", "in"), None)
    return jax.shard_map(
        shards,
        mesh=mesh,
        in_specs=(rows, rows, P(), P()),
        out_specs=(rows, rows),
        check_vma=False,
    )
```

time: 43.2 us -> 40.6 us (0.940)
  matrix products: 22.3 us -> 0 us
  Pallas kernels: 0 us -> 9.93 us
  waiting for transfers between devices: 11.3 us -> 15.1 us
  local copies, waits for them, and re-layouts: 0.01 us -> 3.49 us
  other arithmetic: 0 us -> 1.53 us
  starting transfers between devices: 7.21 us -> 8.32 us
    dot_general x16 -> x0, matrix products: 22.3 us -> none  [pulled(): term = jnp.dot(weights, other, preferred_element_type=jnp.float32)]
    pallas_call x0 -> x3, Pallas kernels: none -> 9.93 us  [pulled(): pl.pallas_call(kernel, out_shape=[jax.ShapeDtypeStruct((height, width), t...]
    ppermute x8, waiting for transfers between devices: 11.3 us -> 15.1 us  [moved(): lax.ppermute(array, axis, [(i, target(i) % peers) for i in range(peers)])]
    unnamed x6 -> x16, local copies, waits for them, and re-layouts: 0.01 us -> 3.49 us
    convert_element_type x0 -> x2, other arithmetic: none -> 1.53 us  [shards(): return (image_total.astype(bf16), text_total.astype(bf16))]
    ppermute x8, starting transfers between devices: 7.21 us -> 8.32 us  [moved(): lax.ppermute(array, axis, [(i, target(i) % peers) for i in range(peers)])]
  transfers between devices with their start and end apart: 8 -> 8, of which waited for: 4 -> 3; matrix products, arithmetic and copies ran while one was open for 49% -> 2% of each run, Pallas kernels for 0% -> 25%
where the time goes in v2:
time: 40.6 us; the launch traced here: 40.4 us
  waiting for transfers between devices  15.1 us (37%)
  Pallas kernels  9.93 us (24%)
  starting transfers between devices  8.32 us (20%)
  local copies, waits for them, and re-layouts  3.49 us (9%)
  between operations  1.98 us (5%)
  other arithmetic  1.53 us (4%)
    ppermute x8, waiting for transfers between devices, moved(): lax.ppermute(array, axis, [(i, target(i) % peers) for i in range(peers)])  15.1 us
    pallas_call x3, Pallas kernels, pulled(): pl.pallas_call(kernel, out_shape=[jax.ShapeDtypeStruct((height, width), t...  9.93 us
    ppermute x8, starting transfers between devices, moved(): lax.ppermute(array, axis, [(i, target(i) % peers) for i in range(peers)])  8.32 us
    unnamed x16, local copies, waits for them, and re-layouts  3.49 us
    convert_element_type x2, other arithmetic, shards(): return (image_total.astype(bf16), text_total.astype(bf16))  1.53 us
  transfers between devices with their start and end apart: 8, of which 3 were waited for; matrix products, arithmetic and copies ran while one was open for 2% of the time, Pallas kernels for 25%

profile of v2, /device:TPU:0, one launch (start us, length us, event | category | flops | bytes accessed | tf_op | source)
XLA Modules:
  0.0 40.4 jit_solution(16693728454275435412)
XLA Ops:
  0.6 3.0 %collective-permute-start.1 = (bf16[128,1152]{1,0:T(8,128)(2,1)}, bf16[128,1152]{1,0:T(8,128)(2,1)S(1)}, u32[]{:S(2)}, u32[]{:S(2)}) collective-permute-start(bf16[128,1152]{1,0:T(8,128)(2,1)} %refs_0_.5), channel_id=1, source_target_pairs={{0,4},{4,8},{8,12},{12,16},{16,20},{20,24},{24,28},{28,0},{1,5},{5... | collective-permute-start | bytes 884744 | tf_op jit(solution)/shard_map/ppermute | solution.py:13
  3.6 1.5 %collective-permute-start = (bf16[128,1152]{1,0:T(8,128)(2,1)}, bf16[128,1152]{1,0:T(8,128)(2,1)S(1)}, u32[]{:S(2)}, u32[]{:S(2)}) collective-permute-start(bf16[128,1152]{1,0:T(8,128)(2,1)} %refs_2_.3), channel_id=1, source_target_pairs={{0,2},{1,3},{2,0},{3,1},{4,6},{5,7},{6,4},{7,5},{8,10},{9,11},{10,... | collective-permute-start | bytes 884744 | tf_op jit(solution)/shard_map/ppermute | solution.py:13
  5.1 0.0 collective-permute-start.3
  5.1 8.8 %collective-permute-done.1.refs_2_.refs_1_ = bf16[128,1152]{1,0:T(8,128)(2,1)S(1)} collective-permute-done((bf16[128,1152]{1,0:T(8,128)(2,1)}, bf16[128,1152]{1,0:T(8,128)(2,1)S(1)}, u32[]{:S(2)}, u32[]{:S(2)}) %collective-permute-start.1) | collective-permute-done | bytes 294944 | tf_op jit(solution)/shard_map/ppermute | solution.py:13
  13.9 0.0 copy-start.3
  13.9 0.0 collective-permute-start.2
  13.9 0.5 %collective-permute-start.5 = (bf16[128,1152]{1,0:T(8,128)(2,1)}, bf16[128,1152]{1,0:T(8,128)(2,1)S(1)}, u32[]{:S(2)}, u32[]{:S(2)}) collective-permute-start(bf16[128,1152]{1,0:T(8,128)(2,1)} %refs_2_.3), channel_id=1, source_target_pairs={{0,1},{1,0},{2,3},{3,2},{4,5},{5,4},{6,7},{7,6},{8,9},{9,8},{10,11... | collective-permute-start | bytes 884744 | tf_op jit(solution)/shard_map/ppermute | solution.py:13
  15.7 0.0 collective-permute-done.refs_1_.refs_4_
  15.7 0.0 copy-start
  15.7 0.1 collective-permute-start.6
  15.8 0.0 collective-permute-done.3.refs_3_
  15.8 0.6 %copy-done = bf16[128,1152]{1,0:T(8,128)(2,1)} copy-done((bf16[128,1152]{1,0:T(8,128)(2,1)}, bf16[128,1152]{1,0:T(8,128)(2,1)S(1)}, u32[]{:S(2)}) %copy-start) | copy-done | bytes 294936
  16.4 0.0 copy-start.5
  16.4 0.7 %copy-done.5 = bf16[128,1152]{1,0:T(8,128)(2,1)} copy-done((bf16[128,1152]{1,0:T(8,128)(2,1)}, bf16[128,1152]{1,0:T(8,128)(2,1)S(1)}, u32[]{:S(2)}) %copy-start.5) | copy-done | bytes 294936
  17.2 3.2 %shard_map.59 = (f32[128,1152]{1,0:T(8,128)}, f32[128,1152]{1,0:T(8,128)}) custom-call(f32[1]{0:T(128)S(6)} %copy.6.scale_ref, f32[1]{0:T(128)S(6)} %copy.7.shift_ref, bf16[128,1152]{1,0:T(8,128)(2,1)} %refs_2_.3, bf16[128,1152]{1,0:T(8,128)(2,1)} %copy-done, bf16[128,1152]{1,0:T(8,128)(2,1)} %refs_0_.5, bf16[128,1152]{1,0:T(8,128)(2,1)} %copy-done.5), custom_call_target="tpu_custom_call" | custom-call | flops 301989888 | tf_op jit(solution)/shard_map/pallas_call | solution.py:54
  20.4 0.0 collective-permute-done.2.refs_3_
  20.4 0.0 copy-start.4
  20.4 0.0 copy-done.3
  20.4 0.7 %copy-done.4 = bf16[128,1152]{1,0:T(8,128)(2,1)} copy-done((bf16[128,1152]{1,0:T(8,128)(2,1)}, bf16[128,1152]{1,0:T(8,128)(2,1)S(1)}, u32[]{:S(2)}) %copy-start.4) | copy-done | bytes 294936
  21.1 3.4 %shard_map.60 = (f32[128,1152]{1,0:T(8,128)}, bf16[128,1152]{1,0:T(8,128)(2,1)}) custom-call(f32[1]{0:T(128)S(6)} %copy.6.scale_ref, f32[1]{0:T(128)S(6)} %copy.7.shift_ref, bf16[128,1152]{1,0:T(8,128)(2,1)} %refs_2_.3, bf16[128,1152]{1,0:T(8,128)(2,1)} %copy-done, bf16[128,1152]{1,0:T(8,128)(2,1)} %copy-done.3, bf16[128,1152]{1,0:T(8,128)(2,1)} %copy-done.4, ...), custom_call_target="tpu_custom_call" | custom-call | flops 301989888 | tf_op jit(solution)/shard_map/pallas_call | solution.py:54
  24.5 0.0 copy-start.1
  24.5 1.5 %collective-permute-start.4 = (bf16[128,1152]{1,0:T(8,128)(2,1)}, bf16[128,1152]{1,0:T(8,128)(2,1)S(1)}, u32[]{:S(2)}, u32[]{:S(2)}) collective-permute-start(bf16[128,1152]{1,0:T(8,128)(2,1)} %get-tuple-element.11), channel_id=1, source_target_pairs={{0,2},{1,3},{2,0},{3,1},{4,6},{5,7},{6,4},{7,5},{8,10},{9,11},{10,... | collective-permute-start | bytes 884744 | tf_op jit(solution)/shard_map/ppermute | solution.py:13
  26.0 0.0 collective-permute-done.5.refs_3_
  26.0 0.0 copy-start.6
  26.0 0.0 collective-permute-done.6.refs_5_
  26.0 0.7 %copy-done.6 = bf16[128,1152]{1,0:T(8,128)(2,1)} copy-done((bf16[128,1152]{1,0:T(8,128)(2,1)}, bf16[128,1152]{1,0:T(8,128)(2,1)S(1)}, u32[]{:S(2)}) %copy-start.6) | copy-done | bytes 294936
  26.7 0.0 copy-start.7
  26.7 0.7 %copy-done.7 = bf16[128,1152]{1,0:T(8,128)(2,1)} copy-done((bf16[128,1152]{1,0:T(8,128)(2,1)}, bf16[128,1152]{1,0:T(8,128)(2,1)S(1)}, u32[]{:S(2)}) %copy-start.7) | copy-done | bytes 294936
  27.5 3.3 %shard_map.61 = (f32[128,1152]{1,0:T(8,128)}, bf16[128,1152]{1,0:T(8,128)(2,1)}) custom-call(f32[1]{0:T(128)S(6)} %copy.6.scale_ref, f32[1]{0:T(128)S(6)} %copy.7.shift_ref, bf16[128,1152]{1,0:T(8,128)(2,1)} %refs_0_.5, bf16[128,1152]{1,0:T(8,128)(2,1)} %copy-done.3, bf16[128,1152]{1,0:T(8,128)(2,1)} %refs_2_.3, bf16[128,1152]{1,0:T(8,128)(2,1)} %copy-done.6, ...), custom_call_target="tpu_custom_call" | custom-call | flops 603979776 | tf_op jit(solution)/shard_map/pallas_call | solution.py:54
  30.8 1.7 %collective-permute-start.7 = (bf16[128,1152]{1,0:T(8,128)(2,1)}, bf16[128,1152]{1,0:T(8,128)(2,1)S(1)}, u32[]{:S(2)}, u32[]{:S(2)}) collective-permute-start(bf16[128,1152]{1,0:T(8,128)(2,1)} %get-tuple-element.13), channel_id=1, source_target_pairs={{0,28},{4,0},{8,4},{12,8},{16,12},{20,16},{24,20},{28,24},{1,29},{... | collective-permute-start | bytes 884744 | tf_op jit(solution)/shard_map/ppermute | solution.py:13
  32.5 1.1 %collective-permute-done.4 = bf16[128,1152]{1,0:T(8,128)(2,1)S(1)} collective-permute-done((bf16[128,1152]{1,0:T(8,128)(2,1)}, bf16[128,1152]{1,0:T(8,128)(2,1)S(1)}, u32[]{:S(2)}, u32[]{:S(2)}) %collective-permute-start.4) | collective-permute-done | bytes 294944 | tf_op jit(solution)/shard_map/ppermute | solution.py:13
  33.6 0.0 copy-done.1
  33.6 0.0 copy-start.2
  33.6 0.8 %add_convert_fusion.1 = bf16[128,1152]{1,0:T(8,128)(2,1)} fusion(f32[128,1152]{1,0:T(8,128)S(1)} %copy-done.1, bf16[128,1152]{1,0:T(8,128)(2,1)S(1)} %collective-permute-done.4), kind=kLoop, calls=%fused_computation.1 | loop fusion | flops 442368 | bytes 1179648 | tf_op jit(solution)/shard_map/convert_element_type | solution.py:93
  34.4 5.2 %collective-permute-done.7 = bf16[128,1152]{1,0:T(8,128)(2,1)S(1)} collective-permute-done((bf16[128,1152]{1,0:T(8,128)(2,1)}, bf16[128,1152]{1,0:T(8,128)(2,1)S(1)}, u32[]{:S(2)}, u32[]{:S(2)}) %collective-permute-start.7) | collective-permute-done | bytes 294944 | tf_op jit(solution)/shard_map/ppermute | solution.py:13
  39.6 0.0 copy-done.2
  39.6 0.8 %add_convert_fusion = bf16[128,1152]{1,0:T(8,128)(2,1)} fusion(f32[128,1152]{1,0:T(8,128)S(1)} %copy-done.2, bf16[128,1152]{1,0:T(8,128)(2,1)S(1)} %collective-permute-done.7), kind=kLoop, calls=%fused_computation | loop fusion | flops 442368 | bytes 1179648 | tf_op jit(solution)/shard_map/convert_element_type | solution.py:93
Async XLA Ops:
  0.6 13.3 %collective-permute-start.1 = (bf16[128,1152]{1,0:T(8,128)(2,1)}, bf16[128,1152]{1,0:T(8,128)(2,1)S(1)}, u32[]{:S(2)}, u32[]{:S(2)}) collective-permute-start(bf16[128,1152]{1,0:T(8,128)(2,1)} %refs_0_.5), channel_id=1, source_target_pairs={{0,4},{4,8},{8,12},{12,16},{16,20},{20,24},{24,28},{28,0},{1,5},{5... | collective-permute-start | bytes 884744 | tf_op jit(solution)/shard_map/ppermute | solution.py:13
  3.6 12.1 %collective-permute-start = (bf16[128,1152]{1,0:T(8,128)(2,1)}, bf16[128,1152]{1,0:T(8,128)(2,1)S(1)}, u32[]{:S(2)}, u32[]{:S(2)}) collective-permute-start(bf16[128,1152]{1,0:T(8,128)(2,1)} %refs_2_.3), channel_id=1, source_target_pairs={{0,2},{1,3},{2,0},{3,1},{4,6},{5,7},{6,4},{7,5},{8,10},{9,11},{10,... | collective-permute-start | bytes 884744 | tf_op jit(solution)/shard_map/ppermute | solution.py:13
  5.1 10.7 %collective-permute-start.3 = (bf16[128,1152]{1,0:T(8,128)(2,1)}, bf16[128,1152]{1,0:T(8,128)(2,1)S(1)}, u32[]{:S(2)}, u32[]{:S(2)}) collective-permute-start(bf16[128,1152]{1,0:T(8,128)(2,1)} %refs_0_.5), channel_id=1, source_target_pairs={{0,1},{1,0},{2,3},{3,2},{4,5},{5,4},{6,7},{7,6},{8,9},{9,8},{10,11... | collective-permute-start | bytes 884744 | tf_op jit(solution)/shard_map/ppermute | solution.py:13
  13.9 6.5 %copy-start.3 = (bf16[128,1152]{1,0:T(8,128)(2,1)}, bf16[128,1152]{1,0:T(8,128)(2,1)S(1)}, u32[]{:S(2)}) copy-start(bf16[128,1152]{1,0:T(8,128)(2,1)S(1)} %collective-permute-done.1.refs_2_.refs_1_) | copy-start | bytes 884740
  13.9 6.4 %collective-permute-start.2 = (bf16[128,1152]{1,0:T(8,128)(2,1)S(1)}, bf16[128,1152]{1,0:T(8,128)(2,1)S(1)}, u32[]{:S(2)}, u32[]{:S(2)}) collective-permute-start(bf16[128,1152]{1,0:T(8,128)(2,1)S(1)} %collective-permute-done.1.refs_2_.refs_1_), channel_id=1, source_target_pairs={{0,1},{1,0},{2,3},{3,2},{4,5},{5,4},{6,7},{7,6},{8,9},{9,8},{10,11... | collective-permute-start | bytes 884744 | tf_op jit(solution)/shard_map/ppermute | solution.py:13
  13.9 12.1 %collective-permute-start.5 = (bf16[128,1152]{1,0:T(8,128)(2,1)}, bf16[128,1152]{1,0:T(8,128)(2,1)S(1)}, u32[]{:S(2)}, u32[]{:S(2)}) collective-permute-start(bf16[128,1152]{1,0:T(8,128)(2,1)} %refs_2_.3), channel_id=1, source_target_pairs={{0,1},{1,0},{2,3},{3,2},{4,5},{5,4},{6,7},{7,6},{8,9},{9,8},{10,11... | collective-permute-start | bytes 884744 | tf_op jit(solution)/shard_map/ppermute | solution.py:13
  15.7 0.7 %copy-start = (bf16[128,1152]{1,0:T(8,128)(2,1)}, bf16[128,1152]{1,0:T(8,128)(2,1)S(1)}, u32[]{:S(2)}) copy-start(bf16[128,1152]{1,0:T(8,128)(2,1)S(1)} %collective-permute-done.refs_1_.refs_4_) | copy-start | bytes 884740
  15.7 10.3 %collective-permute-start.6 = (bf16[128,1152]{1,0:T(8,128)(2,1)S(1)}, bf16[128,1152]{1,0:T(8,128)(2,1)S(1)}, u32[]{:S(2)}, u32[]{:S(2)}) collective-permute-start(bf16[128,1152]{1,0:T(8,128)(2,1)S(1)} %collective-permute-done.refs_1_.refs_4_), channel_id=1, source_target_pairs={{0,1},{1,0},{2,3},{3,2},{4,5},{5,4},{6,7},{7,6},{8,9},{9,8},{10,11... | collective-permute-start | bytes 884744 | tf_op jit(solution)/shard_map/ppermute | solution.py:13
  16.4 0.7 %copy-start.5 = (bf16[128,1152]{1,0:T(8,128)(2,1)}, bf16[128,1152]{1,0:T(8,128)(2,1)S(1)}, u32[]{:S(2)}) copy-start(bf16[128,1152]{1,0:T(8,128)(2,1)S(1)} %collective-permute-done.3.refs_3_) | copy-start | bytes 884740
  20.4 0.7 %copy-start.4 = (bf16[128,1152]{1,0:T(8,128)(2,1)}, bf16[128,1152]{1,0:T(8,128)(2,1)S(1)}, u32[]{:S(2)}) copy-start(bf16[128,1152]{1,0:T(8,128)(2,1)S(1)} %collective-permute-done.2.refs_3_) | copy-start | bytes 884740
  24.5 9.1 %copy-start.1 = (f32[128,1152]{1,0:T(8,128)S(1)}, f32[128,1152]{1,0:T(8,128)}, u32[]{:S(2)}) copy-start(f32[128,1152]{1,0:T(8,128)} %get-tuple-element.10) | copy-start | bytes 1769476
  24.5 9.1 %collective-permute-start.4 = (bf16[128,1152]{1,0:T(8,128)(2,1)}, bf16[128,1152]{1,0:T(8,128)(2,1)S(1)}, u32[]{:S(2)}, u32[]{:S(2)}) collective-permute-start(bf16[128,1152]{1,0:T(8,128)(2,1)} %get-tuple-element.11), channel_id=1, source_target_pairs={{0,2},{1,3},{2,0},{3,1},{4,6},{5,7},{6,4},{7,5},{8,10},{9,11},{10,... | collective-permute-start | bytes 884744 | tf_op jit(solution)/shard_map/ppermute | solution.py:13
  26.0 0.7 %copy-start.6 = (bf16[128,1152]{1,0:T(8,128)(2,1)}, bf16[128,1152]{1,0:T(8,128)(2,1)S(1)}, u32[]{:S(2)}) copy-start(bf16[128,1152]{1,0:T(8,128)(2,1)S(1)} %collective-permute-done.5.refs_3_) | copy-start | bytes 884740
  26.7 0.7 %copy-start.7 = (bf16[128,1152]{1,0:T(8,128)(2,1)}, bf16[128,1152]{1,0:T(8,128)(2,1)S(1)}, u32[]{:S(2)}) copy-start(bf16[128,1152]{1,0:T(8,128)(2,1)S(1)} %collective-permute-done.6.refs_5_) | copy-start | bytes 884740
  30.8 8.9 %collective-permute-start.7 = (bf16[128,1152]{1,0:T(8,128)(2,1)}, bf16[128,1152]{1,0:T(8,128)(2,1)S(1)}, u32[]{:S(2)}, u32[]{:S(2)}) collective-permute-start(bf16[128,1152]{1,0:T(8,128)(2,1)} %get-tuple-element.13), channel_id=1, source_target_pairs={{0,28},{4,0},{8,4},{12,8},{16,12},{20,16},{24,20},{28,24},{1,29},{... | collective-permute-start | bytes 884744 | tf_op jit(solution)/shard_map/ppermute | solution.py:13
  33.6 6.0 %copy-start.2 = (f32[128,1152]{1,0:T(8,128)S(1)}, f32[128,1152]{1,0:T(8,128)}, u32[]{:S(2)}) copy-start(f32[128,1152]{1,0:T(8,128)} %get-tuple-element.12) | copy-start | bytes 1769476

commit v3 on v1

v3 whole, which is shorter than its diff:
```python
import jax
import jax.numpy as jnp
from jax import lax
from jax.experimental import pallas as pl
from jax.experimental.pallas import tpu as pltpu
from jax.sharding import PartitionSpec as P

CORES = 2
VMEM = pl.BlockSpec(memory_space=pltpu.VMEM)
SMEM = pl.BlockSpec(memory_space=pltpu.SMEM)


def moved(array, axis, target):
    peers = lax.axis_size(axis)
    return lax.ppermute(array, axis, [(i, target(i) % peers) for i in range(peers)])


def swapped(array):
    return moved(array, "in", lambda i: i ^ 1)


def held(arrays, scale, shift):
    def kernel(scale_ref, shift_ref, *refs):
        sources, targets, sems = refs[: len(arrays)], refs[len(arrays) : -1], refs[-1]
        copies = [
            pltpu.make_async_copy(source, target, sems.at[i])
            for i, (source, target) in enumerate(zip(sources, targets))
        ]
        for copy in copies:
            copy.start()
        for copy in copies:
            copy.wait()

    return pl.pallas_call(
        kernel,
        out_shape=[jax.ShapeDtypeStruct(a.shape, a.dtype) for a in arrays],
        in_specs=[SMEM] * 2 + [pl.BlockSpec(memory_space=pl.ANY)] * len(arrays),
        out_specs=[VMEM] * len(arrays),
        scratch_shapes=[pltpu.SemaphoreType.DMA((len(arrays),))],
        compiler_params=pltpu.CompilerParams(vmem_limit_bytes=4 << 20),
    )(scale, shift, *arrays)


def pulled(jobs, out_types, scale, shift):
    height, width = jobs[0][0][0].shape
    arrays = [a for rows, others, starts, _ in jobs for a in (*rows, *others, *starts)]

    def kernel(scale_ref, shift_ref, *refs):
        in_refs, out_refs = iter(refs[: len(arrays)]), iter(refs[len(arrays) :])
        scale_now, shift_now = scale_ref[0], shift_ref[0]
        for rows, others, starts, paired in jobs:
            row_refs = [next(in_refs) for _ in rows]
            other_refs = [next(in_refs) for _ in others]
            start_refs = [next(in_refs) for _ in starts]
            left = jnp.concatenate([ref[...] for ref in row_refs], axis=0)
            right = jnp.concatenate([ref[...] for ref in other_refs], axis=0)
            logits = lax.dot_general(
                left, right, (((1,), (1,)), ((), ())), preferred_element_type=jnp.float32
            )
            slope = jax.nn.sigmoid(scale_now * logits + shift_now)
            if paired:
                row_ids = lax.broadcasted_iota(jnp.int32, slope.shape, 0)
                col_ids = lax.broadcasted_iota(jnp.int32, slope.shape, 1)
                matched = (col_ids == row_ids) & (row_ids < height)
                slope = slope - matched.astype(jnp.float32)
            weights = (scale_now * slope).astype(jnp.bfloat16)
            terms = jnp.dot(weights, right, preferred_element_type=jnp.float32)
            for i in range(len(rows)):
                term = terms[i * height : (i + 1) * height]
                if starts:
                    term = term + start_refs[i][...]
                out_ref = next(out_refs)
                out_ref[...] = term.astype(out_ref.dtype)

    pairs = sum(height * height * len(rows) * len(others) for rows, others, _, _ in jobs)
    size = sum(a.size * a.dtype.itemsize for a in arrays)
    size += sum(height * width * jnp.dtype(t).itemsize for t in out_types)
    return pl.pallas_call(
        kernel,
        out_shape=[jax.ShapeDtypeStruct((height, width), t) for t in out_types],
        in_specs=[SMEM] * 2 + [VMEM] * len(arrays),
        out_specs=[VMEM] * len(out_types),
        cost_estimate=pl.CostEstimate(
            flops=4 * pairs * width, bytes_accessed=size, transcendentals=pairs
        ),
        compiler_params=pltpu.CompilerParams(vmem_limit_bytes=2 * size + 16 * pairs + (4 << 20)),
    )(scale, shift, *arrays)


def summed(sums):
    shape = sums[0][0].shape
    arrays = [a for blocks in sums for a in blocks]

    def kernel(*refs):
        in_refs, out_refs = iter(refs[: len(arrays)]), refs[len(arrays) :]
        for blocks, out_ref in zip(sums, out_refs):
            total = next(in_refs)[...]
            for _ in blocks[1:]:
                total = total + next(in_refs)[...].astype(jnp.float32)
            out_ref[...] = total.astype(out_ref.dtype)

    size = sum(a.size * a.dtype.itemsize for a in arrays)
    return pl.pallas_call(
        kernel,
        out_shape=[jax.ShapeDtypeStruct(shape, jnp.bfloat16) for _ in sums],
        in_specs=[VMEM] * len(arrays),
        out_specs=[VMEM] * len(sums),
        cost_estimate=pl.CostEstimate(flops=size, bytes_accessed=size, transcendentals=0),
        compiler_params=pltpu.CompilerParams(vmem_limit_bytes=2 * size + (4 << 20)),
    )(*arrays)


def finished(first, second, second_extra):
    shape, dtype = first.shape, first.dtype

    def kernel(first_ref, second_ref, extra_ref, image_ref, text_ref, rounded_ref, sems):
        is_image_core = lax.rem(lax.axis_index("in"), CORES) == 0

        def to_images(source):
            return pltpu.make_async_copy(source, image_ref, sems.at[0])

        def to_texts(source):
            return pltpu.make_async_copy(source, text_ref, sems.at[1])

        @pl.when(is_image_core)
        def _():
            to_images(first_ref).start()

        @pl.when(jnp.logical_not(is_image_core))
        def _():
            to_texts(first_ref).start()

        total = second_ref[...] + extra_ref[...].astype(jnp.float32)
        rounded_ref[...] = total.astype(dtype)

        @pl.when(is_image_core)
        def _():
            to_texts(rounded_ref).start()

        @pl.when(jnp.logical_not(is_image_core))
        def _():
            to_images(rounded_ref).start()

        to_images(first_ref).wait()
        to_texts(first_ref).wait()

    size = 3 * first.size * 4
    return pl.pallas_call(
        kernel,
        out_shape=[jax.ShapeDtypeStruct(shape, dtype)] * 2,
        in_specs=[VMEM] * 3,
        out_specs=[pl.BlockSpec(memory_space=pl.ANY)] * 2,
        scratch_shapes=[pltpu.VMEM(shape, dtype), pltpu.SemaphoreType.DMA((2,))],
        cost_estimate=pl.CostEstimate(flops=size, bytes_accessed=size, transcendentals=0),
        compiler_params=pltpu.CompilerParams(vmem_limit_bytes=2 * size + (4 << 20)),
    )(first, second, second_extra)


def by_roles(images, texts, scale, shift):
    groups, members = lax.axis_size("grp"), lax.axis_size("in")
    f32, bf16 = jnp.float32, jnp.bfloat16

    def sent(array, target):
        pairs = []
        for group in range(groups):
            for chip in range(members // CORES):
                for core in range(CORES):
                    to_group, to_chip, to_core = target(group, chip, core)
                    pairs.append(
                        (
                            group * members + chip * CORES + core,
                            to_group % groups * members + (to_chip % 2) * CORES + to_core,
                        )
                    )
        return lax.ppermute(array, ("grp", "in"), pairs)

    is_image_core = lax.rem(lax.axis_index("in"), CORES) == 0
    first = jnp.where(is_image_core, images, texts)
    second = jnp.where(is_image_core, texts, images)
    got_a = sent(first, lambda g, x, c: (g, x + 1, 1) if c == 0 else (g + 1, x, 0))
    got_b = sent(second, lambda g, x, c: (g + 1, x, 0) if c == 0 else (g, x + 1, 1))
    other_first, other_second = swapped(first), swapped(second)
    starts = pulled(
        [
            ([first], [second, other_first], [], True),
            ([second], [first, other_second], [], True),
        ],
        [f32, f32],
        scale,
        shift,
    )
    swap_a = swapped(got_a)
    got_b, *starts = lax.optimization_barrier((got_b, *starts))
    swap_b = swapped(got_b)
    [back_a] = pulled(
        [([swap_a], [second, other_first, got_a, got_b], [], False)], [bf16], scale, shift
    )
    [back_b] = pulled(
        [([swap_b], [second, other_first, got_a, got_b], [], False)], [bf16], scale, shift
    )
    home_a = sent(back_a, lambda g, x, c: (g, x + 1, 0) if c == 0 else (g - 1, x, 1))
    home_b = sent(back_b, lambda g, x, c: (g, x + 1, 1) if c == 0 else (g - 1, x, 0))
    first_total, second_total = pulled(
        [
            ([first], [got_a, got_b], starts[:1], False),
            ([second], [swap_a, swap_b], starts[1:], False),
        ],
        [f32, f32],
        scale,
        shift,
    )
    [first_total] = summed([[first_total, home_a]])
    return tuple(finished(first_total, second_total, home_b))


def by_arrays(images, texts, scale, shift):
    chips = lax.axis_size("in") // CORES
    f32, bf16 = jnp.float32, jnp.bfloat16
    back_texts = moved(texts, "grp", lambda i: i + 1)
    near_images = [moved(images, "in", lambda i, k=k: i - CORES * k) for k in range(1, chips)]
    images, texts = held([images, texts], scale, shift)
    core_images, core_texts = swapped(images), swapped(texts)
    far_images = [swapped(block) for block in near_images]
    far_texts = swapped(back_texts)
    own_texts = [texts, core_texts]
    group_images = [images, core_images] + near_images + far_images

    starts = pulled(
        [(near_images, own_texts, [], False)], [f32] * (chips - 1), scale, shift
    )
    [sent_texts] = pulled([([back_texts], group_images, [], False)], [bf16], scale, shift)
    sent_images = pulled(
        [(near_images, [back_texts, far_texts], starts, False)],
        [bf16] * (chips - 1),
        scale,
        shift,
    )
    sent_texts, *sent_images = lax.optimization_barrier((sent_texts, *sent_images))
    sent_images = [
        moved(block, "in", lambda i, k=k: i + CORES * k) for k, block in enumerate(sent_images, 1)
    ]
    sent_texts = moved(sent_texts, "grp", lambda i: i - 1)
    image_total, text_total = pulled(
        [
            ([images], own_texts + [back_texts, far_texts], [], True),
            ([texts], group_images, [], True),
        ],
        [f32, f32],
        scale,
        shift,
    )
    return tuple(summed([[image_total] + sent_images, [text_total, sent_texts]]))


def shards(images, texts, scale, shift):
    if lax.axis_size("in") == 2 * CORES:
        return by_roles(images, texts, scale, shift)
    return by_arrays(images, texts, scale, shift)


def solution(mesh):
    rows = P(("grp", "in"), None)
    return jax.shard_map(
        shards,
        mesh=mesh,
        in_specs=(rows, rows, P(), P()),
        out_specs=(rows, rows),
        check_vma=False,
    )
```

time: 43.2 us -> 26.7 us (0.62)
  matrix products: 22.3 us -> 0 us
  Pallas kernels: 0 us -> 5.16 us
  waiting for transfers between devices: 11.3 us -> 8.66 us
  starting transfers between devices: 7.21 us -> 9.61 us
  other arithmetic: 0 us -> 1.11 us
    dot_general x16 -> x0, matrix products: 22.3 us -> none  [pulled(): term = jnp.dot(weights, other, preferred_element_type=jnp.float32)]
    ppermute x8 -> x4, waiting for transfers between devices: 11.3 us -> 0.01 us  [moved(): lax.ppermute(array, axis, [(i, target(i) % peers) for i in range(peers)])]
    ppermute x0 -> x4, starting transfers between devices: none -> 8.9 us  [sent(): return lax.ppermute(array, ('grp', 'in'), pairs)]
    ppermute x0 -> x4, waiting for transfers between devices: none -> 8.65 us  [sent(): return lax.ppermute(array, ('grp', 'in'), pairs)]
    ppermute x8 -> x4, starting transfers between devices: 7.21 us -> 0.71 us  [moved(): lax.ppermute(array, axis, [(i, target(i) % peers) for i in range(peers)])]
    pallas_call x0 -> x6, Pallas kernels: none -> 5.16 us  [the longest x4 4.27 us: pulled(): pl.pallas_call(kernel, out_shape=[jax.ShapeDtypeStruct((height, width), t...]
    select_n x0 -> x1, other arithmetic: none -> 1.11 us  [by_roles(): second = jnp.where(is_image_core, texts, images)]
  transfers between devices with their start and end apart: 8 -> 8, of which waited for: 4 -> 3; matrix products, arithmetic and copies ran while one was open for 49% -> 0% of each run, Pallas kernels for 0% -> 16%
where the time goes in v3:
time: 26.7 us; the launch traced here: 26.5 us
  starting transfers between devices  9.61 us (36%)
  waiting for transfers between devices  8.66 us (32%)
  Pallas kernels  5.16 us (19%)
  between operations  1.99 us (7%)
  other arithmetic  1.11 us (4%)
    ppermute x4, starting transfers between devices, sent(): return lax.ppermute(array, ('grp', 'in'), pairs)  8.9 us
    ppermute x4, waiting for transfers between devices, sent(): return lax.ppermute(array, ('grp', 'in'), pairs)  8.65 us
    pallas_call x4, Pallas kernels, pulled(): pl.pallas_call(kernel, out_shape=[jax.ShapeDtypeStruct((height, width), t...  4.27 us
    select_n x1, other arithmetic, by_roles(): second = jnp.where(is_image_core, texts, images)  1.11 us
    pallas_call x1, Pallas kernels, finished(): pl.pallas_call(kernel, out_shape=[jax.ShapeDtypeStruct(shape, dtype)] * 2...  0.84 us
    ppermute x4, starting transfers between devices, moved(): lax.ppermute(array, axis, [(i, target(i) % peers) for i in range(peers)])  0.71 us
  transfers between devices with their start and end apart: 8, of which 3 were waited for; matrix products, arithmetic and copies ran while one was open for 0% of the time, Pallas kernels for 16%

profile of v3, /device:TPU:0, one launch (start us, length us, event | category | flops | bytes accessed | tf_op | source)
XLA Modules:
  0.0 26.5 jit_solution(13474827095346097631)
XLA Ops:
  0.6 1.1 %broadcast_select_fusion = (bf16[128,1152]{1,0:T(8,128)(2,1)S(1)}, bf16[128,1152]{1,0:T(8,128)(2,1)S(1)}) fusion(bf16[128,1152]{1,0:T(8,128)(2,1)} %param.5, bf16[128,1152]{1,0:T(8,128)(2,1)} %param.4, pred[]{:T(512)S(6)} %eq.3), kind=kLoop, calls=%fused_computation | loop fusion | flops 294912 | bytes 1179649 | tf_op jit(solution)/shard_map/jit(_where)/select_n | solution.py:179
  1.7 2.4 %collective-permute-start = (bf16[128,1152]{1,0:T(8,128)(2,1)S(1)}, bf16[128,1152]{1,0:T(8,128)(2,1)S(1)}, u32[]{:S(2)}, u32[]{:S(2)}) collective-permute-start(bf16[128,1152]{1,0:T(8,128)(2,1)S(1)} %get-tuple-element.17.refs_0_.refs_4_), channel_id=1, source_target_pairs={{0,3},{1,4},{2,1},{3,6},{4,7},{5,8},{6,5},{7,10},{8,11},{9,12},{10... | collective-permute-start | bytes 884744 | tf_op jit(solution)/shard_map/ppermute | solution.py:175
  4.2 0.7 %collective-permute-start.2 = (bf16[128,1152]{1,0:T(8,128)(2,1)S(1)}, bf16[128,1152]{1,0:T(8,128)(2,1)S(1)}, u32[]{:S(2)}, u32[]{:S(2)}) collective-permute-start(bf16[128,1152]{1,0:T(8,128)(2,1)S(1)} %get-tuple-element.17.refs_0_.refs_4_), channel_id=1, source_target_pairs={{0,1},{1,0},{2,3},{3,2},{4,5},{5,4},{6,7},{7,6},{8,9},{9,8},{10,11... | collective-permute-start | bytes 884744 | tf_op jit(solution)/shard_map/ppermute | solution.py:15
  4.9 0.0 collective-permute-start.3
  4.9 1.5 %collective-permute-start.1 = (bf16[128,1152]{1,0:T(8,128)(2,1)S(1)}, bf16[128,1152]{1,0:T(8,128)(2,1)S(1)}, u32[]{:S(2)}, u32[]{:S(2)}) collective-permute-start(bf16[128,1152]{1,0:T(8,128)(2,1)S(1)} %get-tuple-element.16.refs_1_.refs_3_.refs_4_), channel_id=1, source_target_pairs={{0,4},{1,3},{2,6},{3,1},{4,8},{5,7},{6,10},{7,5},{8,12},{9,11},{10... | collective-permute-start | bytes 884744 | tf_op jit(solution)/shard_map/ppermute | solution.py:175
  7.7 4.4 %collective-permute-done.refs_1_.refs_3_ = bf16[128,1152]{1,0:T(8,128)(2,1)S(1)} collective-permute-done((bf16[128,1152]{1,0:T(8,128)(2,1)S(1)}, bf16[128,1152]{1,0:T(8,128)(2,1)S(1)}, u32[]{:S(2)}, u32[]{:S(2)}) %collective-permute-start) | collective-permute-done | bytes 294944 | tf_op jit(solution)/shard_map/ppermute | solution.py:175
  12.1 0.0 collective-permute-start.4
  12.1 0.0 collective-permute-done.2.refs_2_
  12.1 0.0 collective-permute-done.3.refs_5_
  12.1 1.3 %shard_map.59 = (f32[128,1152]{1,0:T(8,128)S(1)}, f32[128,1152]{1,0:T(8,128)S(1)}) custom-call(f32[1]{0:T(128)S(6)} %copy.6.scale_ref, f32[1]{0:T(128)S(6)} %copy.7.shift_ref, bf16[128,1152]{1,0:T(8,128)(2,1)S(1)} %get-tuple-element.17.refs_0_.refs_4_, bf16[128,1152]{1,0:T(8,128)(2,1)S(1)} %get-tuple-element.16.refs_1_.refs_3_.refs_4_, ...), custom_call_target="tpu_custom_call" | custom-call | flops 301989888 | bytes 2949120 | tf_op jit(solution)/shard_map/pallas_call | solution.py:78
  13.4 1.4 %collective-permute-done.1.refs_2_.refs_4_ = bf16[128,1152]{1,0:T(8,128)(2,1)S(1)} collective-permute-done((bf16[128,1152]{1,0:T(8,128)(2,1)S(1)}, bf16[128,1152]{1,0:T(8,128)(2,1)S(1)}, u32[]{:S(2)}, u32[]{:S(2)}) %collective-permute-start.1) | collective-permute-done | bytes 294944 | tf_op jit(solution)/shard_map/ppermute | solution.py:175
  14.8 0.0 collective-permute-start.5
  14.8 0.0 collective-permute-done.4.refs_5_.refs_0_
  14.8 0.8 %shard_map.61 = bf16[128,1152]{1,0:T(8,128)(2,1)S(1)} custom-call(f32[1]{0:T(128)S(6)} %copy.6.scale_ref, f32[1]{0:T(128)S(6)} %copy.7.shift_ref, bf16[128,1152]{1,0:T(8,128)(2,1)S(1)} %collective-permute-done.4.refs_5_.refs_0_, bf16[128,1152]{1,0:T(8,128)(2,1)S(1)} %get-tuple-element.16.refs_1_.refs_3_.refs_4_, ...), custom_call_target="tpu_custom_call" | custom-call | flops 301989888 | bytes 1769472 | tf_op jit(solution)/shard_map/pallas_call | solution.py:78
  15.7 2.0 %collective-permute-start.6 = (bf16[128,1152]{1,0:T(8,128)(2,1)S(1)}, bf16[128,1152]{1,0:T(8,128)(2,1)S(1)}, u32[]{:S(2)}, u32[]{:S(2)}) collective-permute-start(bf16[128,1152]{1,0:T(8,128)(2,1)S(1)} %shard_map.61), channel_id=1, source_target_pairs={{0,2},{1,29},{2,0},{3,31},{4,6},{5,1},{6,4},{7,3},{8,10},{9,5},{10... | collective-permute-start | bytes 884744 | tf_op jit(solution)/shard_map/ppermute | solution.py:175
  17.6 0.0 collective-permute-done.5.refs_6_.refs_0_
  17.6 0.8 %shard_map.63 = bf16[128,1152]{1,0:T(8,128)(2,1)S(1)} custom-call(f32[1]{0:T(128)S(6)} %copy.6.scale_ref, f32[1]{0:T(128)S(6)} %copy.7.shift_ref, bf16[128,1152]{1,0:T(8,128)(2,1)S(1)} %collective-permute-done.5.refs_6_.refs_0_, bf16[128,1152]{1,0:T(8,128)(2,1)S(1)} %get-tuple-element.16.refs_1_.refs_3_.refs_4_, ...), custom_call_target="tpu_custom_call" | custom-call | flops 301989888 | bytes 1769472 | tf_op jit(solution)/shard_map/pallas_call | solution.py:78
  18.5 3.0 %collective-permute-start.7 = (bf16[128,1152]{1,0:T(8,128)(2,1)S(1)}, bf16[128,1152]{1,0:T(8,128)(2,1)S(1)}, u32[]{:S(2)}, u32[]{:S(2)}) collective-permute-start(bf16[128,1152]{1,0:T(8,128)(2,1)S(1)} %shard_map.63), channel_id=1, source_target_pairs={{0,3},{1,28},{2,1},{3,30},{4,7},{5,0},{6,5},{7,2},{8,11},{9,4},{10... | collective-permute-start | bytes 884744 | tf_op jit(solution)/shard_map/ppermute | solution.py:175
  21.4 1.3 %shard_map.60 = (f32[128,1152]{1,0:T(8,128)S(1)}, f32[128,1152]{1,0:T(8,128)S(1)}) custom-call(f32[1]{0:T(128)S(6)} %copy.6.scale_ref, f32[1]{0:T(128)S(6)} %copy.7.shift_ref, bf16[128,1152]{1,0:T(8,128)(2,1)S(1)} %get-tuple-element.17.refs_0_.refs_4_, bf16[128,1152]{1,0:T(8,128)(2,1)S(1)} %collective-permute-done.refs_1_.refs_3_, ...), custom_call_target="tpu_custom_call" | custom-call | flops 301989888 | bytes 4128768 | tf_op jit(solution)/shard_map/pallas_call | solution.py:78
  22.8 0.0 collective-permute-done.6.refs_1_
  22.8 0.1 shard_map.62.first_ref
  22.8 2.9 %collective-permute-done.7.extra_ref = bf16[128,1152]{1,0:T(8,128)(2,1)S(1)} collective-permute-done((bf16[128,1152]{1,0:T(8,128)(2,1)S(1)}, bf16[128,1152]{1,0:T(8,128)(2,1)S(1)}, u32[]{:S(2)}, u32[]{:S(2)}) %collective-permute-start.7) | collective-permute-done | bytes 294944 | tf_op jit(solution)/shard_map/ppermute | solution.py:175
  25.7 0.8 %shard_map.64 = (bf16[128,1152]{1,0:T(8,128)(2,1)}, bf16[128,1152]{1,0:T(8,128)(2,1)}) custom-call(bf16[128,1152]{1,0:T(8,128)(2,1)S(1)} %shard_map.62.first_ref, f32[128,1152]{1,0:T(8,128)S(1)} %get-tuple-element.15.second_ref, bf16[128,1152]{1,0:T(8,128)(2,1)S(1)} %collective-permute-done.7.extra_ref), custom_call_target="tpu_custom_call" | custom-call | flops 1769472 | bytes 1769472 | tf_op jit(solution)/shard_map/pallas_call | solution.py:148
Async XLA Ops:
  1.7 10.3 %collective-permute-start = (bf16[128,1152]{1,0:T(8,128)(2,1)S(1)}, bf16[128,1152]{1,0:T(8,128)(2,1)S(1)}, u32[]{:S(2)}, u32[]{:S(2)}) collective-permute-start(bf16[128,1152]{1,0:T(8,128)(2,1)S(1)} %get-tuple-element.17.refs_0_.refs_4_), channel_id=1, source_target_pairs={{0,3},{1,4},{2,1},{3,6},{4,7},{5,8},{6,5},{7,10},{8,11},{9,12},{10... | collective-permute-start | bytes 884744 | tf_op jit(solution)/shard_map/ppermute | solution.py:175
  4.2 7.9 %collective-permute-start.2 = (bf16[128,1152]{1,0:T(8,128)(2,1)S(1)}, bf16[128,1152]{1,0:T(8,128)(2,1)S(1)}, u32[]{:S(2)}, u32[]{:S(2)}) collective-permute-start(bf16[128,1152]{1,0:T(8,128)(2,1)S(1)} %get-tuple-element.17.refs_0_.refs_4_), channel_id=1, source_target_pairs={{0,1},{1,0},{2,3},{3,2},{4,5},{5,4},{6,7},{7,6},{8,9},{9,8},{10,11... | collective-permute-start | bytes 884744 | tf_op jit(solution)/shard_map/ppermute | solution.py:15
  4.9 7.2 %collective-permute-start.3 = (bf16[128,1152]{1,0:T(8,128)(2,1)S(1)}, bf16[128,1152]{1,0:T(8,128)(2,1)S(1)}, u32[]{:S(2)}, u32[]{:S(2)}) collective-permute-start(bf16[128,1152]{1,0:T(8,128)(2,1)S(1)} %get-tuple-element.16.refs_1_.refs_3_.refs_4_), channel_id=1, source_target_pairs={{0,1},{1,0},{2,3},{3,2},{4,5},{5,4},{6,7},{7,6},{8,9},{9,8},{10,11... | collective-permute-start | bytes 884744 | tf_op jit(solution)/shard_map/ppermute | solution.py:15
  4.9 9.9 %collective-permute-start.1 = (bf16[128,1152]{1,0:T(8,128)(2,1)S(1)}, bf16[128,1152]{1,0:T(8,128)(2,1)S(1)}, u32[]{:S(2)}, u32[]{:S(2)}) collective-permute-start(bf16[128,1152]{1,0:T(8,128)(2,1)S(1)} %get-tuple-element.16.refs_1_.refs_3_.refs_4_), channel_id=1, source_target_pairs={{0,4},{1,3},{2,6},{3,1},{4,8},{5,7},{6,10},{7,5},{8,12},{9,11},{10... | collective-permute-start | bytes 884744 | tf_op jit(solution)/shard_map/ppermute | solution.py:175
  12.1 2.7 %collective-permute-start.4 = (bf16[128,1152]{1,0:T(8,128)(2,1)S(1)}, bf16[128,1152]{1,0:T(8,128)(2,1)S(1)}, u32[]{:S(2)}, u32[]{:S(2)}) collective-permute-start(bf16[128,1152]{1,0:T(8,128)(2,1)S(1)} %collective-permute-done.refs_1_.refs_3_), channel_id=1, source_target_pairs={{0,1},{1,0},{2,3},{3,2},{4,5},{5,4},{6,7},{7,6},{8,9},{9,8},{10,11... | collective-permute-start | bytes 884744 | tf_op jit(solution)/shard_map/ppermute | solution.py:15
  14.8 2.8 %collective-permute-start.5 = (bf16[128,1152]{1,0:T(8,128)(2,1)S(1)}, bf16[128,1152]{1,0:T(8,128)(2,1)S(1)}, u32[]{:S(2)}, u32[]{:S(2)}) collective-permute-start(bf16[128,1152]{1,0:T(8,128)(2,1)S(1)} %collective-permute-done.1.refs_2_.refs_4_), channel_id=1, source_target_pairs={{0,1},{1,0},{2,3},{3,2},{4,5},{5,4},{6,7},{7,6},{8,9},{9,8},{10,11... | collective-permute-start | bytes 884744 | tf_op jit(solution)/shard_map/ppermute | solution.py:15
  15.7 7.1 %collective-permute-start.6 = (bf16[128,1152]{1,0:T(8,128)(2,1)S(1)}, bf16[128,1152]{1,0:T(8,128)(2,1)S(1)}, u32[]{:S(2)}, u32[]{:S(2)}) collective-permute-start(bf16[128,1152]{1,0:T(8,128)(2,1)S(1)} %shard_map.61), channel_id=1, source_target_pairs={{0,2},{1,29},{2,0},{3,31},{4,6},{5,1},{6,4},{7,3},{8,10},{9,5},{10... | collective-permute-start | bytes 884744 | tf_op jit(solution)/shard_map/ppermute | solution.py:175
  18.5 7.2 %collective-permute-start.7 = (bf16[128,1152]{1,0:T(8,128)(2,1)S(1)}, bf16[128,1152]{1,0:T(8,128)(2,1)S(1)}, u32[]{:S(2)}, u32[]{:S(2)}) collective-permute-start(bf16[128,1152]{1,0:T(8,128)(2,1)S(1)} %shard_map.63), channel_id=1, source_target_pairs={{0,3},{1,28},{2,1},{3,30},{4,7},{5,0},{6,5},{7,2},{8,11},{9,4},{10... | collective-permute-start | bytes 884744 | tf_op jit(solution)/shard_map/ppermute | solution.py:175

commit v4 on v3

--- a/solution.py
+++ b/solution.py
@@ -110,50 +110,68 @@
     )(*arrays)
 
 
-def finished(first, second, second_extra):
-    shape, dtype = first.shape, first.dtype
-
-    def kernel(first_ref, second_ref, extra_ref, image_ref, text_ref, rounded_ref, sems):
-        is_image_core = lax.rem(lax.axis_index("in"), CORES) == 0
-
-        def to_images(source):
-            return pltpu.make_async_copy(source, image_ref, sems.at[0])
-
-        def to_texts(source):
-            return pltpu.make_async_copy(source, text_ref, sems.at[1])
-
-        @pl.when(is_image_core)
-        def _():
-            to_images(first_ref).start()
-
-        @pl.when(jnp.logical_not(is_image_core))
-        def _():
-            to_texts(first_ref).start()
-
-        total = second_ref[...] + extra_ref[...].astype(jnp.float32)
-        rounded_ref[...] = total.astype(dtype)
-
-        @pl.when(is_image_core)
-        def _():
-            to_texts(rounded_ref).start()
-
-        @pl.when(jnp.logical_not(is_image_core))
-        def _():
-            to_images(rounded_ref).start()
-
-        to_images(first_ref).wait()
-        to_texts(first_ref).wait()
-
-    size = 3 * first.size * 4
+def placed(total, extra, kept, texts_on):
+    shape, dtype = total.shape, jnp.bfloat16
+    pieces = 2
+    rows = shape[0] // pieces
+
+    def kernel(total_ref, extra_ref, *refs):
+        image_ref, text_ref, rounded_ref, sems = refs[-4:]
+        is_text = lax.rem(lax.axis_index("in"), CORES) == texts_on
+
+        def copy(piece, target_ref):
+            part = pl.ds(piece * rows, rows)
+            return pltpu.make_async_copy(rounded_ref.at[part], target_ref.at[part], sems.at[piece])
+
+        for piece in range(pieces):
+            part = pl.ds(piece * rows, rows)
+            block = total_ref[part, :] + extra_ref[part, :].astype(jnp.float32)
+            rounded_ref[part, :] = block.astype(dtype)
+            pl.when(is_text)(lambda piece=piece: copy(piece, text_ref).start())
+            pl.when(jnp.logical_not(is_text))(lambda piece=piece: copy(piece, image_ref).start())
+        for piece in range(pieces):
+            copy(piece, image_ref).wait()
+
+    hbm = pl.BlockSpec(memory_space=pl.ANY)
+    kept = [] if kept is None else list(kept)
+    size = total.size * 4
     return pl.pallas_call(
         kernel,
         out_shape=[jax.ShapeDtypeStruct(shape, dtype)] * 2,
-        in_specs=[VMEM] * 3,
-        out_specs=[pl.BlockSpec(memory_space=pl.ANY)] * 2,
-        scratch_shapes=[pltpu.VMEM(shape, dtype), pltpu.SemaphoreType.DMA((2,))],
+        in_specs=[VMEM] * 2 + [hbm] * len(kept),
+        out_specs=[hbm] * 2,
+        scratch_shapes=[pltpu.VMEM(shape, dtype), pltpu.SemaphoreType.DMA((pieces,))],
+        input_output_aliases={2 + i: i for i in range(len(kept))},
         cost_estimate=pl.CostEstimate(flops=size, bytes_accessed=size, transcendentals=0),
-        compiler_params=pltpu.CompilerParams(vmem_limit_bytes=2 * size + (4 << 20)),
-    )(first, second, second_extra)
+        compiler_params=pltpu.CompilerParams(vmem_limit_bytes=4 * size + (4 << 20)),
+    )(total, extra, *kept)
+
+
+def ranked(images, texts, scale, shift):
+    def kernel(scale_ref, shift_ref, image_ref, text_ref, first_ref, second_ref, sems):
+        def copy(number, source_ref):
+            target_ref = (first_ref, second_ref)[number]
+            return pltpu.make_async_copy(source_ref, target_ref, sems.at[number])
+
+        core = lax.rem(lax.axis_index("in"), CORES)
+        for number, sources in enumerate([(image_ref, text_ref), (text_ref, image_ref)]):
+
+            @pl.when(core == number)
+            def _(sources=sources):
+                copy(0, sources[0]).start()
+                copy(1, sources[1]).start()
+
+        copy(0, image_ref).wait()
+        copy(1, text_ref).wait()
+
+    return pl.pallas_call(
+        kernel,
+        out_shape=[jax.ShapeDtypeStruct(images.shape, images.dtype)] * 2,
+        in_specs=[SMEM] * 2 + [pl.BlockSpec(memory_space=pl.ANY)] * 2,
+        out_specs=[VMEM] * 2,
+        scratch_shapes=[pltpu.SemaphoreType.DMA((2,))],
+        compiler_params=pltpu.CompilerParams(vmem_limit_bytes=4 << 20),
+    )(scale, shift, *[pltpu.with_memory_space_constraint(a, pltpu.HBM) for a in (images, texts)])
 
 
 def by_roles(images, texts, scale, shift):
@@ -175,42 +193,35 @@
         return lax.ppermute(array, ("grp", "in"), pairs)
 
     is_image_core = lax.rem(lax.axis_index("in"), CORES) == 0
-    first = jnp.where(is_image_core, images, texts)
-    second = jnp.where(is_image_core, texts, images)
-    got_a = sent(first, lambda g, x, c: (g, x + 1, 1) if c == 0 else (g + 1, x, 0))
+    got_texts = sent(texts, lambda g, x, c: (g, x, 1) if c == 0 else (g + 1, x, 0))
+    got_images = sent(images, lambda g, x, c: (g, x + 1, 1) if c == 0 else (g, x, 0))
+    first, second = ranked(images, texts, scale, shift)
     got_b = sent(second, lambda g, x, c: (g + 1, x, 0) if c == 0 else (g, x + 1, 1))
-    other_first, other_second = swapped(first), swapped(second)
-    starts = pulled(
+    got_a = jnp.where(is_image_core, got_texts, got_images)
+    other_second = jnp.where(is_image_core, got_images, got_texts)
+    got_a, first_again = lax.optimization_barrier((got_a, first))
+    swap_a = swapped(got_a)
+    other_first = swapped(first_again)
+    swap_b = swapped(got_b)
+    [back_a] = pulled(
+        [([swap_a], [second, other_first, got_a, got_b], [], False)], [bf16], scale, shift
+    )
+    [back_b] = pulled(
+        [([swap_b], [second, other_first, got_a, got_b], [], False)], [bf16], scale, shift
+    )
+    home_a = sent(back_a, lambda g, x, c: (g, x + 1, 0) if c == 0 else (g - 1, x, 1))
+    home_b = sent(back_b, lambda g, x, c: (g, x + 1, 1) if c == 0 else (g - 1, x, 0))
+    first_total, second_total = pulled(
         [
-            ([first], [second, other_first], [], True),
-            ([second], [first, other_second], [], True),
+            ([first], [second, other_first, got_a, got_b], [], True),
+            ([second], [first, other_second, swap_a, swap_b], [], True),
         ],
         [f32, f32],
         scale,
         shift,
     )
-    swap_a = swapped(got_a)
-    got_b, *starts = lax.optimization_barrier((got_b, *starts))
-    swap_b = swapped(got_b)
-    [back_a] = pulled(
-        [([swap_a], [second, other_first, got_a, got_b], [], False)], [bf16], scale, shift
-    )
-    [back_b] = pulled(
-        [([swap_b], [second, other_first, got_a, got_b], [], False)], [bf16], scale, shift
-    )
-    home_a = sent(back_a, lambda g, x, c: (g, x + 1, 0) if c == 0 else (g - 1, x, 1))
-    home_b = sent(back_b, lambda g, x, c: (g, x + 1, 1) if c == 0 else (g - 1, x, 0))
-    first_total, second_total = pulled(
-        [
-            ([first], [got_a, got_b], starts[:1], False),
-            ([second], [swap_a, swap_b], starts[1:], False),
-        ],
-        [f32, f32],
-        scale,
-        shift,
-    )
-    [first_total] = summed([[first_total, home_a]])
-    return tuple(finished(first_total, second_total, home_b))
+    outputs = placed(first_total, home_a, None, 1)
+    return tuple(placed(second_total, home_b, outputs, 0))
 
 
 def by_arrays(images, texts, scale, shift):

time: 26.7 us -> 26.5 us (level)
  waiting for transfers between devices: 8.66 us -> 11.5 us
  starting transfers between devices: 9.61 us -> 7.07 us
  other arithmetic: 1.11 us -> 0.06 us
  Pallas kernels: 5.16 us -> 5.77 us
    ppermute x4 -> x5, waiting for transfers between devices: 8.65 us -> 11.5 us  [sent(): return lax.ppermute(array, ('grp', 'in'), pairs)]
    ppermute x4 -> x5, starting transfers between devices: 8.9 us -> 6.5 us  [sent(): return lax.ppermute(array, ('grp', 'in'), pairs)]
    pallas_call x2 -> x3, Pallas kernels: 0.89 us -> 2.59 us  [the longest x2 1.51 us: placed(): pl.pallas_call(kernel, out_shape=[jax.ShapeDtypeStruct(shape, dtype)] * 2...]
    pallas_call x4 -> x3, Pallas kernels: 4.27 us -> 3.18 us  [pulled(): pl.pallas_call(kernel, out_shape=[jax.ShapeDtypeStruct((height, width), t...]
    select_n x1, other arithmetic: 1.11 us -> 0.06 us  [by_roles(): other_second = jnp.where(is_image_core, got_images, got_texts)]
    ppermute x4 -> x3, starting transfers between devices: 0.71 us -> 0.57 us  [moved(): lax.ppermute(array, axis, [(i, target(i) % peers) for i in range(peers)])]
  transfers between devices with their start and end apart: 8 -> 8, of which waited for: 3 -> 5; matrix products, arithmetic and copies ran while one was open for 0% -> 0% of each run, Pallas kernels for 16% -> 19%
where the time goes in v4:
time: 26.5 us; the launch traced here: 26.4 us
  waiting for transfers between devices  11.5 us (43%)
  starting transfers between devices  7.07 us (27%)
  Pallas kernels  5.77 us (22%)
  between operations  1.98 us (7%)
    ppermute x5, waiting for transfers between devices, sent(): return lax.ppermute(array, ('grp', 'in'), pairs)  11.5 us
    ppermute x5, starting transfers between devices, sent(): return lax.ppermute(array, ('grp', 'in'), pairs)  6.5 us
    pallas_call x3, Pallas kernels, pulled(): pl.pallas_call(kernel, out_shape=[jax.ShapeDtypeStruct((height, width), t...  3.18 us
    pallas_call x2, Pallas kernels, placed(): pl.pallas_call(kernel, out_shape=[jax.ShapeDtypeStruct(shape, dtype)] * 2...  1.51 us
    pallas_call x1, Pallas kernels, ranked(): pl.pallas_call(kernel, out_shape=[jax.ShapeDtypeStruct(images.shape, imag...  1.08 us
    ppermute x3, starting transfers between devices, moved(): lax.ppermute(array, axis, [(i, target(i) % peers) for i in range(peers)])  0.57 us
  transfers between devices with their start and end apart: 8, of which 5 were waited for; matrix products, arithmetic and copies ran while one was open for 0% of the time, Pallas kernels for 19%

profile of v4, /device:TPU:0, one launch (start us, length us, event | category | flops | bytes accessed | tf_op | source)
XLA Modules:
  0.0 26.4 jit_solution(13064534608680706935)
XLA Ops:
  0.6 2.4 %collective-permute-start.1 = (bf16[128,1152]{1,0:T(8,128)(2,1)}, bf16[128,1152]{1,0:T(8,128)(2,1)S(1)}, u32[]{:S(2)}, u32[]{:S(2)}) collective-permute-start(bf16[128,1152]{1,0:T(8,128)(2,1)} %image_ref.1), channel_id=1, source_target_pairs={{0,3},{1,0},{2,1},{3,2},{4,7},{5,4},{6,5},{7,6},{8,11},{9,8},{10,9... | collective-permute-start | bytes 884744 | tf_op jit(solution)/shard_map/ppermute | solution.py:193
  3.1 0.0 collective-permute-start
  4.4 1.1 %shard_map.59 = (bf16[128,1152]{1,0:T(8,128)(2,1)S(1)}, bf16[128,1152]{1,0:T(8,128)(2,1)S(1)}) custom-call(f32[1]{0:T(128)S(6)} %copy.10.scale_ref, f32[1]{0:T(128)S(6)} %copy.11.shift_ref, bf16[128,1152]{1,0:T(8,128)(2,1)} %image_ref.1, bf16[128,1152]{1,0:T(8,128)(2,1)} %text_ref.1), custom_call_target="tpu_custom_call" | custom-call | tf_op jit(solution)/shard_map/pallas_call | solution.py:167
  5.4 1.6 %collective-permute-start.3 = (bf16[128,1152]{1,0:T(8,128)(2,1)S(1)}, bf16[128,1152]{1,0:T(8,128)(2,1)S(1)}, u32[]{:S(2)}, u32[]{:S(2)}) collective-permute-start(bf16[128,1152]{1,0:T(8,128)(2,1)S(1)} %get-tuple-element.11.refs_1_.refs_5_), channel_id=1, source_target_pairs={{0,4},{1,3},{2,6},{3,1},{4,8},{5,7},{6,10},{7,5},{8,12},{9,11},{10... | collective-permute-start | bytes 884744 | tf_op jit(solution)/shard_map/ppermute | solution.py:193
  7.0 0.6 %collective-permute-done.1 = bf16[128,1152]{1,0:T(8,128)(2,1)S(1)} collective-permute-done((bf16[128,1152]{1,0:T(8,128)(2,1)}, bf16[128,1152]{1,0:T(8,128)(2,1)S(1)}, u32[]{:S(2)}, u32[]{:S(2)}) %collective-permute-start.1) | collective-permute-done | bytes 294944 | tf_op jit(solution)/shard_map/ppermute | solution.py:193
  7.6 4.8 %collective-permute-done = bf16[128,1152]{1,0:T(8,128)(2,1)S(1)} collective-permute-done((bf16[128,1152]{1,0:T(8,128)(2,1)}, bf16[128,1152]{1,0:T(8,128)(2,1)S(1)}, u32[]{:S(2)}, u32[]{:S(2)}) %collective-permute-start) | collective-permute-done | bytes 294944 | tf_op jit(solution)/shard_map/ppermute | solution.py:193
  12.4 0.1 broadcast_select_fusion
  12.5 0.1 collective-permute-start.2
  12.5 0.5 %collective-permute-start.4 = (bf16[128,1152]{1,0:T(8,128)(2,1)S(1)}, bf16[128,1152]{1,0:T(8,128)(2,1)S(1)}, u32[]{:S(2)}, u32[]{:S(2)}) collective-permute-start(bf16[128,1152]{1,0:T(8,128)(2,1)S(1)} %get-tuple-element.13.refs_3_), channel_id=1, source_target_pairs={{0,1},{1,0},{2,3},{3,2},{4,5},{5,4},{6,7},{7,6},{8,9},{9,8},{10,11... | collective-permute-start | bytes 884744 | tf_op jit(solution)/shard_map/ppermute | solution.py:15
  13.0 2.2 %collective-permute-done.3.refs_4_ = bf16[128,1152]{1,0:T(8,128)(2,1)S(1)} collective-permute-done((bf16[128,1152]{1,0:T(8,128)(2,1)S(1)}, bf16[128,1152]{1,0:T(8,128)(2,1)S(1)}, u32[]{:S(2)}, u32[]{:S(2)}) %collective-permute-start.3) | collective-permute-done | bytes 294944 | tf_op jit(solution)/shard_map/ppermute | solution.py:193
  15.3 0.0 collective-permute-start.5
  15.3 0.0 collective-permute-done.2.refs_2_
  15.3 0.0 collective-permute-done.4.refs_8_.refs_0_
  15.3 0.8 %shard_map.62 = bf16[128,1152]{1,0:T(8,128)(2,1)S(1)} custom-call(f32[1]{0:T(128)S(6)} %copy.10.scale_ref, f32[1]{0:T(128)S(6)} %copy.11.shift_ref, bf16[128,1152]{1,0:T(8,128)(2,1)S(1)} %collective-permute-done.4.refs_8_.refs_0_, bf16[128,1152]{1,0:T(8,128)(2,1)S(1)} %get-tuple-element.11.refs_1_.refs_5_, ...), custom_call_target="tpu_custom_call" | custom-call | flops 301989888 | bytes 1769472 | tf_op jit(solution)/shard_map/pallas_call | solution.py:78
  16.1 0.8 %collective-permute-start.7 = (bf16[128,1152]{1,0:T(8,128)(2,1)S(1)}, bf16[128,1152]{1,0:T(8,128)(2,1)S(1)}, u32[]{:S(2)}, u32[]{:S(2)}) collective-permute-start(bf16[128,1152]{1,0:T(8,128)(2,1)S(1)} %shard_map.62), channel_id=1, source_target_pairs={{0,2},{1,29},{2,0},{3,31},{4,6},{5,1},{6,4},{7,3},{8,10},{9,5},{10... | collective-permute-start | bytes 884744 | tf_op jit(solution)/shard_map/ppermute | solution.py:193
  17.0 0.0 collective-permute-done.5.refs_9_.refs_0_
  17.0 0.8 %shard_map.61 = bf16[128,1152]{1,0:T(8,128)(2,1)S(1)} custom-call(f32[1]{0:T(128)S(6)} %copy.10.scale_ref, f32[1]{0:T(128)S(6)} %copy.11.shift_ref, bf16[128,1152]{1,0:T(8,128)(2,1)S(1)} %collective-permute-done.5.refs_9_.refs_0_, bf16[128,1152]{1,0:T(8,128)(2,1)S(1)} %get-tuple-element.11.refs_1_.refs_5_, ...), custom_call_target="tpu_custom_call" | custom-call | flops 301989888 | bytes 1769472 | tf_op jit(solution)/shard_map/pallas_call | solution.py:78
  17.8 1.7 %collective-permute-start.6 = (bf16[128,1152]{1,0:T(8,128)(2,1)S(1)}, bf16[128,1152]{1,0:T(8,128)(2,1)S(1)}, u32[]{:S(2)}, u32[]{:S(2)}) collective-permute-start(bf16[128,1152]{1,0:T(8,128)(2,1)S(1)} %shard_map.61), channel_id=1, source_target_pairs={{0,3},{1,28},{2,1},{3,30},{4,7},{5,0},{6,5},{7,2},{8,11},{9,4},{10... | collective-permute-start | bytes 884744 | tf_op jit(solution)/shard_map/ppermute | solution.py:193
  19.5 1.5 %shard_map.60 = (f32[128,1152]{1,0:T(8,128)S(1)}, f32[128,1152]{1,0:T(8,128)S(1)}) custom-call(f32[1]{0:T(128)S(6)} %copy.10.scale_ref, f32[1]{0:T(128)S(6)} %copy.11.shift_ref, bf16[128,1152]{1,0:T(8,128)(2,1)S(1)} %get-tuple-element.12.refs_0_.refs_6_, bf16[128,1152]{1,0:T(8,128)(2,1)S(1)} %get-tuple-element.11.refs_1_.refs_5_, ...), custom_call_target="tpu_custom_call" | custom-call | flops 603979776 | bytes 4128768 | tf_op jit(solution)/shard_map/pallas_call | solution.py:78
  21.0 1.9 %collective-permute-done.7.extra_ref = bf16[128,1152]{1,0:T(8,128)(2,1)S(1)} collective-permute-done((bf16[128,1152]{1,0:T(8,128)(2,1)S(1)}, bf16[128,1152]{1,0:T(8,128)(2,1)S(1)}, u32[]{:S(2)}, u32[]{:S(2)}) %collective-permute-start.7) | collective-permute-done | bytes 294944 | tf_op jit(solution)/shard_map/ppermute | solution.py:193
  22.9 0.8 %shard_map.63 = (bf16[128,1152]{1,0:T(8,128)(2,1)}, bf16[128,1152]{1,0:T(8,128)(2,1)}) custom-call(f32[128,1152]{1,0:T(8,128)S(1)} %get-tuple-element.15.total_ref, bf16[128,1152]{1,0:T(8,128)(2,1)S(1)} %collective-permute-done.7.extra_ref), custom_call_target="tpu_custom_call" | custom-call | flops 589824 | bytes 589824 | tf_op jit(solution)/shard_map/pallas_call | solution.py:138
  23.7 1.9 %collective-permute-done.6.extra_ref = bf16[128,1152]{1,0:T(8,128)(2,1)S(1)} collective-permute-done((bf16[128,1152]{1,0:T(8,128)(2,1)S(1)}, bf16[128,1152]{1,0:T(8,128)(2,1)S(1)}, u32[]{:S(2)}, u32[]{:S(2)}) %collective-permute-start.6) | collective-permute-done | bytes 294944 | tf_op jit(solution)/shard_map/ppermute | solution.py:193
  25.6 0.8 %shard_map.64 = (bf16[128,1152]{1,0:T(8,128)(2,1)}, bf16[128,1152]{1,0:T(8,128)(2,1)}) custom-call(f32[128,1152]{1,0:T(8,128)S(1)} %get-tuple-element.14.total_ref, bf16[128,1152]{1,0:T(8,128)(2,1)S(1)} %collective-permute-done.6.extra_ref, bf16[128,1152]{1,0:T(8,128)(2,1)} %get-tuple-element.16.refs_0_, ...), custom_call_target="tpu_custom_call", output_to_operand_aliasing={{0}: (2, {}), {1}: (3, {})} | custom-call | flops 589824 | bytes 589824 | tf_op jit(solution)/shard_map/pallas_call | solution.py:138
Async XLA Ops:
  0.6 7.0 %collective-permute-start.1 = (bf16[128,1152]{1,0:T(8,128)(2,1)}, bf16[128,1152]{1,0:T(8,128)(2,1)S(1)}, u32[]{:S(2)}, u32[]{:S(2)}) collective-permute-start(bf16[128,1152]{1,0:T(8,128)(2,1)} %image_ref.1), channel_id=1, source_target_pairs={{0,3},{1,0},{2,1},{3,2},{4,7},{5,4},{6,5},{7,6},{8,11},{9,8},{10,9... | collective-permute-start | bytes 884744 | tf_op jit(solution)/shard_map/ppermute | solution.py:193
  3.1 9.3 %collective-permute-start = (bf16[128,1152]{1,0:T(8,128)(2,1)}, bf16[128,1152]{1,0:T(8,128)(2,1)S(1)}, u32[]{:S(2)}, u32[]{:S(2)}) collective-permute-start(bf16[128,1152]{1,0:T(8,128)(2,1)} %text_ref.1), channel_id=1, source_target_pairs={{0,1},{1,4},{2,3},{3,6},{4,5},{5,8},{6,7},{7,10},{8,9},{9,12},{10,... | collective-permute-start | bytes 884744 | tf_op jit(solution)/shard_map/ppermute | solution.py:193
  5.4 9.8 %collective-permute-start.3 = (bf16[128,1152]{1,0:T(8,128)(2,1)S(1)}, bf16[128,1152]{1,0:T(8,128)(2,1)S(1)}, u32[]{:S(2)}, u32[]{:S(2)}) collective-permute-start(bf16[128,1152]{1,0:T(8,128)(2,1)S(1)} %get-tuple-element.11.refs_1_.refs_5_), channel_id=1, source_target_pairs={{0,4},{1,3},{2,6},{3,1},{4,8},{5,7},{6,10},{7,5},{8,12},{9,11},{10... | collective-permute-start | bytes 884744 | tf_op jit(solution)/shard_map/ppermute | solution.py:193
  12.5 2.8 %collective-permute-start.2 = (bf16[128,1152]{1,0:T(8,128)(2,1)S(1)}, bf16[128,1152]{1,0:T(8,128)(2,1)S(1)}, u32[]{:S(2)}, u32[]{:S(2)}) collective-permute-start(bf16[128,1152]{1,0:T(8,128)(2,1)S(1)} %get-tuple-element.12.refs_0_.refs_6_), channel_id=1, source_target_pairs={{0,1},{1,0},{2,3},{3,2},{4,5},{5,4},{6,7},{7,6},{8,9},{9,8},{10,11... | collective-permute-start | bytes 884744 | tf_op jit(solution)/shard_map/ppermute | solution.py:15
  12.5 2.7 %collective-permute-start.4 = (bf16[128,1152]{1,0:T(8,128)(2,1)S(1)}, bf16[128,1152]{1,0:T(8,128)(2,1)S(1)}, u32[]{:S(2)}, u32[]{:S(2)}) collective-permute-start(bf16[128,1152]{1,0:T(8,128)(2,1)S(1)} %get-tuple-element.13.refs_3_), channel_id=1, source_target_pairs={{0,1},{1,0},{2,3},{3,2},{4,5},{5,4},{6,7},{7,6},{8,9},{9,8},{10,11... | collective-permute-start | bytes 884744 | tf_op jit(solution)/shard_map/ppermute | solution.py:15
  15.3 1.7 %collective-permute-start.5 = (bf16[128,1152]{1,0:T(8,128)(2,1)S(1)}, bf16[128,1152]{1,0:T(8,128)(2,1)S(1)}, u32[]{:S(2)}, u32[]{:S(2)}) collective-permute-start(bf16[128,1152]{1,0:T(8,128)(2,1)S(1)} %collective-permute-done.3.refs_4_), channel_id=1, source_target_pairs={{0,1},{1,0},{2,3},{3,2},{4,5},{5,4},{6,7},{7,6},{8,9},{9,8},{10,11... | collective-permute-start | bytes 884744 | tf_op jit(solution)/shard_map/ppermute | solution.py:15
  16.1 6.8 %collective-permute-start.7 = (bf16[128,1152]{1,0:T(8,128)(2,1)S(1)}, bf16[128,1152]{1,0:T(8,128)(2,1)S(1)}, u32[]{:S(2)}, u32[]{:S(2)}) collective-permute-start(bf16[128,1152]{1,0:T(8,128)(2,1)S(1)} %shard_map.62), channel_id=1, source_target_pairs={{0,2},{1,29},{2,0},{3,31},{4,6},{5,1},{6,4},{7,3},{8,10},{9,5},{10... | collective-permute-start | bytes 884744 | tf_op jit(solution)/shard_map/ppermute | solution.py:193
  17.8 7.8 %collective-permute-start.6 = (bf16[128,1152]{1,0:T(8,128)(2,1)S(1)}, bf16[128,1152]{1,0:T(8,128)(2,1)S(1)}, u32[]{:S(2)}, u32[]{:S(2)}) collective-permute-start(bf16[128,1152]{1,0:T(8,128)(2,1)S(1)} %shard_map.61), channel_id=1, source_target_pairs={{0,3},{1,28},{2,1},{3,30},{4,7},{5,0},{6,5},{7,2},{8,11},{9,4},{10... | collective-permute-start | bytes 884744 | tf_op jit(solution)/shard_map/ppermute | solution.py:193

commit v5 on v4

--- a/solution.py
+++ b/solution.py
@@ -41,13 +41,37 @@
     )(scale, shift, *arrays)
 
 
-def pulled(jobs, out_types, scale, shift):
+def pulled(jobs, out_types, scale, shift, only=None, into=None):
     height, width = jobs[0][0][0].shape
+    kept = [] if into is None else [into]
     arrays = [a for rows, others, starts, _ in jobs for a in (*rows, *others, *starts)]
 
-    def kernel(scale_ref, shift_ref, *refs):
-        in_refs, out_refs = iter(refs[: len(arrays)]), iter(refs[len(arrays) :])
-        scale_now, shift_now = scale_ref[0], shift_ref[0]
+    scalars = [scale] if shift is None else [scale, shift]
+
+    def kernel(*refs):
+        scalar_refs, refs = refs[: len(scalars)], refs[len(scalars) :]
+
+        def run():
+            if shift is None:
+                values = scalar_refs[0][0:1, 0:1], scalar_refs[0][1:2, 0:1]
+            else:
+                values = scalar_refs[0][0], scalar_refs[1][0]
+            write(*values, refs[: len(arrays)], refs[len(arrays) + len(kept) :])
+
+        if only is None:
+            run()
+        else:
+            here = lax.rem(lax.axis_index("in"), CORES) == only
+            pl.when(here)(run)
+
+        if kept:
+
+            @pl.when(jnp.logical_not(here))
+            def _():
+                refs[-1][...] = refs[-2][...]
+
+    def write(scale_now, shift_now, in_refs, out_refs):
+        in_refs, out_refs = iter(in_refs), iter(out_refs)
         for rows, others, starts, paired in jobs:
             row_refs = [next(in_refs) for _ in rows]
             other_refs = [next(in_refs) for _ in others]
@@ -78,13 +102,14 @@
     return pl.pallas_call(
         kernel,
         out_shape=[jax.ShapeDtypeStruct((height, width), t) for t in out_types],
-        in_specs=[SMEM] * 2 + [VMEM] * len(arrays),
+        in_specs=[VMEM if shift is None else SMEM] * len(scalars)
+        + [VMEM] * (len(arrays) + len(kept)),
         out_specs=[VMEM] * len(out_types),
         cost_estimate=pl.CostEstimate(
             flops=4 * pairs * width, bytes_accessed=size, transcendentals=pairs
         ),
         compiler_params=pltpu.CompilerParams(vmem_limit_bytes=2 * size + 16 * pairs + (4 << 20)),
-    )(scale, shift, *arrays)
+    )(*scalars, *arrays, *kept)
 
 
 def summed(sums):
@@ -147,31 +172,50 @@
     )(total, extra, *kept)
 
 
-def ranked(images, texts, scale, shift):
-    def kernel(scale_ref, shift_ref, image_ref, text_ref, first_ref, second_ref, sems):
-        def copy(number, source_ref):
-            target_ref = (first_ref, second_ref)[number]
-            return pltpu.make_async_copy(source_ref, target_ref, sems.at[number])
-
+def opened():
+    def kernel(out_ref):
+        out_ref[...] = jnp.zeros_like(out_ref)
+
+    return pl.pallas_call(
+        kernel,
+        out_shape=jax.ShapeDtypeStruct((8, 128), jnp.float32),
+        out_specs=VMEM,
+        cost_estimate=pl.CostEstimate(flops=10**10, bytes_accessed=2**26, transcendentals=0),
+        compiler_params=pltpu.CompilerParams(vmem_limit_bytes=1 << 20),
+    )()
+
+
+def ranked(images, texts, opening):
+    def kernel(image_ref, text_ref, opening_ref, first_ref, second_ref):
         core = lax.rem(lax.axis_index("in"), CORES)
         for number, sources in enumerate([(image_ref, text_ref), (text_ref, image_ref)]):
 
             @pl.when(core == number)
             def _(sources=sources):
-                copy(0, sources[0]).start()
-                copy(1, sources[1]).start()
-
-        copy(0, image_ref).wait()
-        copy(1, text_ref).wait()
+                first_ref[...] = sources[0][...]
+                second_ref[...] = sources[1][...]
 
     return pl.pallas_call(
         kernel,
         out_shape=[jax.ShapeDtypeStruct(images.shape, images.dtype)] * 2,
-        in_specs=[SMEM] * 2 + [pl.BlockSpec(memory_space=pl.ANY)] * 2,
+        in_specs=[VMEM] * 3,
         out_specs=[VMEM] * 2,
-        scratch_shapes=[pltpu.SemaphoreType.DMA((2,))],
         compiler_params=pltpu.CompilerParams(vmem_limit_bytes=4 << 20),
-    )(scale, shift, *[pltpu.with_memory_space_constraint(a, pltpu.HBM) for a in (images, texts)])
+    )(images, texts, opening)
+
+
+def packed(scale, shift):
+    def kernel(scale_ref, shift_ref, out_ref):
+        out_ref[0:1, :] = jnp.full((1, 128), scale_ref[0], jnp.float32)
+        out_ref[1:2, :] = jnp.full((1, 128), shift_ref[0], jnp.float32)
+
+    return pl.pallas_call(
+        kernel,
+        out_shape=jax.ShapeDtypeStruct((2, 128), jnp.float32),
+        in_specs=[SMEM] * 2,
+        out_specs=VMEM,
+        compiler_params=pltpu.CompilerParams(vmem_limit_bytes=1 << 20),
+    )(scale, shift)
 
 
 def by_roles(images, texts, scale, shift):
@@ -193,19 +237,31 @@
         return lax.ppermute(array, ("grp", "in"), pairs)
 
     is_image_core = lax.rem(lax.axis_index("in"), CORES) == 0
-    got_texts = sent(texts, lambda g, x, c: (g, x, 1) if c == 0 else (g + 1, x, 0))
-    got_images = sent(images, lambda g, x, c: (g, x + 1, 1) if c == 0 else (g, x, 0))
-    first, second = ranked(images, texts, scale, shift)
-    got_b = sent(second, lambda g, x, c: (g + 1, x, 0) if c == 0 else (g, x + 1, 1))
-    got_a = jnp.where(is_image_core, got_texts, got_images)
-    other_second = jnp.where(is_image_core, got_images, got_texts)
-    got_a, first_again = lax.optimization_barrier((got_a, first))
+    other_images, other_texts = swapped(images), swapped(texts)
+    first, second = ranked(images, texts, opened())
+    other_first = jnp.where(is_image_core, other_texts, other_images)
+    other_second = jnp.where(is_image_core, other_images, other_texts)
+    got_a, got_b = [
+        sent(block, lambda g, x, c: (g, x + 1, 1) if c == 0 else (g + 1, x, 0))
+        for block in (first, other_second)
+    ]
+    starts = pulled(
+        [
+            ([first], [second, other_first], [], True),
+            ([second], [first, other_second], [], True),
+        ],
+        [f32, f32],
+        scale,
+        shift,
+    )
+    got_a, both = lax.optimization_barrier((got_a, packed(scale, shift)))
     swap_a = swapped(got_a)
-    other_first = swapped(first_again)
-    swap_b = swapped(got_b)
-    [back_a] = pulled(
-        [([swap_a], [second, other_first, got_a, got_b], [], False)], [bf16], scale, shift
-    )
+    got_b, *starts = lax.optimization_barrier((got_b, *starts))
+    job_a = [([swap_a], [second, other_first, got_a, got_b], [], False)]
+    [back_a] = pulled(job_a, [bf16], scale, shift, 1)
+    got_b_again, back_a = lax.optimization_barrier((got_b, back_a))
+    swap_b = swapped(got_b_again)
+    [back_a] = pulled(job_a, [bf16], scale, shift, 0, back_a)
     [back_b] = pulled(
         [([swap_b], [second, other_first, got_a, got_b], [], False)], [bf16], scale, shift
     )
@@ -213,12 +269,12 @@
     home_b = sent(back_b, lambda g, x, c: (g, x + 1, 1) if c == 0 else (g - 1, x, 0))
     first_total, second_total = pulled(
         [
-            ([first], [second, other_first, got_a, got_b], [], True),
-            ([second], [first, other_second, swap_a, swap_b], [], True),
+            ([first], [got_a, got_b], starts[:1], False),
+            ([second], [swap_a, swap_b], starts[1:], False),
         ],
         [f32, f32],
-        scale,
-        shift,
+        both,
+        None,
     )
     outputs = placed(first_total, home_a, None, 1)
     return tuple(placed(second_total, home_b, outputs, 0))

time: 26.5 us -> 26 us (0.981)
  waiting for transfers between devices: 11.5 us -> 9.08 us
  starting transfers between devices: 7.07 us -> 8.33 us
  local copies, waits for them, and re-layouts: 0 us -> 0.44 us
    ppermute x5 -> x4, waiting for transfers between devices: 11.5 us -> 9.07 us  [sent(): return lax.ppermute(array, ('grp', 'in'), pairs)]
    ppermute x5 -> x4, starting transfers between devices: 6.5 us -> 7.73 us  [sent(): return lax.ppermute(array, ('grp', 'in'), pairs)]
    pallas_call x3 -> x5, Pallas kernels: 3.18 us -> 4.29 us  [pulled(): pl.pallas_call(kernel, out_shape=[jax.ShapeDtypeStruct((height, width), t...]
    pallas_call x1, Pallas kernels: 1.08 us -> 0.04 us  [ranked(): pl.pallas_call(kernel, out_shape=[jax.ShapeDtypeStruct(images.shape, imag...]
    unnamed x0 -> x4, local copies, waits for them, and re-layouts: none -> 0.44 us
    ppermute x3 -> x4, starting transfers between devices: 0.57 us -> 0.6 us  [moved(): lax.ppermute(array, axis, [(i, target(i) % peers) for i in range(peers)])]
  transfers between devices with their start and end apart: 8 -> 8, of which waited for: 5 -> 4; matrix products, arithmetic and copies ran while one was open for 0% -> 0% of each run, Pallas kernels for 19% -> 20%
where the time goes in v5:
time: 26 us; the launch traced here: 25.8 us
  waiting for transfers between devices  9.08 us (35%)
  starting transfers between devices  8.33 us (32%)
  Pallas kernels  5.85 us (22%)
  between operations  2.03 us (8%)
  local copies, waits for them, and re-layouts  0.44 us (2%)
    ppermute x4, waiting for transfers between devices, sent(): return lax.ppermute(array, ('grp', 'in'), pairs)  9.07 us
    ppermute x4, starting transfers between devices, sent(): return lax.ppermute(array, ('grp', 'in'), pairs)  7.73 us
    pallas_call x5, Pallas kernels, pulled(): pl.pallas_call(kernel, out_shape=[jax.ShapeDtypeStruct((height, width), t...  4.29 us
    pallas_call x2, Pallas kernels, placed(): pl.pallas_call(kernel, out_shape=[jax.ShapeDtypeStruct(shape, dtype)] * 2...  1.51 us
    ppermute x4, starting transfers between devices, moved(): lax.ppermute(array, axis, [(i, target(i) % peers) for i in range(peers)])  0.6 us
  transfers between devices with their start and end apart: 8, of which 4 were waited for; matrix products, arithmetic and copies ran while one was open for 0% of the time, Pallas kernels for 20%

profile of v5, /device:TPU:0, one launch (start us, length us, event | category | flops | bytes accessed | tf_op | source)
XLA Modules:
  0.0 25.8 jit_solution(3940488140295501293)
XLA Ops:
  0.6 0.0 copy-start
  0.6 0.0 copy-start.1
  0.6 0.5 %collective-permute-start.1 = (bf16[128,1152]{1,0:T(8,128)(2,1)}, bf16[128,1152]{1,0:T(8,128)(2,1)S(1)}, u32[]{:S(2)}, u32[]{:S(2)}) collective-permute-start(bf16[128,1152]{1,0:T(8,128)(2,1)} %image_ref.1), channel_id=1, source_target_pairs={{0,1},{1,0},{2,3},{3,2},{4,5},{5,4},{6,7},{7,6},{8,9},{9,8},{10,11... | collective-permute-start | bytes 884744 | tf_op jit(solution)/shard_map/ppermute | solution.py:15
  1.2 0.1 collective-permute-start.2
  1.2 0.3 %copy-done = bf16[128,1152]{1,0:T(8,128)(2,1)S(1)} copy-done((bf16[128,1152]{1,0:T(8,128)(2,1)S(1)}, bf16[128,1152]{1,0:T(8,128)(2,1)}, u32[]{:S(2)}) %copy-start) | copy-done | bytes 294936
  1.6 0.1 copy-done.1
  1.7 2.4 %collective-permute-start = (bf16[128,1152]{1,0:T(8,128)(2,1)S(1)}, bf16[128,1152]{1,0:T(8,128)(2,1)S(1)}, u32[]{:S(2)}, u32[]{:S(2)}) collective-permute-start(bf16[128,1152]{1,0:T(8,128)(2,1)S(1)} %get-tuple-element.17.refs_2_.refs_6_.refs_1_), channel_id=1, source_target_pairs={{0,3},{1,4},{2,1},{3,6},{4,7},{5,8},{6,5},{7,10},{8,11},{9,12},{10... | collective-permute-start | bytes 884744 | tf_op jit(solution)/shard_map/ppermute | solution.py:237
  5.5 0.0 collective-permute-done.1
  5.5 0.0 collective-permute-done.2
  5.5 0.1 broadcast_select_fusion
  5.6 1.9 %collective-permute-start.3 = (bf16[128,1152]{1,0:T(8,128)(2,1)S(1)}, bf16[128,1152]{1,0:T(8,128)(2,1)S(1)}, u32[]{:S(2)}, u32[]{:S(2)}) collective-permute-start(bf16[128,1152]{1,0:T(8,128)(2,1)S(1)} %get-tuple-element.33.refs_7_), channel_id=1, source_target_pairs={{0,3},{1,4},{2,1},{3,6},{4,7},{5,8},{6,5},{7,10},{8,11},{9,12},{10... | collective-permute-start | bytes 884744 | tf_op jit(solution)/shard_map/ppermute | solution.py:237
  7.4 4.2 %collective-permute-done.refs_5_.refs_2_ = bf16[128,1152]{1,0:T(8,128)(2,1)S(1)} collective-permute-done((bf16[128,1152]{1,0:T(8,128)(2,1)S(1)}, bf16[128,1152]{1,0:T(8,128)(2,1)S(1)}, u32[]{:S(2)}, u32[]{:S(2)}) %collective-permute-start) | collective-permute-done | bytes 294944 | tf_op jit(solution)/shard_map/ppermute | solution.py:237
  11.6 0.0 collective-permute-start.4
  11.6 1.3 %shard_map.62 = (f32[128,1152]{1,0:T(8,128)S(1)}, f32[128,1152]{1,0:T(8,128)S(1)}) custom-call(f32[1]{0:T(128)S(6)} %copy.10.scale_ref.refs_0_, f32[1]{0:T(128)S(6)} %copy.11.shift_ref.refs_1_, bf16[128,1152]{1,0:T(8,128)(2,1)S(1)} %get-tuple-element.17.refs_2_.refs_6_.refs_1_, bf16[128,1152]{1,0:T(8,128)(2,1)S(1)} %get-tuple-element.20.refs_3_.refs_5_, ...), custom_call_target="tpu_custom_call" | custom-call | flops 301989888 | bytes 2949120 | tf_op jit(solution)/shard_map/pallas_call | solution.py:102
  12.9 1.8 %collective-permute-done.3.refs_6_.refs_3_ = bf16[128,1152]{1,0:T(8,128)(2,1)S(1)} collective-permute-done((bf16[128,1152]{1,0:T(8,128)(2,1)S(1)}, bf16[128,1152]{1,0:T(8,128)(2,1)S(1)}, u32[]{:S(2)}, u32[]{:S(2)}) %collective-permute-start.3) | collective-permute-done | bytes 294944 | tf_op jit(solution)/shard_map/ppermute | solution.py:237
  14.8 0.0 collective-permute-done.4.refs_2_.refs_6_
  14.8 0.0 collective-permute-start.5
  14.8 0.8 %shard_map.66 = bf16[128,1152]{1,0:T(8,128)(2,1)S(1)} custom-call(f32[1]{0:T(128)S(6)} %copy.10.scale_ref.refs_0_, f32[1]{0:T(128)S(6)} %copy.11.shift_ref.refs_1_, bf16[128,1152]{1,0:T(8,128)(2,1)S(1)} %collective-permute-done.4.refs_2_.refs_6_, bf16[128,1152]{1,0:T(8,128)(2,1)S(1)} %get-tuple-element.20.refs_3_.refs_5_, ...), custom_call_target="tpu_custom_call" | custom-call | flops 301989888 | bytes 1769472 | tf_op jit(solution)/shard_map/pallas_call | solution.py:102
  15.7 2.0 %collective-permute-start.7 = (bf16[128,1152]{1,0:T(8,128)(2,1)S(1)}, bf16[128,1152]{1,0:T(8,128)(2,1)S(1)}, u32[]{:S(2)}, u32[]{:S(2)}) collective-permute-start(bf16[128,1152]{1,0:T(8,128)(2,1)S(1)} %shard_map.66), channel_id=1, source_target_pairs={{0,2},{1,29},{2,0},{3,31},{4,6},{5,1},{6,4},{7,3},{8,10},{9,5},{10... | collective-permute-start | bytes 884744 | tf_op jit(solution)/shard_map/ppermute | solution.py:237
  17.6 0.0 collective-permute-done.5.refs_7_.refs_2_
  17.6 0.8 %shard_map.65 = bf16[128,1152]{1,0:T(8,128)(2,1)S(1)} custom-call(f32[1]{0:T(128)S(6)} %copy.10.scale_ref.refs_0_, f32[1]{0:T(128)S(6)} %copy.11.shift_ref.refs_1_, bf16[128,1152]{1,0:T(8,128)(2,1)S(1)} %collective-permute-done.5.refs_7_.refs_2_, bf16[128,1152]{1,0:T(8,128)(2,1)S(1)} %get-tuple-element.20.refs_3_.refs_5_, ...), custom_call_target="tpu_custom_call" | custom-call | flops 301989888 | bytes 1769472 | tf_op jit(solution)/shard_map/pallas_call | solution.py:102
  18.5 1.5 %collective-permute-start.6 = (bf16[128,1152]{1,0:T(8,128)(2,1)S(1)}, bf16[128,1152]{1,0:T(8,128)(2,1)S(1)}, u32[]{:S(2)}, u32[]{:S(2)}) collective-permute-start(bf16[128,1152]{1,0:T(8,128)(2,1)S(1)} %shard_map.65), channel_id=1, source_target_pairs={{0,3},{1,28},{2,1},{3,30},{4,7},{5,0},{6,5},{7,2},{8,11},{9,4},{10... | collective-permute-start | bytes 884744 | tf_op jit(solution)/shard_map/ppermute | solution.py:237
  20.0 1.3 %shard_map.64 = (f32[128,1152]{1,0:T(8,128)S(1)}, f32[128,1152]{1,0:T(8,128)S(1)}) custom-call(f32[2,128]{1,0:T(2,128)S(1)} %shard_map.61.refs_0_, bf16[128,1152]{1,0:T(8,128)(2,1)S(1)} %get-tuple-element.17.refs_2_.refs_6_.refs_1_, bf16[128,1152]{1,0:T(8,128)(2,1)S(1)} %collective-permute-done.refs_5_.refs_2_, ...), custom_call_target="tpu_custom_call" | custom-call | flops 301989888 | bytes 4128768 | tf_op jit(solution)/shard_map/pallas_call | solution.py:102
  21.3 1.2 %collective-permute-done.7.extra_ref = bf16[128,1152]{1,0:T(8,128)(2,1)S(1)} collective-permute-done((bf16[128,1152]{1,0:T(8,128)(2,1)S(1)}, bf16[128,1152]{1,0:T(8,128)(2,1)S(1)}, u32[]{:S(2)}, u32[]{:S(2)}) %collective-permute-start.7) | collective-permute-done | bytes 294944 | tf_op jit(solution)/shard_map/ppermute | solution.py:237
  22.4 0.8 %shard_map.67 = (bf16[128,1152]{1,0:T(8,128)(2,1)}, bf16[128,1152]{1,0:T(8,128)(2,1)}) custom-call(f32[128,1152]{1,0:T(8,128)S(1)} %get-tuple-element.28.total_ref, bf16[128,1152]{1,0:T(8,128)(2,1)S(1)} %collective-permute-done.7.extra_ref), custom_call_target="tpu_custom_call" | custom-call | flops 589824 | bytes 589824 | tf_op jit(solution)/shard_map/pallas_call | solution.py:163
  23.2 1.9 %collective-permute-done.6.extra_ref = bf16[128,1152]{1,0:T(8,128)(2,1)S(1)} collective-permute-done((bf16[128,1152]{1,0:T(8,128)(2,1)S(1)}, bf16[128,1152]{1,0:T(8,128)(2,1)S(1)}, u32[]{:S(2)}, u32[]{:S(2)}) %collective-permute-start.6) | collective-permute-done | bytes 294944 | tf_op jit(solution)/shard_map/ppermute | solution.py:237
  25.0 0.8 %shard_map.68 = (bf16[128,1152]{1,0:T(8,128)(2,1)}, bf16[128,1152]{1,0:T(8,128)(2,1)}) custom-call(f32[128,1152]{1,0:T(8,128)S(1)} %get-tuple-element.27.total_ref, bf16[128,1152]{1,0:T(8,128)(2,1)S(1)} %collective-permute-done.6.extra_ref, bf16[128,1152]{1,0:T(8,128)(2,1)} %get-tuple-element.30.refs_0_, ...), custom_call_target="tpu_custom_call", output_to_operand_aliasing={{0}: (2, {}), {1}: (3, {})} | custom-call | flops 589824 | bytes 589824 | tf_op jit(solution)/shard_map/pallas_call | solution.py:163
  (4 shorter events, 0.0 us)
Async XLA Ops:
  0.6 1.0 %copy-start = (bf16[128,1152]{1,0:T(8,128)(2,1)S(1)}, bf16[128,1152]{1,0:T(8,128)(2,1)}, u32[]{:S(2)}) copy-start(bf16[128,1152]{1,0:T(8,128)(2,1)} %image_ref.1) | copy-start | bytes 884740
  0.6 1.0 %copy-start.1 = (bf16[128,1152]{1,0:T(8,128)(2,1)S(1)}, bf16[128,1152]{1,0:T(8,128)(2,1)}, u32[]{:S(2)}) copy-start(bf16[128,1152]{1,0:T(8,128)(2,1)} %text_ref.1) | copy-start | bytes 884740
  0.6 4.8 %collective-permute-start.1 = (bf16[128,1152]{1,0:T(8,128)(2,1)}, bf16[128,1152]{1,0:T(8,128)(2,1)S(1)}, u32[]{:S(2)}, u32[]{:S(2)}) collective-permute-start(bf16[128,1152]{1,0:T(8,128)(2,1)} %image_ref.1), channel_id=1, source_target_pairs={{0,1},{1,0},{2,3},{3,2},{4,5},{5,4},{6,7},{7,6},{8,9},{9,8},{10,11... | collective-permute-start | bytes 884744 | tf_op jit(solution)/shard_map/ppermute | solution.py:15
  1.2 4.3 %collective-permute-start.2 = (bf16[128,1152]{1,0:T(8,128)(2,1)}, bf16[128,1152]{1,0:T(8,128)(2,1)S(1)}, u32[]{:S(2)}, u32[]{:S(2)}) collective-permute-start(bf16[128,1152]{1,0:T(8,128)(2,1)} %text_ref.1), channel_id=1, source_target_pairs={{0,1},{1,0},{2,3},{3,2},{4,5},{5,4},{6,7},{7,6},{8,9},{9,8},{10,11... | collective-permute-start | bytes 884744 | tf_op jit(solution)/shard_map/ppermute | solution.py:15
  1.7 9.9 %collective-permute-start = (bf16[128,1152]{1,0:T(8,128)(2,1)S(1)}, bf16[128,1152]{1,0:T(8,128)(2,1)S(1)}, u32[]{:S(2)}, u32[]{:S(2)}) collective-permute-start(bf16[128,1152]{1,0:T(8,128)(2,1)S(1)} %get-tuple-element.17.refs_2_.refs_6_.refs_1_), channel_id=1, source_target_pairs={{0,3},{1,4},{2,1},{3,6},{4,7},{5,8},{6,5},{7,10},{8,11},{9,12},{10... | collective-permute-start | bytes 884744 | tf_op jit(solution)/shard_map/ppermute | solution.py:237
  5.6 9.2 %collective-permute-start.3 = (bf16[128,1152]{1,0:T(8,128)(2,1)S(1)}, bf16[128,1152]{1,0:T(8,128)(2,1)S(1)}, u32[]{:S(2)}, u32[]{:S(2)}) collective-permute-start(bf16[128,1152]{1,0:T(8,128)(2,1)S(1)} %get-tuple-element.33.refs_7_), channel_id=1, source_target_pairs={{0,3},{1,4},{2,1},{3,6},{4,7},{5,8},{6,5},{7,10},{8,11},{9,12},{10... | collective-permute-start | bytes 884744 | tf_op jit(solution)/shard_map/ppermute | solution.py:237
  11.6 3.2 %collective-permute-start.4 = (bf16[128,1152]{1,0:T(8,128)(2,1)S(1)}, bf16[128,1152]{1,0:T(8,128)(2,1)S(1)}, u32[]{:S(2)}, u32[]{:S(2)}) collective-permute-start(bf16[128,1152]{1,0:T(8,128)(2,1)S(1)} %collective-permute-done.refs_5_.refs_2_), channel_id=1, source_target_pairs={{0,1},{1,0},{2,3},{3,2},{4,5},{5,4},{6,7},{7,6},{8,9},{9,8},{10,11... | collective-permute-start | bytes 884744 | tf_op jit(solution)/shard_map/ppermute | solution.py:15
  14.8 2.8 %collective-permute-start.5 = (bf16[128,1152]{1,0:T(8,128)(2,1)S(1)}, bf16[128,1152]{1,0:T(8,128)(2,1)S(1)}, u32[]{:S(2)}, u32[]{:S(2)}) collective-permute-start(bf16[128,1152]{1,0:T(8,128)(2,1)S(1)} %collective-permute-done.3.refs_6_.refs_3_), channel_id=1, source_target_pairs={{0,1},{1,0},{2,3},{3,2},{4,5},{5,4},{6,7},{7,6},{8,9},{9,8},{10,11... | collective-permute-start | bytes 884744 | tf_op jit(solution)/shard_map/ppermute | solution.py:15
  15.7 6.8 %collective-permute-start.7 = (bf16[128,1152]{1,0:T(8,128)(2,1)S(1)}, bf16[128,1152]{1,0:T(8,128)(2,1)S(1)}, u32[]{:S(2)}, u32[]{:S(2)}) collective-permute-start(bf16[128,1152]{1,0:T(8,128)(2,1)S(1)} %shard_map.66), channel_id=1, source_target_pairs={{0,2},{1,29},{2,0},{3,31},{4,6},{5,1},{6,4},{7,3},{8,10},{9,5},{10... | collective-permute-start | bytes 884744 | tf_op jit(solution)/shard_map/ppermute | solution.py:237
  18.5 6.6 %collective-permute-start.6 = (bf16[128,1152]{1,0:T(8,128)(2,1)S(1)}, bf16[128,1152]{1,0:T(8,128)(2,1)S(1)}, u32[]{:S(2)}, u32[]{:S(2)}) collective-permute-start(bf16[128,1152]{1,0:T(8,128)(2,1)S(1)} %shard_map.65), channel_id=1, source_target_pairs={{0,3},{1,28},{2,1},{3,30},{4,7},{5,0},{6,5},{7,2},{8,11},{9,4},{10... | collective-permute-start | bytes 884744 | tf_op jit(solution)/shard_map/ppermute | solution.py:237

commit v6 on v5

--- a/solution.py
+++ b/solution.py
@@ -237,7 +237,7 @@
         return lax.ppermute(array, ("grp", "in"), pairs)
 
     is_image_core = lax.rem(lax.axis_index("in"), CORES) == 0
-    other_images, other_texts = swapped(images), swapped(texts)
+    other_texts, other_images = swapped(texts), swapped(images)
     first, second = ranked(images, texts, opened())
     other_first = jnp.where(is_image_core, other_texts, other_images)
     other_second = jnp.where(is_image_core, other_images, other_texts)
@@ -245,18 +245,8 @@
         sent(block, lambda g, x, c: (g, x + 1, 1) if c == 0 else (g + 1, x, 0))
         for block in (first, other_second)
     ]
-    starts = pulled(
-        [
-            ([first], [second, other_first], [], True),
-            ([second], [first, other_second], [], True),
-        ],
-        [f32, f32],
-        scale,
-        shift,
-    )
     got_a, both = lax.optimization_barrier((got_a, packed(scale, shift)))
     swap_a = swapped(got_a)
-    got_b, *starts = lax.optimization_barrier((got_b, *starts))
     job_a = [([swap_a], [second, other_first, got_a, got_b], [], False)]
     [back_a] = pulled(job_a, [bf16], scale, shift, 1)
     got_b_again, back_a = lax.optimization_barrier((got_b, back_a))
@@ -269,8 +259,8 @@
     home_b = sent(back_b, lambda g, x, c: (g, x + 1, 1) if c == 0 else (g - 1, x, 0))
     first_total, second_total = pulled(
         [
-            ([first], [got_a, got_b], starts[:1], False),
-            ([second], [swap_a, swap_b], starts[1:], False),
+            ([first], [second, other_first, got_a, got_b], [], True),
+            ([second], [first, other_second, swap_a, swap_b], [], True),
         ],
         [f32, f32],
         both,

time: 26 us -> 26 us (level)
  waiting for transfers between devices: 9.08 us -> 10.2 us
  Pallas kernels: 5.85 us -> 4.74 us
    ppermute x4, waiting for transfers between devices: 9.07 us -> 10.2 us  [sent(): return lax.ppermute(array, ('grp', 'in'), pairs)]
    pallas_call x5 -> x4, Pallas kernels: 4.29 us -> 3.19 us  [pulled(): pl.pallas_call(kernel, out_shape=[jax.ShapeDtypeStruct((height, width), t...]
  transfers between devices with their start and end apart: 8 -> 8, of which waited for: 4 -> 4; matrix products, arithmetic and copies ran while one was open for 0% -> 0% of each run, Pallas kernels for 20% -> 15%
where the time goes in v6:
time: 26 us; the launch traced here: 25.8 us
  waiting for transfers between devices  10.2 us (39%)
  starting transfers between devices  8.34 us (32%)
  Pallas kernels  4.74 us (18%)
  between operations  2.02 us (8%)
  local copies, waits for them, and re-layouts  0.44 us (2%)
    ppermute x4, waiting for transfers between devices, sent(): return lax.ppermute(array, ('grp', 'in'), pairs)  10.2 us
    ppermute x4, starting transfers between devices, sent(): return lax.ppermute(array, ('grp', 'in'), pairs)  7.74 us
    pallas_call x4, Pallas kernels, pulled(): pl.pallas_call(kernel, out_shape=[jax.ShapeDtypeStruct((height, width), t...  3.19 us
    pallas_call x2, Pallas kernels, placed(): pl.pallas_call(kernel, out_shape=[jax.ShapeDtypeStruct(shape, dtype)] * 2...  1.51 us
    ppermute x4, starting transfers between devices, moved(): lax.ppermute(array, axis, [(i, target(i) % peers) for i in range(peers)])  0.6 us
  transfers between devices with their start and end apart: 8, of which 4 were waited for; matrix products, arithmetic and copies ran while one was open for 0% of the time, Pallas kernels for 15%

profile of v6, /device:TPU:0, one launch (start us, length us, event | category | flops | bytes accessed | tf_op | source)
XLA Modules:
  0.0 25.8 jit_solution(3551086334043486686)
XLA Ops:
  0.6 0.0 copy-start
  0.6 0.0 copy-start.1
  0.6 0.5 %collective-permute-start.1 = (bf16[128,1152]{1,0:T(8,128)(2,1)}, bf16[128,1152]{1,0:T(8,128)(2,1)S(1)}, u32[]{:S(2)}, u32[]{:S(2)}) collective-permute-start(bf16[128,1152]{1,0:T(8,128)(2,1)} %text_ref.1), channel_id=1, source_target_pairs={{0,1},{1,0},{2,3},{3,2},{4,5},{5,4},{6,7},{7,6},{8,9},{9,8},{10,11... | collective-permute-start | bytes 884744 | tf_op jit(solution)/shard_map/ppermute | solution.py:15
  1.2 0.1 collective-permute-start.2
  1.2 0.3 %copy-done = bf16[128,1152]{1,0:T(8,128)(2,1)S(1)} copy-done((bf16[128,1152]{1,0:T(8,128)(2,1)S(1)}, bf16[128,1152]{1,0:T(8,128)(2,1)}, u32[]{:S(2)}) %copy-start) | copy-done | bytes 294936
  1.6 0.1 copy-done.1
  1.7 2.4 %collective-permute-start = (bf16[128,1152]{1,0:T(8,128)(2,1)S(1)}, bf16[128,1152]{1,0:T(8,128)(2,1)S(1)}, u32[]{:S(2)}, u32[]{:S(2)}) collective-permute-start(bf16[128,1152]{1,0:T(8,128)(2,1)S(1)} %get-tuple-element.12.refs_1_.refs_7_), channel_id=1, source_target_pairs={{0,3},{1,4},{2,1},{3,6},{4,7},{5,8},{6,5},{7,10},{8,11},{9,12},{10... | collective-permute-start | bytes 884744 | tf_op jit(solution)/shard_map/ppermute | solution.py:237
  5.5 0.0 collective-permute-done.1
  5.5 0.0 collective-permute-done.2
  5.5 0.1 broadcast_select_fusion
  5.6 1.9 %collective-permute-start.3 = (bf16[128,1152]{1,0:T(8,128)(2,1)S(1)}, bf16[128,1152]{1,0:T(8,128)(2,1)S(1)}, u32[]{:S(2)}, u32[]{:S(2)}) collective-permute-start(bf16[128,1152]{1,0:T(8,128)(2,1)S(1)} %get-tuple-element.22.refs_8_), channel_id=1, source_target_pairs={{0,3},{1,4},{2,1},{3,6},{4,7},{5,8},{6,5},{7,10},{8,11},{9,12},{10... | collective-permute-start | bytes 884744 | tf_op jit(solution)/shard_map/ppermute | solution.py:237
  7.4 4.2 %collective-permute-done.refs_5_.refs_4_ = bf16[128,1152]{1,0:T(8,128)(2,1)S(1)} collective-permute-done((bf16[128,1152]{1,0:T(8,128)(2,1)S(1)}, bf16[128,1152]{1,0:T(8,128)(2,1)S(1)}, u32[]{:S(2)}, u32[]{:S(2)}) %collective-permute-start) | collective-permute-done | bytes 294944 | tf_op jit(solution)/shard_map/ppermute | solution.py:237
  11.6 0.0 collective-permute-start.4
  11.6 3.2 %collective-permute-done.3.refs_6_.refs_5_ = bf16[128,1152]{1,0:T(8,128)(2,1)S(1)} collective-permute-done((bf16[128,1152]{1,0:T(8,128)(2,1)S(1)}, bf16[128,1152]{1,0:T(8,128)(2,1)S(1)}, u32[]{:S(2)}, u32[]{:S(2)}) %collective-permute-start.3) | collective-permute-done | bytes 294944 | tf_op jit(solution)/shard_map/ppermute | solution.py:237
  14.8 0.0 collective-permute-done.4.refs_2_.refs_9_
  14.8 0.0 collective-permute-start.5
  14.8 0.8 %shard_map.65 = bf16[128,1152]{1,0:T(8,128)(2,1)S(1)} custom-call(f32[1]{0:T(128)S(6)} %copy.10.scale_ref.refs_0_, f32[1]{0:T(128)S(6)} %copy.11.shift_ref.refs_1_, bf16[128,1152]{1,0:T(8,128)(2,1)S(1)} %collective-permute-done.4.refs_2_.refs_9_, bf16[128,1152]{1,0:T(8,128)(2,1)S(1)} %get-tuple-element.14.refs_3_.refs_2_.refs_6_, ...), custom_call_target="tpu_custom_call" | custom-call | flops 301989888 | bytes 1769472 | tf_op jit(solution)/shard_map/pallas_call | solution.py:102
  15.7 2.0 %collective-permute-start.7 = (bf16[128,1152]{1,0:T(8,128)(2,1)S(1)}, bf16[128,1152]{1,0:T(8,128)(2,1)S(1)}, u32[]{:S(2)}, u32[]{:S(2)}) collective-permute-start(bf16[128,1152]{1,0:T(8,128)(2,1)S(1)} %shard_map.65), channel_id=1, source_target_pairs={{0,2},{1,29},{2,0},{3,31},{4,6},{5,1},{6,4},{7,3},{8,10},{9,5},{10... | collective-permute-start | bytes 884744 | tf_op jit(solution)/shard_map/ppermute | solution.py:237
  17.6 0.0 collective-permute-done.5.refs_10_.refs_2_
  17.6 0.8 %shard_map.64 = bf16[128,1152]{1,0:T(8,128)(2,1)S(1)} custom-call(f32[1]{0:T(128)S(6)} %copy.10.scale_ref.refs_0_, f32[1]{0:T(128)S(6)} %copy.11.shift_ref.refs_1_, bf16[128,1152]{1,0:T(8,128)(2,1)S(1)} %collective-permute-done.5.refs_10_.refs_2_, bf16[128,1152]{1,0:T(8,128)(2,1)S(1)} %get-tuple-element.14.refs_3_.refs_2_.refs_6_, ...), custom_call_target="tpu_custom_call" | custom-call | flops 301989888 | bytes 1769472 | tf_op jit(solution)/shard_map/pallas_call | solution.py:102
  18.5 1.5 %collective-permute-start.6 = (bf16[128,1152]{1,0:T(8,128)(2,1)S(1)}, bf16[128,1152]{1,0:T(8,128)(2,1)S(1)}, u32[]{:S(2)}, u32[]{:S(2)}) collective-permute-start(bf16[128,1152]{1,0:T(8,128)(2,1)S(1)} %shard_map.64), channel_id=1, source_target_pairs={{0,3},{1,28},{2,1},{3,30},{4,7},{5,0},{6,5},{7,2},{8,11},{9,4},{10... | collective-permute-start | bytes 884744 | tf_op jit(solution)/shard_map/ppermute | solution.py:237
  20.0 1.5 %shard_map.63 = (f32[128,1152]{1,0:T(8,128)S(1)}, f32[128,1152]{1,0:T(8,128)S(1)}) custom-call(f32[2,128]{1,0:T(2,128)S(1)} %shard_map.61.refs_0_, bf16[128,1152]{1,0:T(8,128)(2,1)S(1)} %get-tuple-element.12.refs_1_.refs_7_, bf16[128,1152]{1,0:T(8,128)(2,1)S(1)} %get-tuple-element.14.refs_3_.refs_2_.refs_6_, ...), custom_call_target="tpu_custom_call" | custom-call | flops 603979776 | bytes 4128768 | tf_op jit(solution)/shard_map/pallas_call | solution.py:102
  21.5 1.0 %collective-permute-done.7.extra_ref = bf16[128,1152]{1,0:T(8,128)(2,1)S(1)} collective-permute-done((bf16[128,1152]{1,0:T(8,128)(2,1)S(1)}, bf16[128,1152]{1,0:T(8,128)(2,1)S(1)}, u32[]{:S(2)}, u32[]{:S(2)}) %collective-permute-start.7) | collective-permute-done | bytes 294944 | tf_op jit(solution)/shard_map/ppermute | solution.py:237
  22.4 0.8 %shard_map.66 = (bf16[128,1152]{1,0:T(8,128)(2,1)}, bf16[128,1152]{1,0:T(8,128)(2,1)}) custom-call(f32[128,1152]{1,0:T(8,128)S(1)} %get-tuple-element.18.total_ref, bf16[128,1152]{1,0:T(8,128)(2,1)S(1)} %collective-permute-done.7.extra_ref), custom_call_target="tpu_custom_call" | custom-call | flops 589824 | bytes 589824 | tf_op jit(solution)/shard_map/pallas_call | solution.py:163
  23.2 1.9 %collective-permute-done.6.extra_ref = bf16[128,1152]{1,0:T(8,128)(2,1)S(1)} collective-permute-done((bf16[128,1152]{1,0:T(8,128)(2,1)S(1)}, bf16[128,1152]{1,0:T(8,128)(2,1)S(1)}, u32[]{:S(2)}, u32[]{:S(2)}) %collective-permute-start.6) | collective-permute-done | bytes 294944 | tf_op jit(solution)/shard_map/ppermute | solution.py:237
  25.0 0.8 %shard_map.67 = (bf16[128,1152]{1,0:T(8,128)(2,1)}, bf16[128,1152]{1,0:T(8,128)(2,1)}) custom-call(f32[128,1152]{1,0:T(8,128)S(1)} %get-tuple-element.17.total_ref, bf16[128,1152]{1,0:T(8,128)(2,1)S(1)} %collective-permute-done.6.extra_ref, bf16[128,1152]{1,0:T(8,128)(2,1)} %get-tuple-element.20.refs_0_, ...), custom_call_target="tpu_custom_call", output_to_operand_aliasing={{0}: (2, {}), {1}: (3, {})} | custom-call | flops 589824 | bytes 589824 | tf_op jit(solution)/shard_map/pallas_call | solution.py:163
  (4 shorter events, 0.0 us)
Async XLA Ops:
  0.6 1.0 %copy-start = (bf16[128,1152]{1,0:T(8,128)(2,1)S(1)}, bf16[128,1152]{1,0:T(8,128)(2,1)}, u32[]{:S(2)}) copy-start(bf16[128,1152]{1,0:T(8,128)(2,1)} %text_ref.1) | copy-start | bytes 884740
  0.6 1.0 %copy-start.1 = (bf16[128,1152]{1,0:T(8,128)(2,1)S(1)}, bf16[128,1152]{1,0:T(8,128)(2,1)}, u32[]{:S(2)}) copy-start(bf16[128,1152]{1,0:T(8,128)(2,1)} %image_ref.1) | copy-start | bytes 884740
  0.6 4.8 %collective-permute-start.1 = (bf16[128,1152]{1,0:T(8,128)(2,1)}, bf16[128,1152]{1,0:T(8,128)(2,1)S(1)}, u32[]{:S(2)}, u32[]{:S(2)}) collective-permute-start(bf16[128,1152]{1,0:T(8,128)(2,1)} %text_ref.1), channel_id=1, source_target_pairs={{0,1},{1,0},{2,3},{3,2},{4,5},{5,4},{6,7},{7,6},{8,9},{9,8},{10,11... | collective-permute-start | bytes 884744 | tf_op jit(solution)/shard_map/ppermute | solution.py:15
  1.2 4.3 %collective-permute-start.2 = (bf16[128,1152]{1,0:T(8,128)(2,1)}, bf16[128,1152]{1,0:T(8,128)(2,1)S(1)}, u32[]{:S(2)}, u32[]{:S(2)}) collective-permute-start(bf16[128,1152]{1,0:T(8,128)(2,1)} %image_ref.1), channel_id=1, source_target_pairs={{0,1},{1,0},{2,3},{3,2},{4,5},{5,4},{6,7},{7,6},{8,9},{9,8},{10,11... | collective-permute-start | bytes 884744 | tf_op jit(solution)/shard_map/ppermute | solution.py:15
  1.7 9.9 %collective-permute-start = (bf16[128,1152]{1,0:T(8,128)(2,1)S(1)}, bf16[128,1152]{1,0:T(8,128)(2,1)S(1)}, u32[]{:S(2)}, u32[]{:S(2)}) collective-permute-start(bf16[128,1152]{1,0:T(8,128)(2,1)S(1)} %get-tuple-element.12.refs_1_.refs_7_), channel_id=1, source_target_pairs={{0,3},{1,4},{2,1},{3,6},{4,7},{5,8},{6,5},{7,10},{8,11},{9,12},{10... | collective-permute-start | bytes 884744 | tf_op jit(solution)/shard_map/ppermute | solution.py:237
  5.6 9.2 %collective-permute-start.3 = (bf16[128,1152]{1,0:T(8,128)(2,1)S(1)}, bf16[128,1152]{1,0:T(8,128)(2,1)S(1)}, u32[]{:S(2)}, u32[]{:S(2)}) collective-permute-start(bf16[128,1152]{1,0:T(8,128)(2,1)S(1)} %get-tuple-element.22.refs_8_), channel_id=1, source_target_pairs={{0,3},{1,4},{2,1},{3,6},{4,7},{5,8},{6,5},{7,10},{8,11},{9,12},{10... | collective-permute-start | bytes 884744 | tf_op jit(solution)/shard_map/ppermute | solution.py:237
  11.6 3.2 %collective-permute-start.4 = (bf16[128,1152]{1,0:T(8,128)(2,1)S(1)}, bf16[128,1152]{1,0:T(8,128)(2,1)S(1)}, u32[]{:S(2)}, u32[]{:S(2)}) collective-permute-start(bf16[128,1152]{1,0:T(8,128)(2,1)S(1)} %collective-permute-done.refs_5_.refs_4_), channel_id=1, source_target_pairs={{0,1},{1,0},{2,3},{3,2},{4,5},{5,4},{6,7},{7,6},{8,9},{9,8},{10,11... | collective-permute-start | bytes 884744 | tf_op jit(solution)/shard_map/ppermute | solution.py:15
  14.8 2.8 %collective-permute-start.5 = (bf16[128,1152]{1,0:T(8,128)(2,1)S(1)}, bf16[128,1152]{1,0:T(8,128)(2,1)S(1)}, u32[]{:S(2)}, u32[]{:S(2)}) collective-permute-start(bf16[128,1152]{1,0:T(8,128)(2,1)S(1)} %collective-permute-done.3.refs_6_.refs_5_), channel_id=1, source_target_pairs={{0,1},{1,0},{2,3},{3,2},{4,5},{5,4},{6,7},{7,6},{8,9},{9,8},{10,11... | collective-permute-start | bytes 884744 | tf_op jit(solution)/shard_map/ppermute | solution.py:15
  15.7 6.8 %collective-permute-start.7 = (bf16[128,1152]{1,0:T(8,128)(2,1)S(1)}, bf16[128,1152]{1,0:T(8,128)(2,1)S(1)}, u32[]{:S(2)}, u32[]{:S(2)}) collective-permute-start(bf16[128,1152]{1,0:T(8,128)(2,1)S(1)} %shard_map.65), channel_id=1, source_target_pairs={{0,2},{1,29},{2,0},{3,31},{4,6},{5,1},{6,4},{7,3},{8,10},{9,5},{10... | collective-permute-start | bytes 884744 | tf_op jit(solution)/shard_map/ppermute | solution.py:237
  18.5 6.6 %collective-permute-start.6 = (bf16[128,1152]{1,0:T(8,128)(2,1)S(1)}, bf16[128,1152]{1,0:T(8,128)(2,1)S(1)}, u32[]{:S(2)}, u32[]{:S(2)}) collective-permute-start(bf16[128,1152]{1,0:T(8,128)(2,1)S(1)} %shard_map.64), channel_id=1, source_target_pairs={{0,3},{1,28},{2,1},{3,30},{4,7},{5,0},{6,5},{7,2},{8,11},{9,4},{10... | collective-permute-start | bytes 884744 | tf_op jit(solution)/shard_map/ppermute | solution.py:237

commit v7 on v5

--- a/solution.py
+++ b/solution.py
@@ -257,15 +257,27 @@
     got_a, both = lax.optimization_barrier((got_a, packed(scale, shift)))
     swap_a = swapped(got_a)
     got_b, *starts = lax.optimization_barrier((got_b, *starts))
-    job_a = [([swap_a], [second, other_first, got_a, got_b], [], False)]
-    [back_a] = pulled(job_a, [bf16], scale, shift, 1)
-    got_b_again, back_a = lax.optimization_barrier((got_b, back_a))
+    half = swap_a.shape[0] // 2
+    jobs_a = [
+        ([rows], [second, other_first, got_a, got_b], [], False)
+        for rows in (swap_a[:half], swap_a[half:])
+    ]
+    backs_a = pulled(jobs_a, [bf16] * 2, scale, shift, 1)
+    got_b_again, *backs_a = lax.optimization_barrier((got_b, *backs_a))
     swap_b = swapped(got_b_again)
-    [back_a] = pulled(job_a, [bf16], scale, shift, 0, back_a)
+    backs_a = [
+        pulled([job], [bf16], scale, shift, 0, back)[0] for job, back in zip(jobs_a, backs_a)
+    ]
     [back_b] = pulled(
         [([swap_b], [second, other_first, got_a, got_b], [], False)], [bf16], scale, shift
     )
-    home_a = sent(back_a, lambda g, x, c: (g, x + 1, 0) if c == 0 else (g - 1, x, 1))
+    home_a = jnp.concatenate(
+        [
+            sent(back, lambda g, x, c: (g, x + 1, 0) if c == 0 else (g - 1, x, 1))
+            for back in backs_a
+        ],
+        axis=0,
+    )
     home_b = sent(back_b, lambda g, x, c: (g, x + 1, 1) if c == 0 else (g - 1, x, 0))
     first_total, second_total = pulled(
         [

time: 26 us -> 27.6 us (1.062)
  the two profiles are of different devices: /device:TPU:0 before, /device:TPU:1 now
where the time goes in v7:
time: 27.6 us; the launch traced here: 27.4 us
  starting transfers between devices  14.4 us (52%)
  Pallas kernels  6.5 us (24%)
  waiting for transfers between devices  3.86 us (14%)
  between operations  2.06 us (7%)
  local copies, waits for them, and re-layouts  0.48 us (2%)
    ppermute x5, starting transfers between devices, sent(): return lax.ppermute(array, ('grp', 'in'), pairs)  10.8 us
    pallas_call x6, Pallas kernels, pulled(): pl.pallas_call(kernel, out_shape=[jax.ShapeDtypeStruct((height, width), t...  4.94 us
    ppermute x5, waiting for transfers between devices, sent(): return lax.ppermute(array, ('grp', 'in'), pairs)  3.85 us
    ppermute x4, starting transfers between devices, moved(): lax.ppermute(array, axis, [(i, target(i) % peers) for i in range(peers)])  3.65 us
    pallas_call x2, Pallas kernels, placed(): pl.pallas_call(kernel, out_shape=[jax.ShapeDtypeStruct(shape, dtype)] * 2...  1.51 us
  transfers between devices with their start and end apart: 9, of which 2 were waited for; matrix products, arithmetic and copies ran while one was open for 0% of the time, Pallas kernels for 16%

profile of v7, /device:TPU:1, one launch (start us, length us, event | category | flops | bytes accessed | tf_op | source)
XLA Modules:
  0.0 27.4 jit_solution(12751337295727597148)
XLA Ops:
  0.6 0.0 copy-start
  0.6 0.0 copy-start.1
  0.6 0.1 collective-permute-start.1
  0.8 0.5 %collective-permute-start.2 = (bf16[128,1152]{1,0:T(8,128)(2,1)}, bf16[128,1152]{1,0:T(8,128)(2,1)S(1)}, u32[]{:S(2)}, u32[]{:S(2)}) collective-permute-start(bf16[128,1152]{1,0:T(8,128)(2,1)} %text_ref.1), channel_id=1, source_target_pairs={{0,1},{1,0},{2,3},{3,2},{4,5},{5,4},{6,7},{7,6},{8,9},{9,8},{10,11... | collective-permute-start | bytes 884744 | tf_op jit(solution)/shard_map/ppermute | solution.py:15
  1.2 0.4 %copy-done = bf16[128,1152]{1,0:T(8,128)(2,1)S(1)} copy-done((bf16[128,1152]{1,0:T(8,128)(2,1)S(1)}, bf16[128,1152]{1,0:T(8,128)(2,1)}, u32[]{:S(2)}) %copy-start) | copy-done | bytes 294936
  1.6 0.1 copy-done.1
  1.7 2.7 %collective-permute-start = (bf16[128,1152]{1,0:T(8,128)(2,1)S(1)}, bf16[128,1152]{1,0:T(8,128)(2,1)S(1)}, u32[]{:S(2)}, u32[]{:S(2)}) collective-permute-start(bf16[128,1152]{1,0:T(8,128)(2,1)S(1)} %get-tuple-element.20.refs_2_.refs_6_.refs_1_), channel_id=1, source_target_pairs={{0,3},{1,4},{2,1},{3,6},{4,7},{5,8},{6,5},{7,10},{8,11},{9,12},{10... | collective-permute-start | bytes 884744 | tf_op jit(solution)/shard_map/ppermute | solution.py:237
  5.7 0.0 collective-permute-done.1
  5.7 0.0 collective-permute-done.2
  5.7 0.1 broadcast_select_fusion
  5.8 1.0 %collective-permute-start.3 = (bf16[128,1152]{1,0:T(8,128)(2,1)S(1)}, bf16[128,1152]{1,0:T(8,128)(2,1)S(1)}, u32[]{:S(2)}, u32[]{:S(2)}) collective-permute-start(bf16[128,1152]{1,0:T(8,128)(2,1)S(1)} %get-tuple-element.39.refs_7_), channel_id=1, source_target_pairs={{0,3},{1,4},{2,1},{3,6},{4,7},{5,8},{6,5},{7,10},{8,11},{9,12},{10... | collective-permute-start | bytes 884744 | tf_op jit(solution)/shard_map/ppermute | solution.py:237
  6.8 2.3 %collective-permute-done.refs_5_.refs_10_.refs_2_ = bf16[128,1152]{1,0:T(8,128)(2,1)S(1)} collective-permute-done((bf16[128,1152]{1,0:T(8,128)(2,1)S(1)}, bf16[128,1152]{1,0:T(8,128)(2,1)S(1)}, u32[]{:S(2)}, u32[]{:S(2)}) %collective-permute-start) | collective-permute-done | bytes 294944 | tf_op jit(solution)/shard_map/ppermute | solution.py:237
  9.1 2.6 %collective-permute-start.4 = (bf16[128,1152]{1,0:T(8,128)(2,1)S(1)}, bf16[128,1152]{1,0:T(8,128)(2,1)S(1)}, u32[]{:S(2)}, u32[]{:S(2)}) collective-permute-start(bf16[128,1152]{1,0:T(8,128)(2,1)S(1)} %collective-permute-done.refs_5_.refs_10_.refs_2_), channel_id=1, source_target_pairs={{0,1},{1,0},{2,3},{3,2},{4,5},{5,4},{6,7},{7,6},{8,9},{9,8},{10,11... | collective-permute-start | bytes 884744 | tf_op jit(solution)/shard_map/ppermute | solution.py:15
  11.7 1.3 %shard_map.62 = (f32[128,1152]{1,0:T(8,128)S(1)}, f32[128,1152]{1,0:T(8,128)S(1)}) custom-call(f32[1]{0:T(128)S(6)} %copy.10.scale_ref.refs_0_, f32[1]{0:T(128)S(6)} %copy.11.shift_ref.refs_1_, bf16[128,1152]{1,0:T(8,128)(2,1)S(1)} %get-tuple-element.20.refs_2_.refs_6_.refs_1_, bf16[128,1152]{1,0:T(8,128)(2,1)S(1)} %get-tuple-element.23.refs_3_.refs_5_.refs_8_, ...), custom_call_target="tpu_custom_call" | custom-call | flops 301989888 | bytes 2949120 | tf_op jit(solution)/shard_map/pallas_call | solution.py:102
  13.0 0.0 collective-permute-done.3.refs_6_.refs_11_.refs_3_
  13.0 0.0 collective-permute-done.4.refs_6_
  13.1 1.4 %shard_map.63 = (bf16[64,1152]{1,0:T(8,128)(2,1)S(1)}, bf16[64,1152]{1,0:T(8,128)(2,1)S(1)}) custom-call(f32[1]{0:T(128)S(6)} %copy.10.scale_ref.refs_0_, f32[1]{0:T(128)S(6)} %copy.11.shift_ref.refs_1_, bf16[64,1152]{1,0:T(8,128)(2,1)S(1)} %get-tuple-element.41.refs_2_, bf16[128,1152]{1,0:T(8,128)(2,1)S(1)} %get-tuple-element.23.refs_3_.refs_5_.refs_8_, ...), custom_call_target="tpu_custom_call" | custom-call | flops 150994944 | bytes 2949120 | tf_op jit(solution)/shard_map/pallas_call | solution.py:102
  14.5 0.5 %collective-permute-start.5 = (bf16[128,1152]{1,0:T(8,128)(2,1)S(1)}, bf16[128,1152]{1,0:T(8,128)(2,1)S(1)}, u32[]{:S(2)}, u32[]{:S(2)}) collective-permute-start(bf16[128,1152]{1,0:T(8,128)(2,1)S(1)} %collective-permute-done.3.refs_6_.refs_11_.refs_3_), channel_id=1, source_target_pairs={{0,1},{1,0},{2,3},{3,2},{4,5},{5,4},{6,7},{7,6},{8,9},{9,8},{10,11... | collective-permute-start | bytes 884744 | tf_op jit(solution)/shard_map/ppermute | solution.py:15
  15.0 3.1 %collective-permute-start.7 = (bf16[64,1152]{1,0:T(8,128)(2,1)S(1)}, bf16[64,1152]{1,0:T(8,128)(2,1)S(1)}, u32[]{:S(2)}, u32[]{:S(2)}) collective-permute-start(bf16[64,1152]{1,0:T(8,128)(2,1)S(1)} %shard_map.66), channel_id=1, source_target_pairs={{0,2},{1,29},{2,0},{3,31},{4,6},{5,1},{6,4},{7,3},{8,10},{9,5},{10... | collective-permute-start | bytes 442376 | tf_op jit(solution)/shard_map/ppermute | solution.py:237
  18.2 0.3 %collective-permute-start.8 = (bf16[64,1152]{1,0:T(8,128)(2,1)S(1)}, bf16[64,1152]{1,0:T(8,128)(2,1)S(1)}, u32[]{:S(2)}, u32[]{:S(2)}) collective-permute-start(bf16[64,1152]{1,0:T(8,128)(2,1)S(1)} %shard_map.67), channel_id=1, source_target_pairs={{0,2},{1,29},{2,0},{3,31},{4,6},{5,1},{6,4},{7,3},{8,10},{9,5},{10... | collective-permute-start | bytes 442376 | tf_op jit(solution)/shard_map/ppermute | solution.py:237
  18.5 0.0 collective-permute-done.5.refs_7_.refs_2_
  18.5 0.8 %shard_map.65 = bf16[128,1152]{1,0:T(8,128)(2,1)S(1)} custom-call(f32[1]{0:T(128)S(6)} %copy.10.scale_ref.refs_0_, f32[1]{0:T(128)S(6)} %copy.11.shift_ref.refs_1_, bf16[128,1152]{1,0:T(8,128)(2,1)S(1)} %collective-permute-done.5.refs_7_.refs_2_, bf16[128,1152]{1,0:T(8,128)(2,1)S(1)} %get-tuple-element.23.refs_3_.refs_5_.refs_8_, ...), custom_call_target="tpu_custom_call" | custom-call | flops 301989888 | bytes 1769472 | tf_op jit(solution)/shard_map/pallas_call | solution.py:102
  19.4 3.6 %collective-permute-start.6 = (bf16[128,1152]{1,0:T(8,128)(2,1)S(1)}, bf16[128,1152]{1,0:T(8,128)(2,1)S(1)}, u32[]{:S(2)}, u32[]{:S(2)}) collective-permute-start(bf16[128,1152]{1,0:T(8,128)(2,1)S(1)} %shard_map.65), channel_id=1, source_target_pairs={{0,3},{1,28},{2,1},{3,30},{4,7},{5,0},{6,5},{7,2},{8,11},{9,4},{10... | collective-permute-start | bytes 884744 | tf_op jit(solution)/shard_map/ppermute | solution.py:237
  23.0 0.0 collective-permute-done.7
  23.0 0.0 collective-permute-done.8
  23.0 1.3 %shard_map.64 = (f32[128,1152]{1,0:T(8,128)S(1)}, f32[128,1152]{1,0:T(8,128)S(1)}) custom-call(f32[2,128]{1,0:T(2,128)S(1)} %shard_map.61.refs_0_, bf16[128,1152]{1,0:T(8,128)(2,1)S(1)} %get-tuple-element.20.refs_2_.refs_6_.refs_1_, bf16[128,1152]{1,0:T(8,128)(2,1)S(1)} %collective-permute-done.refs_5_.refs_10_.refs_2_, ...), custom_call_target="tpu_custom_call" | custom-call | flops 301989888 | bytes 4128768 | tf_op jit(solution)/shard_map/pallas_call | solution.py:102
  24.3 0.8 %shard_map.68 = (bf16[128,1152]{1,0:T(8,128)(2,1)}, bf16[128,1152]{1,0:T(8,128)(2,1)}) custom-call(f32[128,1152]{1,0:T(8,128)S(1)} %get-tuple-element.33.total_ref, bf16[128,1152]{1,0:T(8,128)(2,1)S(1)} %pad_maximum_fusion.extra_ref), custom_call_target="tpu_custom_call" | custom-call | flops 589824 | bytes 589824 | tf_op jit(solution)/shard_map/pallas_call | solution.py:163
  25.1 1.5 %collective-permute-done.6.extra_ref = bf16[128,1152]{1,0:T(8,128)(2,1)S(1)} collective-permute-done((bf16[128,1152]{1,0:T(8,128)(2,1)S(1)}, bf16[128,1152]{1,0:T(8,128)(2,1)S(1)}, u32[]{:S(2)}, u32[]{:S(2)}) %collective-permute-start.6) | collective-permute-done | bytes 294944 | tf_op jit(solution)/shard_map/ppermute | solution.py:237
  26.6 0.8 %shard_map.69 = (bf16[128,1152]{1,0:T(8,128)(2,1)}, bf16[128,1152]{1,0:T(8,128)(2,1)}) custom-call(f32[128,1152]{1,0:T(8,128)S(1)} %get-tuple-element.32.total_ref, bf16[128,1152]{1,0:T(8,128)(2,1)S(1)} %collective-permute-done.6.extra_ref, bf16[128,1152]{1,0:T(8,128)(2,1)} %get-tuple-element.36.refs_0_, ...), custom_call_target="tpu_custom_call", output_to_operand_aliasing={{0}: (2, {}), {1}: (3, {})} | custom-call | flops 589824 | bytes 589824 | tf_op jit(solution)/shard_map/pallas_call | solution.py:163
  (7 shorter events, 0.1 us)
Async XLA Ops:
  0.6 1.0 %copy-start = (bf16[128,1152]{1,0:T(8,128)(2,1)S(1)}, bf16[128,1152]{1,0:T(8,128)(2,1)}, u32[]{:S(2)}) copy-start(bf16[128,1152]{1,0:T(8,128)(2,1)} %image_ref.1) | copy-start | bytes 884740
  0.6 1.0 %copy-start.1 = (bf16[128,1152]{1,0:T(8,128)(2,1)S(1)}, bf16[128,1152]{1,0:T(8,128)(2,1)}, u32[]{:S(2)}) copy-start(bf16[128,1152]{1,0:T(8,128)(2,1)} %text_ref.1) | copy-start | bytes 884740
  0.6 5.1 %collective-permute-start.1 = (bf16[128,1152]{1,0:T(8,128)(2,1)}, bf16[128,1152]{1,0:T(8,128)(2,1)S(1)}, u32[]{:S(2)}, u32[]{:S(2)}) collective-permute-start(bf16[128,1152]{1,0:T(8,128)(2,1)} %image_ref.1), channel_id=1, source_target_pairs={{0,1},{1,0},{2,3},{3,2},{4,5},{5,4},{6,7},{7,6},{8,9},{9,8},{10,11... | collective-permute-start | bytes 884744 | tf_op jit(solution)/shard_map/ppermute | solution.py:15
  0.8 5.0 %collective-permute-start.2 = (bf16[128,1152]{1,0:T(8,128)(2,1)}, bf16[128,1152]{1,0:T(8,128)(2,1)S(1)}, u32[]{:S(2)}, u32[]{:S(2)}) collective-permute-start(bf16[128,1152]{1,0:T(8,128)(2,1)} %text_ref.1), channel_id=1, source_target_pairs={{0,1},{1,0},{2,3},{3,2},{4,5},{5,4},{6,7},{7,6},{8,9},{9,8},{10,11... | collective-permute-start | bytes 884744 | tf_op jit(solution)/shard_map/ppermute | solution.py:15
  1.7 7.4 %collective-permute-start = (bf16[128,1152]{1,0:T(8,128)(2,1)S(1)}, bf16[128,1152]{1,0:T(8,128)(2,1)S(1)}, u32[]{:S(2)}, u32[]{:S(2)}) collective-permute-start(bf16[128,1152]{1,0:T(8,128)(2,1)S(1)} %get-tuple-element.20.refs_2_.refs_6_.refs_1_), channel_id=1, source_target_pairs={{0,3},{1,4},{2,1},{3,6},{4,7},{5,8},{6,5},{7,10},{8,11},{9,12},{10... | collective-permute-start | bytes 884744 | tf_op jit(solution)/shard_map/ppermute | solution.py:237
  5.8 7.2 %collective-permute-start.3 = (bf16[128,1152]{1,0:T(8,128)(2,1)S(1)}, bf16[128,1152]{1,0:T(8,128)(2,1)S(1)}, u32[]{:S(2)}, u32[]{:S(2)}) collective-permute-start(bf16[128,1152]{1,0:T(8,128)(2,1)S(1)} %get-tuple-element.39.refs_7_), channel_id=1, source_target_pairs={{0,3},{1,4},{2,1},{3,6},{4,7},{5,8},{6,5},{7,10},{8,11},{9,12},{10... | collective-permute-start | bytes 884744 | tf_op jit(solution)/shard_map/ppermute | solution.py:237
  9.1 3.9 %collective-permute-start.4 = (bf16[128,1152]{1,0:T(8,128)(2,1)S(1)}, bf16[128,1152]{1,0:T(8,128)(2,1)S(1)}, u32[]{:S(2)}, u32[]{:S(2)}) collective-permute-start(bf16[128,1152]{1,0:T(8,128)(2,1)S(1)} %collective-permute-done.refs_5_.refs_10_.refs_2_), channel_id=1, source_target_pairs={{0,1},{1,0},{2,3},{3,2},{4,5},{5,4},{6,7},{7,6},{8,9},{9,8},{10,11... | collective-permute-start | bytes 884744 | tf_op jit(solution)/shard_map/ppermute | solution.py:15
  14.5 4.0 %collective-permute-start.5 = (bf16[128,1152]{1,0:T(8,128)(2,1)S(1)}, bf16[128,1152]{1,0:T(8,128)(2,1)S(1)}, u32[]{:S(2)}, u32[]{:S(2)}) collective-permute-start(bf16[128,1152]{1,0:T(8,128)(2,1)S(1)} %collective-permute-done.3.refs_6_.refs_11_.refs_3_), channel_id=1, source_target_pairs={{0,1},{1,0},{2,3},{3,2},{4,5},{5,4},{6,7},{7,6},{8,9},{9,8},{10,11... | collective-permute-start | bytes 884744 | tf_op jit(solution)/shard_map/ppermute | solution.py:15
  15.0 8.0 %collective-permute-start.7 = (bf16[64,1152]{1,0:T(8,128)(2,1)S(1)}, bf16[64,1152]{1,0:T(8,128)(2,1)S(1)}, u32[]{:S(2)}, u32[]{:S(2)}) collective-permute-start(bf16[64,1152]{1,0:T(8,128)(2,1)S(1)} %shard_map.66), channel_id=1, source_target_pairs={{0,2},{1,29},{2,0},{3,31},{4,6},{5,1},{6,4},{7,3},{8,10},{9,5},{10... | collective-permute-start | bytes 442376 | tf_op jit(solution)/shard_map/ppermute | solution.py:237
  18.2 4.8 %collective-permute-start.8 = (bf16[64,1152]{1,0:T(8,128)(2,1)S(1)}, bf16[64,1152]{1,0:T(8,128)(2,1)S(1)}, u32[]{:S(2)}, u32[]{:S(2)}) collective-permute-start(bf16[64,1152]{1,0:T(8,128)(2,1)S(1)} %shard_map.67), channel_id=1, source_target_pairs={{0,2},{1,29},{2,0},{3,31},{4,6},{5,1},{6,4},{7,3},{8,10},{9,5},{10... | collective-permute-start | bytes 442376 | tf_op jit(solution)/shard_map/ppermute | solution.py:237
  19.4 7.3 %collective-permute-start.6 = (bf16[128,1152]{1,0:T(8,128)(2,1)S(1)}, bf16[128,1152]{1,0:T(8,128)(2,1)S(1)}, u32[]{:S(2)}, u32[]{:S(2)}) collective-permute-start(bf16[128,1152]{1,0:T(8,128)(2,1)S(1)} %shard_map.65), channel_id=1, source_target_pairs={{0,3},{1,28},{2,1},{3,30},{4,7},{5,0},{6,5},{7,2},{8,11},{9,4},{10... | collective-permute-start | bytes 884744 | tf_op jit(solution)/shard_map/ppermute | solution.py:237

commit v8 on v5

--- a/solution.py
+++ b/solution.py
@@ -137,7 +137,7 @@
 
 def placed(total, extra, kept, texts_on):
     shape, dtype = total.shape, jnp.bfloat16
-    pieces = 2
+    pieces = 4
     rows = shape[0] // pieces
 
     def kernel(total_ref, extra_ref, *refs):

time: 26 us -> 26 us (level)
  no operation moved by 1% of the time
where the time goes in v8:
time: 26 us; the launch traced here: 25.8 us
  waiting for transfers between devices  9.08 us (35%)
  starting transfers between devices  8.33 us (32%)
  Pallas kernels  5.85 us (22%)
  between operations  2.03 us (8%)
  local copies, waits for them, and re-layouts  0.44 us (2%)
    ppermute x4, waiting for transfers between devices, sent(): return lax.ppermute(array, ('grp', 'in'), pairs)  9.07 us
    ppermute x4, starting transfers between devices, sent(): return lax.ppermute(array, ('grp', 'in'), pairs)  7.73 us
    pallas_call x5, Pallas kernels, pulled(): pl.pallas_call(kernel, out_shape=[jax.ShapeDtypeStruct((height, width), t...  4.29 us
    pallas_call x2, Pallas kernels, placed(): pl.pallas_call(kernel, out_shape=[jax.ShapeDtypeStruct(shape, dtype)] * 2...  1.51 us
    ppermute x4, starting transfers between devices, moved(): lax.ppermute(array, axis, [(i, target(i) % peers) for i in range(peers)])  0.6 us
  transfers between devices with their start and end apart: 8, of which 4 were waited for; matrix products, arithmetic and copies ran while one was open for 0% of the time, Pallas kernels for 20%

profile of v8, /device:TPU:0, one launch (start us, length us, event | category | flops | bytes accessed | tf_op | source)
XLA Modules:
  0.0 25.8 jit_solution(3470837390052897597)
XLA Ops:
  0.6 0.0 copy-start
  0.6 0.0 copy-start.1
  0.6 0.5 %collective-permute-start.1 = (bf16[128,1152]{1,0:T(8,128)(2,1)}, bf16[128,1152]{1,0:T(8,128)(2,1)S(1)}, u32[]{:S(2)}, u32[]{:S(2)}) collective-permute-start(bf16[128,1152]{1,0:T(8,128)(2,1)} %image_ref.1), channel_id=1, source_target_pairs={{0,1},{1,0},{2,3},{3,2},{4,5},{5,4},{6,7},{7,6},{8,9},{9,8},{10,11... | collective-permute-start | bytes 884744 | tf_op jit(solution)/shard_map/ppermute | solution.py:15
  1.2 0.1 collective-permute-start.2
  1.2 0.3 %copy-done = bf16[128,1152]{1,0:T(8,128)(2,1)S(1)} copy-done((bf16[128,1152]{1,0:T(8,128)(2,1)S(1)}, bf16[128,1152]{1,0:T(8,128)(2,1)}, u32[]{:S(2)}) %copy-start) | copy-done | bytes 294936
  1.6 0.1 copy-done.1
  1.7 2.4 %collective-permute-start = (bf16[128,1152]{1,0:T(8,128)(2,1)S(1)}, bf16[128,1152]{1,0:T(8,128)(2,1)S(1)}, u32[]{:S(2)}, u32[]{:S(2)}) collective-permute-start(bf16[128,1152]{1,0:T(8,128)(2,1)S(1)} %get-tuple-element.17.refs_2_.refs_6_.refs_1_), channel_id=1, source_target_pairs={{0,3},{1,4},{2,1},{3,6},{4,7},{5,8},{6,5},{7,10},{8,11},{9,12},{10... | collective-permute-start | bytes 884744 | tf_op jit(solution)/shard_map/ppermute | solution.py:237
  5.5 0.0 collective-permute-done.1
  5.5 0.0 collective-permute-done.2
  5.5 0.1 broadcast_select_fusion
  5.6 1.9 %collective-permute-start.3 = (bf16[128,1152]{1,0:T(8,128)(2,1)S(1)}, bf16[128,1152]{1,0:T(8,128)(2,1)S(1)}, u32[]{:S(2)}, u32[]{:S(2)}) collective-permute-start(bf16[128,1152]{1,0:T(8,128)(2,1)S(1)} %get-tuple-element.33.refs_7_), channel_id=1, source_target_pairs={{0,3},{1,4},{2,1},{3,6},{4,7},{5,8},{6,5},{7,10},{8,11},{9,12},{10... | collective-permute-start | bytes 884744 | tf_op jit(solution)/shard_map/ppermute | solution.py:237
  7.4 4.2 %collective-permute-done.refs_5_.refs_2_ = bf16[128,1152]{1,0:T(8,128)(2,1)S(1)} collective-permute-done((bf16[128,1152]{1,0:T(8,128)(2,1)S(1)}, bf16[128,1152]{1,0:T(8,128)(2,1)S(1)}, u32[]{:S(2)}, u32[]{:S(2)}) %collective-permute-start) | collective-permute-done | bytes 294944 | tf_op jit(solution)/shard_map/ppermute | solution.py:237
  11.6 0.0 collective-permute-start.4
  11.6 1.3 %shard_map.62 = (f32[128,1152]{1,0:T(8,128)S(1)}, f32[128,1152]{1,0:T(8,128)S(1)}) custom-call(f32[1]{0:T(128)S(6)} %copy.10.scale_ref.refs_0_, f32[1]{0:T(128)S(6)} %copy.11.shift_ref.refs_1_, bf16[128,1152]{1,0:T(8,128)(2,1)S(1)} %get-tuple-element.17.refs_2_.refs_6_.refs_1_, bf16[128,1152]{1,0:T(8,128)(2,1)S(1)} %get-tuple-element.20.refs_3_.refs_5_, ...), custom_call_target="tpu_custom_call" | custom-call | flops 301989888 | bytes 2949120 | tf_op jit(solution)/shard_map/pallas_call | solution.py:102
  12.9 1.8 %collective-permute-done.3.refs_6_.refs_3_ = bf16[128,1152]{1,0:T(8,128)(2,1)S(1)} collective-permute-done((bf16[128,1152]{1,0:T(8,128)(2,1)S(1)}, bf16[128,1152]{1,0:T(8,128)(2,1)S(1)}, u32[]{:S(2)}, u32[]{:S(2)}) %collective-permute-start.3) | collective-permute-done | bytes 294944 | tf_op jit(solution)/shard_map/ppermute | solution.py:237
  14.8 0.0 collective-permute-done.4.refs_2_.refs_6_
  14.8 0.0 collective-permute-start.5
  14.8 0.8 %shard_map.66 = bf16[128,1152]{1,0:T(8,128)(2,1)S(1)} custom-call(f32[1]{0:T(128)S(6)} %copy.10.scale_ref.refs_0_, f32[1]{0:T(128)S(6)} %copy.11.shift_ref.refs_1_, bf16[128,1152]{1,0:T(8,128)(2,1)S(1)} %collective-permute-done.4.refs_2_.refs_6_, bf16[128,1152]{1,0:T(8,128)(2,1)S(1)} %get-tuple-element.20.refs_3_.refs_5_, ...), custom_call_target="tpu_custom_call" | custom-call | flops 301989888 | bytes 1769472 | tf_op jit(solution)/shard_map/pallas_call | solution.py:102
  15.7 2.0 %collective-permute-start.7 = (bf16[128,1152]{1,0:T(8,128)(2,1)S(1)}, bf16[128,1152]{1,0:T(8,128)(2,1)S(1)}, u32[]{:S(2)}, u32[]{:S(2)}) collective-permute-start(bf16[128,1152]{1,0:T(8,128)(2,1)S(1)} %shard_map.66), channel_id=1, source_target_pairs={{0,2},{1,29},{2,0},{3,31},{4,6},{5,1},{6,4},{7,3},{8,10},{9,5},{10... | collective-permute-start | bytes 884744 | tf_op jit(solution)/shard_map/ppermute | solution.py:237
  17.6 0.0 collective-permute-done.5.refs_7_.refs_2_
  17.6 0.8 %shard_map.65 = bf16[128,1152]{1,0:T(8,128)(2,1)S(1)} custom-call(f32[1]{0:T(128)S(6)} %copy.10.scale_ref.refs_0_, f32[1]{0:T(128)S(6)} %copy.11.shift_ref.refs_1_, bf16[128,1152]{1,0:T(8,128)(2,1)S(1)} %collective-permute-done.5.refs_7_.refs_2_, bf16[128,1152]{1,0:T(8,128)(2,1)S(1)} %get-tuple-element.20.refs_3_.refs_5_, ...), custom_call_target="tpu_custom_call" | custom-call | flops 301989888 | bytes 1769472 | tf_op jit(solution)/shard_map/pallas_call | solution.py:102
  18.5 1.5 %collective-permute-start.6 = (bf16[128,1152]{1,0:T(8,128)(2,1)S(1)}, bf16[128,1152]{1,0:T(8,128)(2,1)S(1)}, u32[]{:S(2)}, u32[]{:S(2)}) collective-permute-start(bf16[128,1152]{1,0:T(8,128)(2,1)S(1)} %shard_map.65), channel_id=1, source_target_pairs={{0,3},{1,28},{2,1},{3,30},{4,7},{5,0},{6,5},{7,2},{8,11},{9,4},{10... | collective-permute-start | bytes 884744 | tf_op jit(solution)/shard_map/ppermute | solution.py:237
  20.0 1.3 %shard_map.64 = (f32[128,1152]{1,0:T(8,128)S(1)}, f32[128,1152]{1,0:T(8,128)S(1)}) custom-call(f32[2,128]{1,0:T(2,128)S(1)} %shard_map.61.refs_0_, bf16[128,1152]{1,0:T(8,128)(2,1)S(1)} %get-tuple-element.17.refs_2_.refs_6_.refs_1_, bf16[128,1152]{1,0:T(8,128)(2,1)S(1)} %collective-permute-done.refs_5_.refs_2_, ...), custom_call_target="tpu_custom_call" | custom-call | flops 301989888 | bytes 4128768 | tf_op jit(solution)/shard_map/pallas_call | solution.py:102
  21.3 1.2 %collective-permute-done.7.extra_ref = bf16[128,1152]{1,0:T(8,128)(2,1)S(1)} collective-permute-done((bf16[128,1152]{1,0:T(8,128)(2,1)S(1)}, bf16[128,1152]{1,0:T(8,128)(2,1)S(1)}, u32[]{:S(2)}, u32[]{:S(2)}) %collective-permute-start.7) | collective-permute-done | bytes 294944 | tf_op jit(solution)/shard_map/ppermute | solution.py:237
  22.4 0.8 %shard_map.67 = (bf16[128,1152]{1,0:T(8,128)(2,1)}, bf16[128,1152]{1,0:T(8,128)(2,1)}) custom-call(f32[128,1152]{1,0:T(8,128)S(1)} %get-tuple-element.28.total_ref, bf16[128,1152]{1,0:T(8,128)(2,1)S(1)} %collective-permute-done.7.extra_ref), custom_call_target="tpu_custom_call" | custom-call | flops 589824 | bytes 589824 | tf_op jit(solution)/shard_map/pallas_call | solution.py:163
  23.2 1.9 %collective-permute-done.6.extra_ref = bf16[128,1152]{1,0:T(8,128)(2,1)S(1)} collective-permute-done((bf16[128,1152]{1,0:T(8,128)(2,1)S(1)}, bf16[128,1152]{1,0:T(8,128)(2,1)S(1)}, u32[]{:S(2)}, u32[]{:S(2)}) %collective-permute-start.6) | collective-permute-done | bytes 294944 | tf_op jit(solution)/shard_map/ppermute | solution.py:237
  25.0 0.8 %shard_map.68 = (bf16[128,1152]{1,0:T(8,128)(2,1)}, bf16[128,1152]{1,0:T(8,128)(2,1)}) custom-call(f32[128,1152]{1,0:T(8,128)S(1)} %get-tuple-element.27.total_ref, bf16[128,1152]{1,0:T(8,128)(2,1)S(1)} %collective-permute-done.6.extra_ref, bf16[128,1152]{1,0:T(8,128)(2,1)} %get-tuple-element.30.refs_0_, ...), custom_call_target="tpu_custom_call", output_to_operand_aliasing={{0}: (2, {}), {1}: (3, {})} | custom-call | flops 589824 | bytes 589824 | tf_op jit(solution)/shard_map/pallas_call | solution.py:163
  (4 shorter events, 0.0 us)
Async XLA Ops:
  0.6 1.0 %copy-start = (bf16[128,1152]{1,0:T(8,128)(2,1)S(1)}, bf16[128,1152]{1,0:T(8,128)(2,1)}, u32[]{:S(2)}) copy-start(bf16[128,1152]{1,0:T(8,128)(2,1)} %image_ref.1) | copy-start | bytes 884740
  0.6 1.0 %copy-start.1 = (bf16[128,1152]{1,0:T(8,128)(2,1)S(1)}, bf16[128,1152]{1,0:T(8,128)(2,1)}, u32[]{:S(2)}) copy-start(bf16[128,1152]{1,0:T(8,128)(2,1)} %text_ref.1) | copy-start | bytes 884740
  0.6 4.8 %collective-permute-start.1 = (bf16[128,1152]{1,0:T(8,128)(2,1)}, bf16[128,1152]{1,0:T(8,128)(2,1)S(1)}, u32[]{:S(2)}, u32[]{:S(2)}) collective-permute-start(bf16[128,1152]{1,0:T(8,128)(2,1)} %image_ref.1), channel_id=1, source_target_pairs={{0,1},{1,0},{2,3},{3,2},{4,5},{5,4},{6,7},{7,6},{8,9},{9,8},{10,11... | collective-permute-start | bytes 884744 | tf_op jit(solution)/shard_map/ppermute | solution.py:15
  1.2 4.3 %collective-permute-start.2 = (bf16[128,1152]{1,0:T(8,128)(2,1)}, bf16[128,1152]{1,0:T(8,128)(2,1)S(1)}, u32[]{:S(2)}, u32[]{:S(2)}) collective-permute-start(bf16[128,1152]{1,0:T(8,128)(2,1)} %text_ref.1), channel_id=1, source_target_pairs={{0,1},{1,0},{2,3},{3,2},{4,5},{5,4},{6,7},{7,6},{8,9},{9,8},{10,11... | collective-permute-start | bytes 884744 | tf_op jit(solution)/shard_map/ppermute | solution.py:15
  1.7 9.9 %collective-permute-start = (bf16[128,1152]{1,0:T(8,128)(2,1)S(1)}, bf16[128,1152]{1,0:T(8,128)(2,1)S(1)}, u32[]{:S(2)}, u32[]{:S(2)}) collective-permute-start(bf16[128,1152]{1,0:T(8,128)(2,1)S(1)} %get-tuple-element.17.refs_2_.refs_6_.refs_1_), channel_id=1, source_target_pairs={{0,3},{1,4},{2,1},{3,6},{4,7},{5,8},{6,5},{7,10},{8,11},{9,12},{10... | collective-permute-start | bytes 884744 | tf_op jit(solution)/shard_map/ppermute | solution.py:237
  5.6 9.2 %collective-permute-start.3 = (bf16[128,1152]{1,0:T(8,128)(2,1)S(1)}, bf16[128,1152]{1,0:T(8,128)(2,1)S(1)}, u32[]{:S(2)}, u32[]{:S(2)}) collective-permute-start(bf16[128,1152]{1,0:T(8,128)(2,1)S(1)} %get-tuple-element.33.refs_7_), channel_id=1, source_target_pairs={{0,3},{1,4},{2,1},{3,6},{4,7},{5,8},{6,5},{7,10},{8,11},{9,12},{10... | collective-permute-start | bytes 884744 | tf_op jit(solution)/shard_map/ppermute | solution.py:237
  11.6 3.2 %collective-permute-start.4 = (bf16[128,1152]{1,0:T(8,128)(2,1)S(1)}, bf16[128,1152]{1,0:T(8,128)(2,1)S(1)}, u32[]{:S(2)}, u32[]{:S(2)}) collective-permute-start(bf16[128,1152]{1,0:T(8,128)(2,1)S(1)} %collective-permute-done.refs_5_.refs_2_), channel_id=1, source_target_pairs={{0,1},{1,0},{2,3},{3,2},{4,5},{5,4},{6,7},{7,6},{8,9},{9,8},{10,11... | collective-permute-start | bytes 884744 | tf_op jit(solution)/shard_map/ppermute | solution.py:15
  14.8 2.8 %collective-permute-start.5 = (bf16[128,1152]{1,0:T(8,128)(2,1)S(1)}, bf16[128,1152]{1,0:T(8,128)(2,1)S(1)}, u32[]{:S(2)}, u32[]{:S(2)}) collective-permute-start(bf16[128,1152]{1,0:T(8,128)(2,1)S(1)} %collective-permute-done.3.refs_6_.refs_3_), channel_id=1, source_target_pairs={{0,1},{1,0},{2,3},{3,2},{4,5},{5,4},{6,7},{7,6},{8,9},{9,8},{10,11... | collective-permute-start | bytes 884744 | tf_op jit(solution)/shard_map/ppermute | solution.py:15
  15.7 6.8 %collective-permute-start.7 = (bf16[128,1152]{1,0:T(8,128)(2,1)S(1)}, bf16[128,1152]{1,0:T(8,128)(2,1)S(1)}, u32[]{:S(2)}, u32[]{:S(2)}) collective-permute-start(bf16[128,1152]{1,0:T(8,128)(2,1)S(1)} %shard_map.66), channel_id=1, source_target_pairs={{0,2},{1,29},{2,0},{3,31},{4,6},{5,1},{6,4},{7,3},{8,10},{9,5},{10... | collective-permute-start | bytes 884744 | tf_op jit(solution)/shard_map/ppermute | solution.py:237
  18.5 6.6 %collective-permute-start.6 = (bf16[128,1152]{1,0:T(8,128)(2,1)S(1)}, bf16[128,1152]{1,0:T(8,128)(2,1)S(1)}, u32[]{:S(2)}, u32[]{:S(2)}) collective-permute-start(bf16[128,1152]{1,0:T(8,128)(2,1)S(1)} %shard_map.65), channel_id=1, source_target_pairs={{0,3},{1,28},{2,1},{3,30},{4,7},{5,0},{6,5},{7,2},{8,11},{9,4},{10... | collective-permute-start | bytes 884744 | tf_op jit(solution)/shard_map/ppermute | solution.py:237

commit v9 on v8

--- a/solution.py
+++ b/solution.py
@@ -137,7 +137,7 @@
 
 def placed(total, extra, kept, texts_on):
     shape, dtype = total.shape, jnp.bfloat16
-    pieces = 4
+    pieces = 1
     rows = shape[0] // pieces
 
     def kernel(total_ref, extra_ref, *refs):

time: 26 us -> 26 us (level)
  no operation moved by 1% of the time
where the time goes in v9:
time: 26 us; the launch traced here: 25.8 us
  waiting for transfers between devices  9.07 us (35%)
  starting transfers between devices  8.33 us (32%)
  Pallas kernels  5.89 us (23%)
  between operations  2.03 us (8%)
  local copies, waits for them, and re-layouts  0.44 us (2%)
    ppermute x4, waiting for transfers between devices, sent(): return lax.ppermute(array, ('grp', 'in'), pairs)  9.05 us
    ppermute x4, starting transfers between devices, sent(): return lax.ppermute(array, ('grp', 'in'), pairs)  7.73 us
    pallas_call x5, Pallas kernels, pulled(): pl.pallas_call(kernel, out_shape=[jax.ShapeDtypeStruct((height, width), t...  4.29 us
    pallas_call x2, Pallas kernels, placed(): pl.pallas_call(kernel, out_shape=[jax.ShapeDtypeStruct(shape, dtype)] * 2...  1.55 us
    ppermute x4, starting transfers between devices, moved(): lax.ppermute(array, axis, [(i, target(i) % peers) for i in range(peers)])  0.6 us
  transfers between devices with their start and end apart: 8, of which 4 were waited for; matrix products, arithmetic and copies ran while one was open for 0% of the time, Pallas kernels for 20%

profile of v9, /device:TPU:0, one launch (start us, length us, event | category | flops | bytes accessed | tf_op | source)
XLA Modules:
  0.0 25.8 jit_solution(13051272836236036902)
XLA Ops:
  0.6 0.0 copy-start
  0.6 0.0 copy-start.1
  0.6 0.5 %collective-permute-start.1 = (bf16[128,1152]{1,0:T(8,128)(2,1)}, bf16[128,1152]{1,0:T(8,128)(2,1)S(1)}, u32[]{:S(2)}, u32[]{:S(2)}) collective-permute-start(bf16[128,1152]{1,0:T(8,128)(2,1)} %image_ref.1), channel_id=1, source_target_pairs={{0,1},{1,0},{2,3},{3,2},{4,5},{5,4},{6,7},{7,6},{8,9},{9,8},{10,11... | collective-permute-start | bytes 884744 | tf_op jit(solution)/shard_map/ppermute | solution.py:15
  1.2 0.1 collective-permute-start.2
  1.2 0.3 %copy-done = bf16[128,1152]{1,0:T(8,128)(2,1)S(1)} copy-done((bf16[128,1152]{1,0:T(8,128)(2,1)S(1)}, bf16[128,1152]{1,0:T(8,128)(2,1)}, u32[]{:S(2)}) %copy-start) | copy-done | bytes 294936
  1.6 0.1 copy-done.1
  1.7 2.4 %collective-permute-start = (bf16[128,1152]{1,0:T(8,128)(2,1)S(1)}, bf16[128,1152]{1,0:T(8,128)(2,1)S(1)}, u32[]{:S(2)}, u32[]{:S(2)}) collective-permute-start(bf16[128,1152]{1,0:T(8,128)(2,1)S(1)} %get-tuple-element.17.refs_2_.refs_6_.refs_1_), channel_id=1, source_target_pairs={{0,3},{1,4},{2,1},{3,6},{4,7},{5,8},{6,5},{7,10},{8,11},{9,12},{10... | collective-permute-start | bytes 884744 | tf_op jit(solution)/shard_map/ppermute | solution.py:237
  5.5 0.0 collective-permute-done.1
  5.5 0.0 collective-permute-done.2
  5.5 0.1 broadcast_select_fusion
  5.6 1.9 %collective-permute-start.3 = (bf16[128,1152]{1,0:T(8,128)(2,1)S(1)}, bf16[128,1152]{1,0:T(8,128)(2,1)S(1)}, u32[]{:S(2)}, u32[]{:S(2)}) collective-permute-start(bf16[128,1152]{1,0:T(8,128)(2,1)S(1)} %get-tuple-element.33.refs_7_), channel_id=1, source_target_pairs={{0,3},{1,4},{2,1},{3,6},{4,7},{5,8},{6,5},{7,10},{8,11},{9,12},{10... | collective-permute-start | bytes 884744 | tf_op jit(solution)/shard_map/ppermute | solution.py:237
  7.4 4.2 %collective-permute-done.refs_5_.refs_2_ = bf16[128,1152]{1,0:T(8,128)(2,1)S(1)} collective-permute-done((bf16[128,1152]{1,0:T(8,128)(2,1)S(1)}, bf16[128,1152]{1,0:T(8,128)(2,1)S(1)}, u32[]{:S(2)}, u32[]{:S(2)}) %collective-permute-start) | collective-permute-done | bytes 294944 | tf_op jit(solution)/shard_map/ppermute | solution.py:237
  11.6 0.0 collective-permute-start.4
  11.6 1.3 %shard_map.62 = (f32[128,1152]{1,0:T(8,128)S(1)}, f32[128,1152]{1,0:T(8,128)S(1)}) custom-call(f32[1]{0:T(128)S(6)} %copy.10.scale_ref.refs_0_, f32[1]{0:T(128)S(6)} %copy.11.shift_ref.refs_1_, bf16[128,1152]{1,0:T(8,128)(2,1)S(1)} %get-tuple-element.17.refs_2_.refs_6_.refs_1_, bf16[128,1152]{1,0:T(8,128)(2,1)S(1)} %get-tuple-element.20.refs_3_.refs_5_, ...), custom_call_target="tpu_custom_call" | custom-call | flops 301989888 | bytes 2949120 | tf_op jit(solution)/shard_map/pallas_call | solution.py:102
  12.9 1.8 %collective-permute-done.3.refs_6_.refs_3_ = bf16[128,1152]{1,0:T(8,128)(2,1)S(1)} collective-permute-done((bf16[128,1152]{1,0:T(8,128)(2,1)S(1)}, bf16[128,1152]{1,0:T(8,128)(2,1)S(1)}, u32[]{:S(2)}, u32[]{:S(2)}) %collective-permute-start.3) | collective-permute-done | bytes 294944 | tf_op jit(solution)/shard_map/ppermute | solution.py:237
  14.8 0.0 collective-permute-done.4.refs_2_.refs_6_
  14.8 0.0 collective-permute-start.5
  14.8 0.8 %shard_map.66 = bf16[128,1152]{1,0:T(8,128)(2,1)S(1)} custom-call(f32[1]{0:T(128)S(6)} %copy.10.scale_ref.refs_0_, f32[1]{0:T(128)S(6)} %copy.11.shift_ref.refs_1_, bf16[128,1152]{1,0:T(8,128)(2,1)S(1)} %collective-permute-done.4.refs_2_.refs_6_, bf16[128,1152]{1,0:T(8,128)(2,1)S(1)} %get-tuple-element.20.refs_3_.refs_5_, ...), custom_call_target="tpu_custom_call" | custom-call | flops 301989888 | bytes 1769472 | tf_op jit(solution)/shard_map/pallas_call | solution.py:102
  15.7 2.0 %collective-permute-start.7 = (bf16[128,1152]{1,0:T(8,128)(2,1)S(1)}, bf16[128,1152]{1,0:T(8,128)(2,1)S(1)}, u32[]{:S(2)}, u32[]{:S(2)}) collective-permute-start(bf16[128,1152]{1,0:T(8,128)(2,1)S(1)} %shard_map.66), channel_id=1, source_target_pairs={{0,2},{1,29},{2,0},{3,31},{4,6},{5,1},{6,4},{7,3},{8,10},{9,5},{10... | collective-permute-start | bytes 884744 | tf_op jit(solution)/shard_map/ppermute | solution.py:237
  17.6 0.0 collective-permute-done.5.refs_7_.refs_2_
  17.6 0.8 %shard_map.65 = bf16[128,1152]{1,0:T(8,128)(2,1)S(1)} custom-call(f32[1]{0:T(128)S(6)} %copy.10.scale_ref.refs_0_, f32[1]{0:T(128)S(6)} %copy.11.shift_ref.refs_1_, bf16[128,1152]{1,0:T(8,128)(2,1)S(1)} %collective-permute-done.5.refs_7_.refs_2_, bf16[128,1152]{1,0:T(8,128)(2,1)S(1)} %get-tuple-element.20.refs_3_.refs_5_, ...), custom_call_target="tpu_custom_call" | custom-call | flops 301989888 | bytes 1769472 | tf_op jit(solution)/shard_map/pallas_call | solution.py:102
  18.5 1.5 %collective-permute-start.6 = (bf16[128,1152]{1,0:T(8,128)(2,1)S(1)}, bf16[128,1152]{1,0:T(8,128)(2,1)S(1)}, u32[]{:S(2)}, u32[]{:S(2)}) collective-permute-start(bf16[128,1152]{1,0:T(8,128)(2,1)S(1)} %shard_map.65), channel_id=1, source_target_pairs={{0,3},{1,28},{2,1},{3,30},{4,7},{5,0},{6,5},{7,2},{8,11},{9,4},{10... | collective-permute-start | bytes 884744 | tf_op jit(solution)/shard_map/ppermute | solution.py:237
  20.0 1.3 %shard_map.64 = (f32[128,1152]{1,0:T(8,128)S(1)}, f32[128,1152]{1,0:T(8,128)S(1)}) custom-call(f32[2,128]{1,0:T(2,128)S(1)} %shard_map.61.refs_0_, bf16[128,1152]{1,0:T(8,128)(2,1)S(1)} %get-tuple-element.17.refs_2_.refs_6_.refs_1_, bf16[128,1152]{1,0:T(8,128)(2,1)S(1)} %collective-permute-done.refs_5_.refs_2_, ...), custom_call_target="tpu_custom_call" | custom-call | flops 301989888 | bytes 4128768 | tf_op jit(solution)/shard_map/pallas_call | solution.py:102
  21.3 1.2 %collective-permute-done.7.extra_ref = bf16[128,1152]{1,0:T(8,128)(2,1)S(1)} collective-permute-done((bf16[128,1152]{1,0:T(8,128)(2,1)S(1)}, bf16[128,1152]{1,0:T(8,128)(2,1)S(1)}, u32[]{:S(2)}, u32[]{:S(2)}) %collective-permute-start.7) | collective-permute-done | bytes 294944 | tf_op jit(solution)/shard_map/ppermute | solution.py:237
  22.4 0.8 %shard_map.67 = (bf16[128,1152]{1,0:T(8,128)(2,1)}, bf16[128,1152]{1,0:T(8,128)(2,1)}) custom-call(f32[128,1152]{1,0:T(8,128)S(1)} %get-tuple-element.28.total_ref, bf16[128,1152]{1,0:T(8,128)(2,1)S(1)} %collective-permute-done.7.extra_ref), custom_call_target="tpu_custom_call" | custom-call | flops 589824 | bytes 589824 | tf_op jit(solution)/shard_map/pallas_call | solution.py:163
  23.2 1.8 %collective-permute-done.6.extra_ref = bf16[128,1152]{1,0:T(8,128)(2,1)S(1)} collective-permute-done((bf16[128,1152]{1,0:T(8,128)(2,1)S(1)}, bf16[128,1152]{1,0:T(8,128)(2,1)S(1)}, u32[]{:S(2)}, u32[]{:S(2)}) %collective-permute-start.6) | collective-permute-done | bytes 294944 | tf_op jit(solution)/shard_map/ppermute | solution.py:237
  25.0 0.8 %shard_map.68 = (bf16[128,1152]{1,0:T(8,128)(2,1)}, bf16[128,1152]{1,0:T(8,128)(2,1)}) custom-call(f32[128,1152]{1,0:T(8,128)S(1)} %get-tuple-element.27.total_ref, bf16[128,1152]{1,0:T(8,128)(2,1)S(1)} %collective-permute-done.6.extra_ref, bf16[128,1152]{1,0:T(8,128)(2,1)} %get-tuple-element.30.refs_0_, ...), custom_call_target="tpu_custom_call", output_to_operand_aliasing={{0}: (2, {}), {1}: (3, {})} | custom-call | flops 589824 | bytes 589824 | tf_op jit(solution)/shard_map/pallas_call | solution.py:163
  (4 shorter events, 0.0 us)
Async XLA Ops:
  0.6 1.0 %copy-start = (bf16[128,1152]{1,0:T(8,128)(2,1)S(1)}, bf16[128,1152]{1,0:T(8,128)(2,1)}, u32[]{:S(2)}) copy-start(bf16[128,1152]{1,0:T(8,128)(2,1)} %image_ref.1) | copy-start | bytes 884740
  0.6 1.0 %copy-start.1 = (bf16[128,1152]{1,0:T(8,128)(2,1)S(1)}, bf16[128,1152]{1,0:T(8,128)(2,1)}, u32[]{:S(2)}) copy-start(bf16[128,1152]{1,0:T(8,128)(2,1)} %text_ref.1) | copy-start | bytes 884740
  0.6 4.8 %collective-permute-start.1 = (bf16[128,1152]{1,0:T(8,128)(2,1)}, bf16[128,1152]{1,0:T(8,128)(2,1)S(1)}, u32[]{:S(2)}, u32[]{:S(2)}) collective-permute-start(bf16[128,1152]{1,0:T(8,128)(2,1)} %image_ref.1), channel_id=1, source_target_pairs={{0,1},{1,0},{2,3},{3,2},{4,5},{5,4},{6,7},{7,6},{8,9},{9,8},{10,11... | collective-permute-start | bytes 884744 | tf_op jit(solution)/shard_map/ppermute | solution.py:15
  1.2 4.3 %collective-permute-start.2 = (bf16[128,1152]{1,0:T(8,128)(2,1)}, bf16[128,1152]{1,0:T(8,128)(2,1)S(1)}, u32[]{:S(2)}, u32[]{:S(2)}) collective-permute-start(bf16[128,1152]{1,0:T(8,128)(2,1)} %text_ref.1), channel_id=1, source_target_pairs={{0,1},{1,0},{2,3},{3,2},{4,5},{5,4},{6,7},{7,6},{8,9},{9,8},{10,11... | collective-permute-start | bytes 884744 | tf_op jit(solution)/shard_map/ppermute | solution.py:15
  1.7 9.9 %collective-permute-start = (bf16[128,1152]{1,0:T(8,128)(2,1)S(1)}, bf16[128,1152]{1,0:T(8,128)(2,1)S(1)}, u32[]{:S(2)}, u32[]{:S(2)}) collective-permute-start(bf16[128,1152]{1,0:T(8,128)(2,1)S(1)} %get-tuple-element.17.refs_2_.refs_6_.refs_1_), channel_id=1, source_target_pairs={{0,3},{1,4},{2,1},{3,6},{4,7},{5,8},{6,5},{7,10},{8,11},{9,12},{10... | collective-permute-start | bytes 884744 | tf_op jit(solution)/shard_map/ppermute | solution.py:237
  5.6 9.2 %collective-permute-start.3 = (bf16[128,1152]{1,0:T(8,128)(2,1)S(1)}, bf16[128,1152]{1,0:T(8,128)(2,1)S(1)}, u32[]{:S(2)}, u32[]{:S(2)}) collective-permute-start(bf16[128,1152]{1,0:T(8,128)(2,1)S(1)} %get-tuple-element.33.refs_7_), channel_id=1, source_target_pairs={{0,3},{1,4},{2,1},{3,6},{4,7},{5,8},{6,5},{7,10},{8,11},{9,12},{10... | collective-permute-start | bytes 884744 | tf_op jit(solution)/shard_map/ppermute | solution.py:237
  11.6 3.2 %collective-permute-start.4 = (bf16[128,1152]{1,0:T(8,128)(2,1)S(1)}, bf16[128,1152]{1,0:T(8,128)(2,1)S(1)}, u32[]{:S(2)}, u32[]{:S(2)}) collective-permute-start(bf16[128,1152]{1,0:T(8,128)(2,1)S(1)} %collective-permute-done.refs_5_.refs_2_), channel_id=1, source_target_pairs={{0,1},{1,0},{2,3},{3,2},{4,5},{5,4},{6,7},{7,6},{8,9},{9,8},{10,11... | collective-permute-start | bytes 884744 | tf_op jit(solution)/shard_map/ppermute | solution.py:15
  14.8 2.8 %collective-permute-start.5 = (bf16[128,1152]{1,0:T(8,128)(2,1)S(1)}, bf16[128,1152]{1,0:T(8,128)(2,1)S(1)}, u32[]{:S(2)}, u32[]{:S(2)}) collective-permute-start(bf16[128,1152]{1,0:T(8,128)(2,1)S(1)} %collective-permute-done.3.refs_6_.refs_3_), channel_id=1, source_target_pairs={{0,1},{1,0},{2,3},{3,2},{4,5},{5,4},{6,7},{7,6},{8,9},{9,8},{10,11... | collective-permute-start | bytes 884744 | tf_op jit(solution)/shard_map/ppermute | solution.py:15
  15.7 6.8 %collective-permute-start.7 = (bf16[128,1152]{1,0:T(8,128)(2,1)S(1)}, bf16[128,1152]{1,0:T(8,128)(2,1)S(1)}, u32[]{:S(2)}, u32[]{:S(2)}) collective-permute-start(bf16[128,1152]{1,0:T(8,128)(2,1)S(1)} %shard_map.66), channel_id=1, source_target_pairs={{0,2},{1,29},{2,0},{3,31},{4,6},{5,1},{6,4},{7,3},{8,10},{9,5},{10... | collective-permute-start | bytes 884744 | tf_op jit(solution)/shard_map/ppermute | solution.py:237
  18.5 6.6 %collective-permute-start.6 = (bf16[128,1152]{1,0:T(8,128)(2,1)S(1)}, bf16[128,1152]{1,0:T(8,128)(2,1)S(1)}, u32[]{:S(2)}, u32[]{:S(2)}) collective-permute-start(bf16[128,1152]{1,0:T(8,128)(2,1)S(1)} %shard_map.65), channel_id=1, source_target_pairs={{0,3},{1,28},{2,1},{3,30},{4,7},{5,0},{6,5},{7,2},{8,11},{9,4},{10... | collective-permute-start | bytes 884744 | tf_op jit(solution)/shard_map/ppermute | solution.py:237

commit v10 on v5

--- a/solution.py
+++ b/solution.py
@@ -259,9 +259,9 @@
     got_b, *starts = lax.optimization_barrier((got_b, *starts))
     job_a = [([swap_a], [second, other_first, got_a, got_b], [], False)]
     [back_a] = pulled(job_a, [bf16], scale, shift, 1)
+    [back_a] = pulled(job_a, [bf16], scale, shift, 0, back_a)
     got_b_again, back_a = lax.optimization_barrier((got_b, back_a))
     swap_b = swapped(got_b_again)
-    [back_a] = pulled(job_a, [bf16], scale, shift, 0, back_a)
     [back_b] = pulled(
         [([swap_b], [second, other_first, got_a, got_b], [], False)], [bf16], scale, shift
     )

time: 26 us -> 26.1 us (level)
  starting transfers between devices: 8.33 us -> 8.62 us
  transfers between devices with their start and end apart: 8 -> 8, of which waited for: 4 -> 4; matrix products, arithmetic and copies ran while one was open for 0% -> 0% of each run, Pallas kernels for 20% -> 16%
where the time goes in v10:
time: 26.1 us; the launch traced here: 25.9 us
  waiting for transfers between devices  8.89 us (34%)
  starting transfers between devices  8.62 us (33%)
  Pallas kernels  5.84 us (22%)
  between operations  2.04 us (8%)
  local copies, waits for them, and re-layouts  0.44 us (2%)
    ppermute x4, waiting for transfers between devices, sent(): return lax.ppermute(array, ('grp', 'in'), pairs)  8.88 us
    ppermute x4, starting transfers between devices, sent(): return lax.ppermute(array, ('grp', 'in'), pairs)  7.95 us
    pallas_call x5, Pallas kernels, pulled(): pl.pallas_call(kernel, out_shape=[jax.ShapeDtypeStruct((height, width), t...  4.29 us
    pallas_call x2, Pallas kernels, placed(): pl.pallas_call(kernel, out_shape=[jax.ShapeDtypeStruct(shape, dtype)] * 2...  1.51 us
    ppermute x4, starting transfers between devices, moved(): lax.ppermute(array, axis, [(i, target(i) % peers) for i in range(peers)])  0.67 us
  transfers between devices with their start and end apart: 8, of which 4 were waited for; matrix products, arithmetic and copies ran while one was open for 0% of the time, Pallas kernels for 16%

profile of v10, /device:TPU:0, one launch (start us, length us, event | category | flops | bytes accessed | tf_op | source)
XLA Modules:
  0.0 25.9 jit_solution(1571384237536816542)
XLA Ops:
  0.6 0.0 copy-start
  0.6 0.0 copy-start.1
  0.6 0.5 %collective-permute-start.1 = (bf16[128,1152]{1,0:T(8,128)(2,1)}, bf16[128,1152]{1,0:T(8,128)(2,1)S(1)}, u32[]{:S(2)}, u32[]{:S(2)}) collective-permute-start(bf16[128,1152]{1,0:T(8,128)(2,1)} %image_ref.1), channel_id=1, source_target_pairs={{0,1},{1,0},{2,3},{3,2},{4,5},{5,4},{6,7},{7,6},{8,9},{9,8},{10,11... | collective-permute-start | bytes 884744 | tf_op jit(solution)/shard_map/ppermute | solution.py:15
  1.2 0.1 collective-permute-start.2
  1.2 0.3 %copy-done = bf16[128,1152]{1,0:T(8,128)(2,1)S(1)} copy-done((bf16[128,1152]{1,0:T(8,128)(2,1)S(1)}, bf16[128,1152]{1,0:T(8,128)(2,1)}, u32[]{:S(2)}) %copy-start) | copy-done | bytes 294936
  1.6 0.1 copy-done.1
  1.7 2.4 %collective-permute-start = (bf16[128,1152]{1,0:T(8,128)(2,1)S(1)}, bf16[128,1152]{1,0:T(8,128)(2,1)S(1)}, u32[]{:S(2)}, u32[]{:S(2)}) collective-permute-start(bf16[128,1152]{1,0:T(8,128)(2,1)S(1)} %get-tuple-element.17.refs_2_.refs_6_.refs_1_), channel_id=1, source_target_pairs={{0,3},{1,4},{2,1},{3,6},{4,7},{5,8},{6,5},{7,10},{8,11},{9,12},{10... | collective-permute-start | bytes 884744 | tf_op jit(solution)/shard_map/ppermute | solution.py:237
  5.5 0.0 collective-permute-done.1
  5.5 0.0 collective-permute-done.2
  5.5 0.1 broadcast_select_fusion
  5.6 1.9 %collective-permute-start.3 = (bf16[128,1152]{1,0:T(8,128)(2,1)S(1)}, bf16[128,1152]{1,0:T(8,128)(2,1)S(1)}, u32[]{:S(2)}, u32[]{:S(2)}) collective-permute-start(bf16[128,1152]{1,0:T(8,128)(2,1)S(1)} %get-tuple-element.33.refs_7_), channel_id=1, source_target_pairs={{0,3},{1,4},{2,1},{3,6},{4,7},{5,8},{6,5},{7,10},{8,11},{9,12},{10... | collective-permute-start | bytes 884744 | tf_op jit(solution)/shard_map/ppermute | solution.py:237
  7.4 4.2 %collective-permute-done.refs_5_.refs_2_ = bf16[128,1152]{1,0:T(8,128)(2,1)S(1)} collective-permute-done((bf16[128,1152]{1,0:T(8,128)(2,1)S(1)}, bf16[128,1152]{1,0:T(8,128)(2,1)S(1)}, u32[]{:S(2)}, u32[]{:S(2)}) %collective-permute-start) | collective-permute-done | bytes 294944 | tf_op jit(solution)/shard_map/ppermute | solution.py:237
  11.6 0.0 collective-permute-start.4
  11.6 1.3 %shard_map.62 = (f32[128,1152]{1,0:T(8,128)S(1)}, f32[128,1152]{1,0:T(8,128)S(1)}) custom-call(f32[1]{0:T(128)S(6)} %copy.10.scale_ref.refs_0_, f32[1]{0:T(128)S(6)} %copy.11.shift_ref.refs_1_, bf16[128,1152]{1,0:T(8,128)(2,1)S(1)} %get-tuple-element.17.refs_2_.refs_6_.refs_1_, bf16[128,1152]{1,0:T(8,128)(2,1)S(1)} %get-tuple-element.20.refs_3_.refs_5_, ...), custom_call_target="tpu_custom_call" | custom-call | flops 301989888 | bytes 2949120 | tf_op jit(solution)/shard_map/pallas_call | solution.py:102
  12.9 1.8 %collective-permute-done.3.refs_6_.refs_3_ = bf16[128,1152]{1,0:T(8,128)(2,1)S(1)} collective-permute-done((bf16[128,1152]{1,0:T(8,128)(2,1)S(1)}, bf16[128,1152]{1,0:T(8,128)(2,1)S(1)}, u32[]{:S(2)}, u32[]{:S(2)}) %collective-permute-start.3) | collective-permute-done | bytes 294944 | tf_op jit(solution)/shard_map/ppermute | solution.py:237
  14.8 0.0 collective-permute-done.4.refs_2_.refs_6_
  14.8 0.8 %shard_map.64 = bf16[128,1152]{1,0:T(8,128)(2,1)S(1)} custom-call(f32[1]{0:T(128)S(6)} %copy.10.scale_ref.refs_0_, f32[1]{0:T(128)S(6)} %copy.11.shift_ref.refs_1_, bf16[128,1152]{1,0:T(8,128)(2,1)S(1)} %collective-permute-done.4.refs_2_.refs_6_, bf16[128,1152]{1,0:T(8,128)(2,1)S(1)} %get-tuple-element.20.refs_3_.refs_5_, ...), custom_call_target="tpu_custom_call" | custom-call | flops 301989888 | bytes 1769472 | tf_op jit(solution)/shard_map/pallas_call | solution.py:102
  15.6 0.1 collective-permute-start.5
  15.7 2.0 %collective-permute-start.7 = (bf16[128,1152]{1,0:T(8,128)(2,1)S(1)}, bf16[128,1152]{1,0:T(8,128)(2,1)S(1)}, u32[]{:S(2)}, u32[]{:S(2)}) collective-permute-start(bf16[128,1152]{1,0:T(8,128)(2,1)S(1)} %shard_map.64), channel_id=1, source_target_pairs={{0,2},{1,29},{2,0},{3,31},{4,6},{5,1},{6,4},{7,3},{8,10},{9,5},{10... | collective-permute-start | bytes 884744 | tf_op jit(solution)/shard_map/ppermute | solution.py:237
  17.7 0.0 collective-permute-done.5.refs_7_.refs_2_
  17.7 0.8 %shard_map.66 = bf16[128,1152]{1,0:T(8,128)(2,1)S(1)} custom-call(f32[1]{0:T(128)S(6)} %copy.10.scale_ref.refs_0_, f32[1]{0:T(128)S(6)} %copy.11.shift_ref.refs_1_, bf16[128,1152]{1,0:T(8,128)(2,1)S(1)} %collective-permute-done.5.refs_7_.refs_2_, bf16[128,1152]{1,0:T(8,128)(2,1)S(1)} %get-tuple-element.20.refs_3_.refs_5_, ...), custom_call_target="tpu_custom_call" | custom-call | flops 301989888 | bytes 1769472 | tf_op jit(solution)/shard_map/pallas_call | solution.py:102
  18.6 1.7 %collective-permute-start.6 = (bf16[128,1152]{1,0:T(8,128)(2,1)S(1)}, bf16[128,1152]{1,0:T(8,128)(2,1)S(1)}, u32[]{:S(2)}, u32[]{:S(2)}) collective-permute-start(bf16[128,1152]{1,0:T(8,128)(2,1)S(1)} %shard_map.66), channel_id=1, source_target_pairs={{0,3},{1,28},{2,1},{3,30},{4,7},{5,0},{6,5},{7,2},{8,11},{9,4},{10... | collective-permute-start | bytes 884744 | tf_op jit(solution)/shard_map/ppermute | solution.py:237
  20.2 1.3 %shard_map.65 = (f32[128,1152]{1,0:T(8,128)S(1)}, f32[128,1152]{1,0:T(8,128)S(1)}) custom-call(f32[2,128]{1,0:T(2,128)S(1)} %shard_map.61.refs_0_, bf16[128,1152]{1,0:T(8,128)(2,1)S(1)} %get-tuple-element.17.refs_2_.refs_6_.refs_1_, bf16[128,1152]{1,0:T(8,128)(2,1)S(1)} %collective-permute-done.refs_5_.refs_2_, ...), custom_call_target="tpu_custom_call" | custom-call | flops 301989888 | bytes 4128768 | tf_op jit(solution)/shard_map/pallas_call | solution.py:102
  21.6 0.9 %collective-permute-done.7.extra_ref = bf16[128,1152]{1,0:T(8,128)(2,1)S(1)} collective-permute-done((bf16[128,1152]{1,0:T(8,128)(2,1)S(1)}, bf16[128,1152]{1,0:T(8,128)(2,1)S(1)}, u32[]{:S(2)}, u32[]{:S(2)}) %collective-permute-start.7) | collective-permute-done | bytes 294944 | tf_op jit(solution)/shard_map/ppermute | solution.py:237
  22.5 0.8 %shard_map.67 = (bf16[128,1152]{1,0:T(8,128)(2,1)}, bf16[128,1152]{1,0:T(8,128)(2,1)}) custom-call(f32[128,1152]{1,0:T(8,128)S(1)} %get-tuple-element.28.total_ref, bf16[128,1152]{1,0:T(8,128)(2,1)S(1)} %collective-permute-done.7.extra_ref), custom_call_target="tpu_custom_call" | custom-call | flops 589824 | bytes 589824 | tf_op jit(solution)/shard_map/pallas_call | solution.py:163
  23.3 1.9 %collective-permute-done.6.extra_ref = bf16[128,1152]{1,0:T(8,128)(2,1)S(1)} collective-permute-done((bf16[128,1152]{1,0:T(8,128)(2,1)S(1)}, bf16[128,1152]{1,0:T(8,128)(2,1)S(1)}, u32[]{:S(2)}, u32[]{:S(2)}) %collective-permute-start.6) | collective-permute-done | bytes 294944 | tf_op jit(solution)/shard_map/ppermute | solution.py:237
  25.1 0.8 %shard_map.68 = (bf16[128,1152]{1,0:T(8,128)(2,1)}, bf16[128,1152]{1,0:T(8,128)(2,1)}) custom-call(f32[128,1152]{1,0:T(8,128)S(1)} %get-tuple-element.27.total_ref, bf16[128,1152]{1,0:T(8,128)(2,1)S(1)} %collective-permute-done.6.extra_ref, bf16[128,1152]{1,0:T(8,128)(2,1)} %get-tuple-element.30.refs_0_, ...), custom_call_target="tpu_custom_call", output_to_operand_aliasing={{0}: (2, {}), {1}: (3, {})} | custom-call | flops 589824 | bytes 589824 | tf_op jit(solution)/shard_map/pallas_call | solution.py:163
  (4 shorter events, 0.0 us)
Async XLA Ops:
  0.6 1.0 %copy-start = (bf16[128,1152]{1,0:T(8,128)(2,1)S(1)}, bf16[128,1152]{1,0:T(8,128)(2,1)}, u32[]{:S(2)}) copy-start(bf16[128,1152]{1,0:T(8,128)(2,1)} %image_ref.1) | copy-start | bytes 884740
  0.6 1.0 %copy-start.1 = (bf16[128,1152]{1,0:T(8,128)(2,1)S(1)}, bf16[128,1152]{1,0:T(8,128)(2,1)}, u32[]{:S(2)}) copy-start(bf16[128,1152]{1,0:T(8,128)(2,1)} %text_ref.1) | copy-start | bytes 884740
  0.6 4.8 %collective-permute-start.1 = (bf16[128,1152]{1,0:T(8,128)(2,1)}, bf16[128,1152]{1,0:T(8,128)(2,1)S(1)}, u32[]{:S(2)}, u32[]{:S(2)}) collective-permute-start(bf16[128,1152]{1,0:T(8,128)(2,1)} %image_ref.1), channel_id=1, source_target_pairs={{0,1},{1,0},{2,3},{3,2},{4,5},{5,4},{6,7},{7,6},{8,9},{9,8},{10,11... | collective-permute-start | bytes 884744 | tf_op jit(solution)/shard_map/ppermute | solution.py:15
  1.2 4.3 %collective-permute-start.2 = (bf16[128,1152]{1,0:T(8,128)(2,1)}, bf16[128,1152]{1,0:T(8,128)(2,1)S(1)}, u32[]{:S(2)}, u32[]{:S(2)}) collective-permute-start(bf16[128,1152]{1,0:T(8,128)(2,1)} %text_ref.1), channel_id=1, source_target_pairs={{0,1},{1,0},{2,3},{3,2},{4,5},{5,4},{6,7},{7,6},{8,9},{9,8},{10,11... | collective-permute-start | bytes 884744 | tf_op jit(solution)/shard_map/ppermute | solution.py:15
  1.7 9.9 %collective-permute-start = (bf16[128,1152]{1,0:T(8,128)(2,1)S(1)}, bf16[128,1152]{1,0:T(8,128)(2,1)S(1)}, u32[]{:S(2)}, u32[]{:S(2)}) collective-permute-start(bf16[128,1152]{1,0:T(8,128)(2,1)S(1)} %get-tuple-element.17.refs_2_.refs_6_.refs_1_), channel_id=1, source_target_pairs={{0,3},{1,4},{2,1},{3,6},{4,7},{5,8},{6,5},{7,10},{8,11},{9,12},{10... | collective-permute-start | bytes 884744 | tf_op jit(solution)/shard_map/ppermute | solution.py:237
  5.6 9.2 %collective-permute-start.3 = (bf16[128,1152]{1,0:T(8,128)(2,1)S(1)}, bf16[128,1152]{1,0:T(8,128)(2,1)S(1)}, u32[]{:S(2)}, u32[]{:S(2)}) collective-permute-start(bf16[128,1152]{1,0:T(8,128)(2,1)S(1)} %get-tuple-element.33.refs_7_), channel_id=1, source_target_pairs={{0,3},{1,4},{2,1},{3,6},{4,7},{5,8},{6,5},{7,10},{8,11},{9,12},{10... | collective-permute-start | bytes 884744 | tf_op jit(solution)/shard_map/ppermute | solution.py:237
  11.6 3.2 %collective-permute-start.4 = (bf16[128,1152]{1,0:T(8,128)(2,1)S(1)}, bf16[128,1152]{1,0:T(8,128)(2,1)S(1)}, u32[]{:S(2)}, u32[]{:S(2)}) collective-permute-start(bf16[128,1152]{1,0:T(8,128)(2,1)S(1)} %collective-permute-done.refs_5_.refs_2_), channel_id=1, source_target_pairs={{0,1},{1,0},{2,3},{3,2},{4,5},{5,4},{6,7},{7,6},{8,9},{9,8},{10,11... | collective-permute-start | bytes 884744 | tf_op jit(solution)/shard_map/ppermute | solution.py:15
  15.6 2.1 %collective-permute-start.5 = (bf16[128,1152]{1,0:T(8,128)(2,1)S(1)}, bf16[128,1152]{1,0:T(8,128)(2,1)S(1)}, u32[]{:S(2)}, u32[]{:S(2)}) collective-permute-start(bf16[128,1152]{1,0:T(8,128)(2,1)S(1)} %collective-permute-done.3.refs_6_.refs_3_), channel_id=1, source_target_pairs={{0,1},{1,0},{2,3},{3,2},{4,5},{5,4},{6,7},{7,6},{8,9},{9,8},{10,11... | collective-permute-start | bytes 884744 | tf_op jit(solution)/shard_map/ppermute | solution.py:15
  15.7 6.8 %collective-permute-start.7 = (bf16[128,1152]{1,0:T(8,128)(2,1)S(1)}, bf16[128,1152]{1,0:T(8,128)(2,1)S(1)}, u32[]{:S(2)}, u32[]{:S(2)}) collective-permute-start(bf16[128,1152]{1,0:T(8,128)(2,1)S(1)} %shard_map.64), channel_id=1, source_target_pairs={{0,2},{1,29},{2,0},{3,31},{4,6},{5,1},{6,4},{7,3},{8,10},{9,5},{10... | collective-permute-start | bytes 884744 | tf_op jit(solution)/shard_map/ppermute | solution.py:237
  18.6 6.6 %collective-permute-start.6 = (bf16[128,1152]{1,0:T(8,128)(2,1)S(1)}, bf16[128,1152]{1,0:T(8,128)(2,1)S(1)}, u32[]{:S(2)}, u32[]{:S(2)}) collective-permute-start(bf16[128,1152]{1,0:T(8,128)(2,1)S(1)} %shard_map.66), channel_id=1, source_target_pairs={{0,3},{1,28},{2,1},{3,30},{4,7},{5,0},{6,5},{7,2},{8,11},{9,4},{10... | collective-permute-start | bytes 884744 | tf_op jit(solution)/shard_map/ppermute | solution.py:237
